TPU v7x, 32 devices: a whole 2x2x4 slice. The times are simulated.
32 devices in a mesh: dp: 8 (over y, x, core), cp: 4 (over z).
Axes of the slice: x: 2, y: 2, z: 4, core: 2. Of those that a mesh axis runs over, the one named last changes fastest.
Arguments:
- tokens: bfloat16 [8, 1024, 1536], P('dp', 'cp'), may hold values from -6 to 6
- routes: int32 [8, 1024, 4], P('dp', 'cp'), may hold values from 0 to 7, all different within a row; in each aligned block of 256 rows (0 to 255, 256 to 511, ..., all dimensions but the last counted through in order) at most 170 rows name the same one
- out_grad: bfloat16 [8, 1024, 1536], P('dp', 'cp'), may hold values from -6 to 6
- norm_attn: bfloat16 [1536], P('cp'), may hold values from 0.5 to 1.5
- w_query: bfloat16 [1536, 1536], P('cp'), may hold values from -0.15625 to 0.15625
- key_weight: bfloat16 [1536, 256], P('cp'), may hold values from -0.15625 to 0.15625
- value_weight: bfloat16 [1536, 256], P('cp'), may hold values from -0.15625 to 0.15625
- w_out: bfloat16 [1536, 1536], P('cp'), may hold values from -6 to 6
- norm_mix: bfloat16 [1536], P('cp'), may hold values from 0.5 to 1.5
- w_router: bfloat16 [1536, 8], P('cp'), may hold values from -0.078125 to 0.078125
- w_gate: bfloat16 [8, 1536, 768], P(None, 'cp'), may hold values from -0.15625 to 0.15625
- w_up: bfloat16 [8, 1536, 768], P(None, 'cp'), may hold values from -0.15625 to 0.15625
- w_down: bfloat16 [8, 768, 1536], P(None, 'cp'), may hold values from -0.4375 to 0.4375
Outputs:
- output: bfloat16 [8, 1024, 1536], P('dp', 'cp')
- input_grad: bfloat16 [8, 1024, 1536], P('dp', 'cp')
- grad_norm_attn: float32 [1536], P('cp')
- grad_w_query: float32 [1536, 1536], P('cp')
- grad_w_key: float32 [1536, 256], P('cp')
- grad_w_value: float32 [1536, 256], P('cp')
- grad_w_out: float32 [1536, 1536], P('cp')
- grad_norm_mix: float32 [1536], P('cp')
- grad_w_router: float32 [1536, 8], P('cp')
- grad_w_gate: float32 [8, 1536, 768], P(None, 'cp')
- grad_w_up: float32 [8, 1536, 768], P(None, 'cp')
- grad_w_down: float32 [8, 768, 1536], P(None, 'cp')
Inputs may be any that keep to these rules, and one draw needn't show every extreme that they name: `routes`: each row names 4 different experts; in the rows of one device (aligned blocks of 256 rows) no expert is named by more than 170 rows.
All inputs are finite; a program needn't handle non-finite values.
Results may differ from a plain program's by a relative error of at most 0.028.
Values may be sent and summed in bfloat16 or wider, within the bound.
No kernel may reach another device: no remote copies, remote signals or barrier semaphores. Data moves between devices by JAX's collectives and lax.ppermute only.
A program may use at most 384 MiB of HBM per device.

v0:
```python
import math

import jax
import jax.numpy as jnp
from jax import lax
from jax.sharding import PartitionSpec as P

MODEL_WIDTH = 1536
QUERY_HEADS = 12
KEY_VALUE_HEADS = 2
HEAD_WIDTH = 128
EXPERTS = 8
TOPK = 4
BLK = 256
CAP = 170


norm_eps = 1e-06
rope_base = 1000000.0
mask_fill = -1e30


def rope_tables(token_positions, head_size):
    half_size = head_size // 2
    frequency = rope_base ** (-2.0 * jnp.arange(half_size, dtype=jnp.float32) / head_size)
    angles = token_positions.astype(jnp.float32)[:, None] * frequency[None, :]
    cosine_table = jnp.concatenate([jnp.cos(angles), jnp.cos(angles)], 1)[:, None, :]
    sine_table = jnp.concatenate([jnp.sin(angles), jnp.sin(angles)], 1)[:, None, :]
    return (cosine_table, sine_table)


def rotate_pairs(values, cosine_table, sine_table):
    half_size = values.shape[-1] // 2
    turned = jnp.concatenate([-values[..., half_size:], values[..., :half_size]], -1)
    return values * cosine_table + turned * sine_table


def rotate_pairs_back(gradient, cosine_table, sine_table):
    half_size = gradient.shape[-1] // 2
    scaled = gradient * sine_table
    turned = jnp.concatenate([scaled[..., half_size:], -scaled[..., :half_size]], -1)
    return gradient * cosine_table + turned


def norm_forward(values, gain_vec):
    inverse = lax.rsqrt(jnp.mean(values * values, -1, keepdims=True) + norm_eps)
    scaled = values * inverse
    return (scaled * gain_vec, scaled, inverse)


def norm_backward(gradient, gain_vec, scaled, inverse):
    gain_grad = jnp.sum(gradient * scaled, 0)
    inner_vals = gradient * gain_vec
    return (
        inverse * (inner_vals - scaled * jnp.mean(inner_vals * scaled, -1, keepdims=True)),
        gain_grad,
    )


def gather_attention(norm_attn, w_query, key_weight, value_weight, w_out):
    return (
        lax.all_gather(norm_attn, "cp", axis=0, tiled=True),
        lax.all_gather(w_query, "cp", axis=0, tiled=True),
        lax.all_gather(key_weight, "cp", axis=0, tiled=True),
        lax.all_gather(value_weight, "cp", axis=0, tiled=True),
        lax.all_gather(w_out, "cp", axis=0, tiled=True),
    )


def gather_mixture(norm_mix, w_router, w_gate, w_up, w_down):
    return (
        lax.all_gather(norm_mix, "cp", axis=0, tiled=True),
        lax.all_gather(w_router, "cp", axis=0, tiled=True),
        lax.all_gather(w_gate, "cp", axis=1, tiled=True),
        lax.all_gather(w_up, "cp", axis=1, tiled=True),
        lax.all_gather(w_down, "cp", axis=1, tiled=True),
    )


def local(
    tokens,
    routes,
    out_grad,
    norm_attn,
    w_query,
    key_weight,
    value_weight,
    w_out,
    norm_mix,
    w_router,
    w_gate,
    w_up,
    w_down,
):
    token_count = tokens.shape[1]
    cp_count = lax.axis_size("cp")
    token_length = token_count * cp_count
    cp_rank = lax.axis_index("cp")
    token_positions = cp_rank * token_count + jnp.arange(token_count, dtype=jnp.int32)
    query_blocks = token_positions // BLK
    last_block = (cp_rank * token_count + token_count - 1) // BLK
    inputs = tokens[0].astype(jnp.float32)
    route_rows = routes[0]
    query_group_width = QUERY_HEADS // KEY_VALUE_HEADS
    score_scale = 1.0 / math.sqrt(HEAD_WIDTH)
    gain_one, full_query, full_key, full_value, full_out = gather_attention(
        norm_attn, w_query, key_weight, value_weight, w_out
    )
    first_normalized, scaled_one, inverse_one = norm_forward(inputs, gain_one.astype(jnp.float32))
    normed_low = first_normalized.astype(jnp.bfloat16)
    query_linear = jnp.dot(normed_low, full_query, preferred_element_type=jnp.float32)
    key_linear = jnp.dot(normed_low, full_key, preferred_element_type=jnp.float32)
    value_low = jnp.dot(normed_low, full_value, preferred_element_type=jnp.float32).astype(
        jnp.bfloat16
    )
    cosine_table, sine_table = rope_tables(token_positions, HEAD_WIDTH)
    query_heads = (
        rotate_pairs(
            query_linear.reshape(token_count, QUERY_HEADS, HEAD_WIDTH), cosine_table, sine_table
        )
        .astype(jnp.bfloat16)
        .reshape(token_count, KEY_VALUE_HEADS, query_group_width, HEAD_WIDTH)
    )
    rotated_key = (
        rotate_pairs(
            key_linear.reshape(token_count, KEY_VALUE_HEADS, HEAD_WIDTH), cosine_table, sine_table
        )
        .astype(jnp.bfloat16)
        .reshape(token_count, KEY_VALUE_HEADS * HEAD_WIDTH)
    )
    statistic_shape = (KEY_VALUE_HEADS, query_group_width, token_count)
    initial = (
        jnp.full(statistic_shape, mask_fill, jnp.float32),
        jnp.zeros(statistic_shape, jnp.float32),
        jnp.zeros(statistic_shape + (HEAD_WIDTH,), jnp.float32),
    )
    key_portion = lax.all_gather(rotated_key, "cp", axis=0, tiled=True)
    value_portion = lax.all_gather(value_low, "cp", axis=0, tiled=True)
    portion_rows = key_portion.shape[0]

    def update(current):
        run_max, run_sum, run_acc = current
        key_head_rows = key_portion.reshape(portion_rows, KEY_VALUE_HEADS, HEAD_WIDTH)
        value_head_rows = value_portion.reshape(portion_rows, KEY_VALUE_HEADS, HEAD_WIDTH)
        key_blocks = jnp.arange(portion_rows, dtype=jnp.int32) // BLK
        visible = key_blocks[None, :] <= query_blocks[:, None]
        scores = (
            jnp.einsum(
                "tgjh,sgh->gjts", query_heads, key_head_rows, preferred_element_type=jnp.float32
            )
            * score_scale
        )
        scores = jnp.where(visible, scores, mask_fill)
        new_max = jnp.maximum(run_max, jnp.max(scores, -1))
        weights = jnp.where(visible, jnp.exp(scores - new_max[..., None]), 0.0)
        new_sum = jnp.sum(weights, -1)
        new_acc = jnp.einsum(
            "gjts,sgh->gjth",
            weights.astype(jnp.bfloat16),
            value_head_rows,
            preferred_element_type=jnp.float32,
        )
        return (new_max, new_sum, new_acc)

    final_max, final_sum, final_acc = lax.cond(
        jnp.int32(0) // BLK > last_block, lambda current: current, update, initial
    )
    attn_mix = final_acc / final_sum[..., None]
    log_total = final_max + jnp.log(final_sum)
    attn_low = (
        jnp.transpose(attn_mix, (2, 0, 1, 3))
        .reshape(token_count, QUERY_HEADS * HEAD_WIDTH)
        .astype(jnp.bfloat16)
    )
    middle = inputs + jnp.dot(attn_low, full_out, preferred_element_type=jnp.float32)
    mix_full = gather_mixture(norm_mix, w_router, w_gate, w_up, w_down)
    gain_two, full_router, full_gate, full_up, full_down = mix_full
    normed_two, scaled_two, inverse_two = norm_forward(middle, gain_two.astype(jnp.float32))
    normed_low_two = normed_two.astype(jnp.bfloat16)
    logits = jnp.dot(normed_low_two, full_router, preferred_element_type=jnp.float32)
    chosen = jnp.take_along_axis(logits, route_rows, 1)
    gate_raise = jnp.exp(chosen - jnp.max(chosen, -1, keepdims=True))
    gate_vals = gate_raise / jnp.sum(gate_raise, -1, keepdims=True)
    expert_ids = route_rows.reshape(-1)
    expert_range = jnp.arange(EXPERTS, dtype=jnp.int32)
    id_flags = (expert_ids[:, None] == expert_range[None, :]).astype(jnp.int32)
    places = jnp.sum((jnp.cumsum(id_flags, 0) - 1) * id_flags, 1)
    slot_index = expert_ids * CAP + places
    token_ids = jnp.arange(token_count * TOPK, dtype=jnp.int32) // TOPK
    slot_token = jnp.zeros((EXPERTS * CAP,), jnp.int32).at[slot_index].set(token_ids)
    slot_gate = jnp.zeros((EXPERTS * CAP,), jnp.float32).at[slot_index].set(gate_vals.reshape(-1))
    expert_in = normed_low_two[slot_token].reshape(EXPERTS, CAP, MODEL_WIDTH)
    gate_pre = jnp.einsum("ecd,edf->ecf", expert_in, full_gate, preferred_element_type=jnp.float32)
    up_pre = jnp.einsum("ecd,edf->ecf", expert_in, full_up, preferred_element_type=jnp.float32)
    sig_vals = jax.nn.sigmoid(gate_pre)
    swish_vals = gate_pre * sig_vals
    active_low = (swish_vals * up_pre).astype(jnp.bfloat16)
    expert_out = jnp.einsum(
        "ecf,efd->ecd", active_low, full_down, preferred_element_type=jnp.float32
    ).reshape(EXPERTS * CAP, MODEL_WIDTH)
    picked = expert_out[slot_index].reshape(token_count, TOPK, MODEL_WIDTH)
    result = middle + jnp.sum(gate_vals[:, :, None] * picked, 1)
    output = result.astype(jnp.bfloat16)[None]
    upstream = out_grad[0].astype(jnp.float32)
    back_gain_two, back_router, back_gate, back_up, back_down = gather_mixture(
        norm_mix, w_router, w_gate, w_up, w_down
    )
    gate_grad = jnp.sum(picked * upstream[:, None, :], -1)
    slot_grad = (
        (slot_gate[:, None] * upstream[slot_token])
        .astype(jnp.bfloat16)
        .reshape(EXPERTS, CAP, MODEL_WIDTH)
    )
    active_grad = jnp.einsum(
        "ecd,efd->ecf", slot_grad, back_down, preferred_element_type=jnp.float32
    )
    swish_slope = sig_vals * (1.0 + gate_pre * (1.0 - sig_vals))
    gate_pre_grad = (active_grad * up_pre * swish_slope).astype(jnp.bfloat16)
    up_pre_grad = (active_grad * swish_vals).astype(jnp.bfloat16)
    slot_in_grad = jnp.einsum(
        "ecf,edf->ecd", gate_pre_grad, back_gate, preferred_element_type=jnp.float32
    )
    slot_in_grad = slot_in_grad + jnp.einsum(
        "ecf,edf->ecd", up_pre_grad, back_up, preferred_element_type=jnp.float32
    )
    normed_two_grad = jnp.sum(
        slot_in_grad.reshape(EXPERTS * CAP, MODEL_WIDTH)[slot_index].reshape(
            token_count, TOPK, MODEL_WIDTH
        ),
        1,
    )
    weighted = gate_vals * gate_grad
    chosen_grad = weighted - gate_vals * jnp.sum(weighted, -1, keepdims=True)
    route_flags = (route_rows[:, :, None] == expert_range[None, None, :]).astype(jnp.float32)
    logit_grad = jnp.sum(chosen_grad[:, :, None] * route_flags, 1).astype(jnp.bfloat16)
    router_grad = jnp.einsum(
        "td,te->de", normed_low_two, logit_grad, preferred_element_type=jnp.float32
    )
    normed_two_grad = normed_two_grad + jnp.einsum(
        "te,de->td", logit_grad, back_router, preferred_element_type=jnp.float32
    )
    middle_norm_grad, gain_two_grad = norm_backward(
        normed_two_grad, back_gain_two.astype(jnp.float32), scaled_two, inverse_two
    )
    middle_grad = upstream + middle_norm_grad
    input_cols, active_cols = (
        lax.all_to_all(expert_in, "cp", split_axis=2, concat_axis=1, tiled=True),
        lax.all_to_all(active_low, "cp", split_axis=2, concat_axis=1, tiled=True),
    )
    every_gate_grad, every_up_grad, every_slot_grad = (
        lax.all_gather(gate_pre_grad, "cp", axis=1, tiled=True),
        lax.all_gather(up_pre_grad, "cp", axis=1, tiled=True),
        lax.all_gather(slot_grad, "cp", axis=1, tiled=True),
    )
    gate_w_grad = jnp.einsum(
        "ecd,ecf->edf", input_cols, every_gate_grad, preferred_element_type=jnp.float32
    )
    up_w_grad = jnp.einsum(
        "ecd,ecf->edf", input_cols, every_up_grad, preferred_element_type=jnp.float32
    )
    down_w_grad = jnp.einsum(
        "ecf,ecd->efd", active_cols, every_slot_grad, preferred_element_type=jnp.float32
    )
    small_sums = (
        lax.psum_scatter(
            gain_two_grad.astype(jnp.bfloat16), "cp", scatter_dimension=0, tiled=True
        ).astype(jnp.float32),
        lax.psum_scatter(
            router_grad.astype(jnp.bfloat16), "cp", scatter_dimension=0, tiled=True
        ).astype(jnp.float32),
    )
    mix_sums = (small_sums[0], small_sums[1], gate_w_grad, up_w_grad, down_w_grad)
    mix_totals = (
        lax.psum(mix_sums[0].astype(jnp.bfloat16), "dp").astype(jnp.float32),
        lax.psum(mix_sums[1].astype(jnp.bfloat16), "dp").astype(jnp.float32),
        lax.psum(mix_sums[2].astype(jnp.bfloat16), "dp").astype(jnp.float32),
        lax.psum(mix_sums[3].astype(jnp.bfloat16), "dp").astype(jnp.float32),
        lax.psum(mix_sums[4].astype(jnp.bfloat16), "dp").astype(jnp.float32),
    )
    back_gain_one, back_query, back_key, back_value, back_out = gather_attention(
        norm_attn, w_query, key_weight, value_weight, w_out
    )
    branch_grad = middle_grad.astype(jnp.bfloat16)
    out_w_grad = jnp.einsum("ti,td->id", attn_low, branch_grad, preferred_element_type=jnp.float32)
    attention_lowp_grads = jnp.einsum(
        "td,id->ti", branch_grad, back_out, preferred_element_type=jnp.float32
    ).astype(jnp.bfloat16)
    attention_head_grads = attention_lowp_grads.reshape(
        token_count, KEY_VALUE_HEADS, query_group_width, HEAD_WIDTH
    )
    row_delta = jnp.sum(
        jnp.transpose(attention_head_grads.astype(jnp.float32), (1, 2, 0, 3)) * attn_mix, -1
    )
    every_key_row, every_value_row = (
        lax.all_gather(rotated_key, "cp", axis=0, tiled=True),
        lax.all_gather(value_low, "cp", axis=0, tiled=True),
    )
    single_key_block = 512
    number_of_blocks = token_length // single_key_block
    key_division = every_key_row.reshape(
        number_of_blocks, single_key_block, KEY_VALUE_HEADS, HEAD_WIDTH
    )
    value_division = every_value_row.reshape(
        number_of_blocks, single_key_block, KEY_VALUE_HEADS, HEAD_WIDTH
    )

    def backward_block(query_grad, block_inputs):
        block_no, key_part, value_part = block_inputs
        first_row = block_no * single_key_block

        def compute(unused_arg):
            key_blocks = (first_row + jnp.arange(single_key_block, dtype=jnp.int32)) // BLK
            visible = key_blocks[None, :] <= query_blocks[:, None]
            scores = (
                jnp.einsum(
                    "tgjh,sgh->gjts", query_heads, key_part, preferred_element_type=jnp.float32
                )
                * score_scale
            )
            prob_vals = jnp.where(visible, jnp.exp(scores - log_total[..., None]), 0.0)
            value_gradient = jnp.einsum(
                "gjts,tgjh->sgh",
                prob_vals.astype(jnp.bfloat16),
                attention_head_grads,
                preferred_element_type=jnp.float32,
            )
            prob_grad = jnp.einsum(
                "tgjh,sgh->gjts",
                attention_head_grads,
                value_part,
                preferred_element_type=jnp.float32,
            )
            score_grad = (prob_vals * (prob_grad - row_delta[..., None])).astype(jnp.bfloat16)
            query_step = (
                jnp.einsum(
                    "gjts,sgh->gjth", score_grad, key_part, preferred_element_type=jnp.float32
                )
                * score_scale
            )
            key_gradient = (
                jnp.einsum(
                    "gjts,tgjh->sgh", score_grad, query_heads, preferred_element_type=jnp.float32
                )
                * score_scale
            )
            return (query_step, key_gradient, value_gradient)

        def skipped(unused_arg):
            return (
                jnp.zeros(
                    (KEY_VALUE_HEADS, query_group_width, token_count, HEAD_WIDTH), jnp.float32
                ),
                jnp.zeros((single_key_block, KEY_VALUE_HEADS, HEAD_WIDTH), jnp.float32),
                jnp.zeros((single_key_block, KEY_VALUE_HEADS, HEAD_WIDTH), jnp.float32),
            )

        query_step, key_gradient, value_gradient = lax.cond(
            first_row // BLK > last_block, skipped, compute, 0
        )
        return (
            query_grad + query_step,
            (
                key_gradient.reshape(single_key_block, KEY_VALUE_HEADS * HEAD_WIDTH),
                value_gradient.reshape(single_key_block, KEY_VALUE_HEADS * HEAD_WIDTH),
            ),
        )

    query_zeroed = jnp.zeros(
        (KEY_VALUE_HEADS, query_group_width, token_count, HEAD_WIDTH), jnp.float32
    )
    block_ids = jnp.arange(number_of_blocks, dtype=jnp.int32)
    query_grad, (key_gradient_list, value_gradient_list) = lax.scan(
        backward_block, query_zeroed, (block_ids, key_division, value_division)
    )
    local_key_rows, value_own = (
        lax.psum_scatter(
            key_gradient_list.reshape(token_length, KEY_VALUE_HEADS * HEAD_WIDTH).astype(
                jnp.bfloat16
            ),
            "cp",
            scatter_dimension=0,
            tiled=True,
        ).astype(jnp.float32),
        lax.psum_scatter(
            value_gradient_list.reshape(token_length, KEY_VALUE_HEADS * HEAD_WIDTH).astype(
                jnp.bfloat16
            ),
            "cp",
            scatter_dimension=0,
            tiled=True,
        ).astype(jnp.float32),
    )
    query_rot_grad = jnp.transpose(query_grad, (2, 0, 1, 3)).reshape(
        token_count, QUERY_HEADS, HEAD_WIDTH
    )
    query_lin_grad = (
        rotate_pairs_back(query_rot_grad, cosine_table, sine_table)
        .astype(jnp.bfloat16)
        .reshape(token_count, QUERY_HEADS * HEAD_WIDTH)
    )
    key_lin_grad = (
        rotate_pairs_back(
            local_key_rows.reshape(token_count, KEY_VALUE_HEADS, HEAD_WIDTH),
            cosine_table,
            sine_table,
        )
        .astype(jnp.bfloat16)
        .reshape(token_count, KEY_VALUE_HEADS * HEAD_WIDTH)
    )
    value_lin_grad = value_own.astype(jnp.bfloat16)
    query_w_grad = jnp.einsum(
        "td,ti->di", normed_low, query_lin_grad, preferred_element_type=jnp.float32
    )
    key_w_grad = jnp.einsum(
        "td,ti->di", normed_low, key_lin_grad, preferred_element_type=jnp.float32
    )
    value_w_grad = jnp.einsum(
        "td,ti->di", normed_low, value_lin_grad, preferred_element_type=jnp.float32
    )
    normed_one_grad = jnp.einsum(
        "ti,di->td", query_lin_grad, back_query, preferred_element_type=jnp.float32
    )
    normed_one_grad = normed_one_grad + jnp.einsum(
        "ti,di->td", key_lin_grad, back_key, preferred_element_type=jnp.float32
    )
    normed_one_grad = normed_one_grad + jnp.einsum(
        "ti,di->td", value_lin_grad, back_value, preferred_element_type=jnp.float32
    )
    input_norm_grad, gain_one_grad = norm_backward(
        normed_one_grad, back_gain_one.astype(jnp.float32), scaled_one, inverse_one
    )
    input_grad = (middle_grad + input_norm_grad).astype(jnp.bfloat16)[None]
    attn_sums = (
        lax.psum_scatter(
            gain_one_grad.astype(jnp.bfloat16), "cp", scatter_dimension=0, tiled=True
        ).astype(jnp.float32),
        lax.psum_scatter(
            query_w_grad.astype(jnp.bfloat16), "cp", scatter_dimension=0, tiled=True
        ).astype(jnp.float32),
        lax.psum_scatter(
            key_w_grad.astype(jnp.bfloat16), "cp", scatter_dimension=0, tiled=True
        ).astype(jnp.float32),
        lax.psum_scatter(
            value_w_grad.astype(jnp.bfloat16), "cp", scatter_dimension=0, tiled=True
        ).astype(jnp.float32),
        lax.psum_scatter(
            out_w_grad.astype(jnp.bfloat16), "cp", scatter_dimension=0, tiled=True
        ).astype(jnp.float32),
    )
    attn_totals = (
        lax.psum(attn_sums[0].astype(jnp.bfloat16), "dp").astype(jnp.float32),
        lax.psum(attn_sums[1].astype(jnp.bfloat16), "dp").astype(jnp.float32),
        lax.psum(attn_sums[2].astype(jnp.bfloat16), "dp").astype(jnp.float32),
        lax.psum(attn_sums[3].astype(jnp.bfloat16), "dp").astype(jnp.float32),
        lax.psum(attn_sums[4].astype(jnp.bfloat16), "dp").astype(jnp.float32),
    )
    return (
        output,
        input_grad,
        attn_totals[0],
        attn_totals[1],
        attn_totals[2],
        attn_totals[3],
        attn_totals[4],
        mix_totals[0],
        mix_totals[1],
        mix_totals[2],
        mix_totals[3],
        mix_totals[4],
    )


def solution(mesh):
    in_specs = (
        P("dp", "cp", None),
        P("dp", "cp", None),
        P("dp", "cp", None),
        P("cp"),
        P("cp", None),
        P("cp", None),
        P("cp", None),
        P("cp", None),
        P("cp"),
        P("cp", None),
        P(None, "cp", None),
        P(None, "cp", None),
        P(None, "cp", None),
    )
    out_specs = (
        P("dp", "cp", None),
        P("dp", "cp", None),
        P("cp"),
        P("cp", None),
        P("cp", None),
        P("cp", None),
        P("cp", None),
        P("cp"),
        P("cp", None),
        P(None, "cp", None),
        P(None, "cp", None),
        P(None, "cp", None),
    )
    return jax.shard_map(local, mesh=mesh, in_specs=in_specs, out_specs=out_specs, check_vma=False)
```

profile of v0, /device:TPU:0, one launch (start us, length us, event | category | flops | bytes accessed | tf_op | source)
XLA Modules:
  0.0 2696.2 jit_solution(14743596951300165947)
XLA Ops:
  11.1 13.5 all-gather
  24.7 29.2 %all_gather.58 = bf16[1536,256]{1,0:T(8,128)(2,1)S(1)} all-gather(bf16[384,256]{1,0:T(8,128)(2,1)S(1)} %copy-done.44), channel_id=1, replica_groups=mesh['dp'=8,'cp'=4] {'cp'}, dimensions={0}, use_global_device_ids=true | all-gather | bytes 983040 | tf_op jit(solution)/shard_map/all_gather | solution.py:64
  58.2 13.2 all-gather.1
  87.0 9.5 gather.25
  97.2 20.7 all_gather.59
  118.9 18.0 all_gather.61
  138.3 21.5 all_gather.62
  160.8 14.0 all_gather.65
  186.8 14.7 conditional.2
  202.9 19.9 all-gather.13.cloned.1.call-done
  257.2 288.8 %all-gather.15.cloned.1.call-done = bf16[8,1536,768]{2,1,0:T(8,128)(2,1)} async-done(((bf16[8,384,768]{2,1,0:T(8,128)(2,1)}), bf16[8,1536,768]{2,1,0:T(8,128)(2,1)}) %all-gather.15.cloned.1.call-update) | async-done | bytes 18874384 | tf_op jit(solution)/shard_map/all_gather | solution.py:74
  546.0 13.9 fusion.134
  559.9 308.9 %all-gather.17.cloned.1.call-done = bf16[8,1536,768]{2,1,0:T(8,128)(2,1)} async-done(((bf16[8,384,768]{2,1,0:T(8,128)(2,1)}), bf16[8,1536,768]{2,1,0:T(8,128)(2,1)}) %all-gather.17.cloned.1.call-update) | async-done | bytes 18874384 | tf_op jit(solution)/shard_map/all_gather | solution.py:75
  868.8 13.9 fusion.135
  882.7 308.9 %all-gather.19.cloned.1.call-done = bf16[8,768,1536]{2,1,0:T(8,128)(2,1)} async-done(((bf16[8,192,1536]{2,1,0:T(8,128)(2,1)}), bf16[8,768,1536]{2,1,0:T(8,128)(2,1)}) %all-gather.19.cloned.1.call-update) | async-done | bytes 18874384 | tf_op jit(solution)/shard_map/all_gather | solution.py:76
  1191.6 15.3 multiply_convert_fusion.1
  1206.9 14.2 fusion.136
  1221.1 9.4 reshape.451
  1230.5 11.0 gather_fusion.1
  1241.5 7.7 reshape.452
  1249.2 9.6 multiply_reduce_fusion
  1259.1 12.9 fusion.137
  1272.1 14.1 convolution_add_fusion
  1286.2 9.4 reshape.453
  1295.6 11.2 gather_fusion.3
  1331.3 21.6 while.17
  1333.1 11.2 conditional.5
  1368.0 15.9 reduce-scatter.10.cloned.1.call-done
  1387.8 18.3 reduce-scatter.12.cloned.1.call-done
  1423.9 9.2 copy.151
  1443.5 301.3 %all-to-all-done = bf16[8,170,1536]{1,0,2:T(8,128)(2,1)} async-done(((bf16[8,170,1536]{1,0,2:T(8,128)(2,1)}), bf16[8,170,1536]{1,0,2:T(8,128)(2,1)}, u32[]{:S(2)}, u32[]{:S(2)}) %all-to-all-start) | async-done | bytes 4177952 | tf_op jit(solution)/shard_map/all_to_all | solution.py:247
  1749.5 12.8 copy.183
  1768.3 102.7 %all-to-all-done.1 = bf16[8,170,768]{1,0,2:T(8,128)(2,1)} async-done(((bf16[8,170,768]{1,0,2:T(8,128)(2,1)}), bf16[8,170,768]{1,0,2:T(8,128)(2,1)}, u32[]{:S(2)}, u32[]{:S(2)}) %all-to-all-start.1) | async-done | bytes 2088992 | tf_op jit(solution)/shard_map/all_to_all | solution.py:248
  1871.0 9.3 copy.184
  1884.1 9.4 all-gather.25.cloned.1.call-done
  1893.5 20.6 fusion.51
  1914.2 128.2 %all-gather.21.cloned.1.call-done = bf16[8,680,768]{2,0,1:T(8,128)(2,1)} async-done(((bf16[8,170,768]{2,0,1:T(8,128)(2,1)}), bf16[8,680,768]{2,0,1:T(8,128)(2,1)}) %all-gather.21.cloned.1.call-update) | async-done | bytes 8355856 | tf_op jit(solution)/shard_map/all_gather | solution.py:251
  2042.4 12.3 fusion.57
  2054.7 137.0 %all-gather.23.cloned.1.call-done = bf16[8,680,768]{2,0,1:T(8,128)(2,1)} async-done(((bf16[8,170,768]{2,0,1:T(8,128)(2,1)}), bf16[8,680,768]{2,0,1:T(8,128)(2,1)}) %all-gather.23.cloned.1.call-update) | async-done | bytes 8355856 | tf_op jit(solution)/shard_map/all_gather | solution.py:252
  2191.7 12.0 fusion.62
  2203.7 12.5 reduce-scatter.16.cloned.1.call-done
  2216.2 24.8 reduce-scatter.18.cloned.1.call-done
  2240.9 87.4 %reduce-scatter.14.cloned.1.call-done = bf16[384,1536]{1,0:T(8,128)(2,1)} async-done(((bf16[1536,1536]{1,0:T(8,128)(2,1)}), bf16[384,1536]{1,0:T(8,128)(2,1)}) %reduce-scatter.14.cloned.1.call-update) | async-done | bytes 1179664 | tf_op jit(solution)/shard_map/reduce_scatter | solution.py:437
  2328.4 88.5 %reduce-scatter.20.cloned.1.call-done = bf16[384,1536]{1,0:T(8,128)(2,1)} async-done(((bf16[1536,1536]{1,0:T(8,128)(2,1)}), bf16[384,1536]{1,0:T(8,128)(2,1)}) %reduce-scatter.20.cloned.1.call-update) | async-done | bytes 1179664 | tf_op jit(solution)/shard_map/reduce_scatter | solution.py:446
  2425.6 15.2 reduce-scatter.22.cloned.1.call-done
  2445.5 8.9 all-reduce.4
  2454.5 13.0 all-reduce.2
  2472.1 195.5 %all-reduce.7.cloned.1.call-done = (bf16[384,1536]{1,0:T(8,128)(2,1)}, bf16[384,256]{1,0:T(8,128)(2,1)}, bf16[384,256]{1,0:T(8,128)(2,1)}, bf16[384,1536]{1,0:T(...) async-done(((bf16[384,1536]{1,0:T(8,128)(2,1)}, bf16[384,256]{1,0:T(8,128)(2,1)}, ...) | async-done | bytes 16908304 | tf_op jit(solution)/shard_map/psum | solution.py:452
  (351 shorter events, 235.1 us)
Async XLA Ops:
  7.2 167.7 %all-gather.11.cloned.1.call-start = ((), (), s32[]{:S(2)}) async-start(), calls=%async_computation.9 | async-start | bytes 5898240 | tf_op jit(solution)/shard_map/all_gather | solution.py:63
  7.9 214.9 %all-gather.13.cloned.1.call-start = ((), (), s32[]{:S(2)}) async-start(), calls=%async_computation.10 | async-start | bytes 5898240 | tf_op jit(solution)/shard_map/all_gather | solution.py:66
  8.7 537.3 %all-gather.15.cloned.1.call-start = ((), (), s32[]{:S(2)}) async-start(), calls=%async_computation.11 | async-start | bytes 23592960 | tf_op jit(solution)/shard_map/all_gather | solution.py:74
  9.4 859.4 %all-gather.17.cloned.1.call-start = ((), (), s32[]{:S(2)}) async-start(), calls=%async_computation.12 | async-start | bytes 23592960 | tf_op jit(solution)/shard_map/all_gather | solution.py:75
  10.0 14.7 copy-start.44
  10.0 45.4 %copy-start.6 = (bf16[1,256,1536]{2,1,0:T(8,128)(2,1)S(1)}, bf16[1,256,1536]{2,1,0:T(8,128)(2,1)}, u32[]{:S(2)}) copy-start(bf16[1,256,1536]{2,1,0:T(8,128)(2,1)} %param.19) | copy-start | bytes 2359300
  10.0 1181.6 %all-gather.19.cloned.1.call-start = ((), (), s32[]{:S(2)}) async-start(), calls=%async_computation.13 | async-start | bytes 23592960 | tf_op jit(solution)/shard_map/all_gather | solution.py:76
  10.6 1373.3 %reduce-scatter.10.cloned.1.call-start = ((), (), s32[]{:S(2)}) async-start(), calls=%async_computation.14 | async-start | bytes 655360 | tf_op jit(solution)/shard_map/reduce_scatter | solution.py:376
  24.7 156.9 %copy-start.36 = (f32[1536]{0:T(1024)}, f32[1536]{0:T(1024)S(1)}, u32[]{:S(2)}) copy-start(f32[1536]{0:T(1024)S(1)} %reshape.524) | copy-start | bytes 18436
  55.1 25.4 copy-start.27
  55.4 130.2 %copy-start.23 = (f32[256,128]{0,1:T(8,128)}, f32[256,128]{0,1:T(8,128)S(1)}, u32[]{:S(2)}) copy-start(f32[256,128]{0,1:T(8,128)S(1)} %pad_maximum_fusion.2) | copy-start | bytes 393220
  55.5 130.2 %copy-start.25 = (f32[256,128]{0,1:T(8,128)}, f32[256,128]{0,1:T(8,128)S(1)}, u32[]{:S(2)}) copy-start(f32[256,128]{0,1:T(8,128)S(1)} %pad_maximum_fusion.3) | copy-start | bytes 393220
  55.7 24.1 copy-start.51
  87.0 10.2 copy-start.34
  87.0 31.9 %copy-start.45 = (bf16[384,256]{1,0:T(8,128)(2,1)S(1)}, bf16[384,256]{1,0:T(8,128)(2,1)}, u32[]{:S(2)}) copy-start(bf16[384,256]{1,0:T(8,128)(2,1)} %param.25) | copy-start | bytes 589828
  96.5 41.3 %copy-start.52 = (f32[256]{0:T(256)S(1)}, f32[256]{0:T(256)}, u32[]{:S(2)}) copy-start(f32[256]{0:T(256)} %copy-done.51) | copy-start | bytes 3076
  118.9 41.9 %copy-start.60 = (bf16[384,8]{0,1:T(8,128)(2,1)S(1)}, bf16[384,8]{0,1:T(8,128)(2,1)}, u32[]{:S(2)}) copy-start(bf16[384,8]{0,1:T(8,128)(2,1)} %param.28) | copy-start | bytes 18436
  118.9 56.0 %copy-start.58 = (s32[1024,1]{0,1:T(1,128)S(1)}, s32[1024,1]{0,1:T(1,128)}, u32[]{:S(2)}) copy-start(s32[1024,1]{0,1:T(1,128)} %copy-done.57) | copy-start | bytes 12292
  174.8 59.3 %copy-start.40 = (bf16[1536,8]{0,1:T(8,128)(2,1)}, bf16[1536,8]{0,1:T(8,128)(2,1)S(1)}, u32[]{:S(2)}) copy-start(bf16[1536,8]{0,1:T(8,128)(2,1)S(1)} %all_gather.65) | copy-start | bytes 73732
  201.6 25.1 copy-start.38
  202.9 23.8 copy-start.11
  226.7 7.4 copy-start.54
  1206.9 14.2 copy-start.16
  1241.5 7.7 copy-start.1
  1259.1 12.9 copy-start.15
  1314.4 6.7 copy-start.55
  1352.9 53.1 %reduce-scatter.12.cloned.1.call-start = ((), (), s32[]{:S(2)}) async-start(), calls=%async_computation.15 | async-start | bytes 655360 | tf_op jit(solution)/shard_map/reduce_scatter | solution.py:384
  1353.7 539.8 %all-gather.25.cloned.1.call-start = ((), (), s32[]{:S(2)}) async-start(), calls=%async_computation.22 | async-start | bytes 20889600 | tf_op jit(solution)/shard_map/all_gather | solution.py:253
  1360.3 682.0 %all-gather.21.cloned.1.call-start = ((), (), s32[]{:S(2)}) async-start(), calls=%async_computation.20 | async-start | bytes 10444800 | tf_op jit(solution)/shard_map/all_gather | solution.py:251
  1364.0 20.9 copy-start.26
  1364.0 827.7 %all-gather.23.cloned.1.call-start = ((), (), s32[]{:S(2)}) async-start(), calls=%async_computation.21 | async-start | bytes 10444800 | tf_op jit(solution)/shard_map/all_gather | solution.py:252
  1367.7 18.4 copy-start.7
  1367.7 18.4 copy-start.37
  1367.7 18.4 copy-start.53
  1367.7 848.4 %reduce-scatter.16.cloned.1.call-start = ((), (), s32[]{:S(2)}) async-start(), calls=%async_computation.17 | async-start | bytes 983040 | tf_op jit(solution)/shard_map/reduce_scatter | solution.py:440
  1387.5 853.4 %reduce-scatter.18.cloned.1.call-start = ((), (), s32[]{:S(2)}) async-start(), calls=%async_computation.18 | async-start | bytes 983040 | tf_op jit(solution)/shard_map/reduce_scatter | solution.py:443
  1408.4 919.9 %reduce-scatter.14.cloned.1.call-start = ((), (), s32[]{:S(2)}) async-start(), calls=%async_computation.16 | async-start | bytes 5898240 | tf_op jit(solution)/shard_map/reduce_scatter | solution.py:437
  1417.5 999.4 %reduce-scatter.20.cloned.1.call-start = ((), (), s32[]{:S(2)}) async-start(), calls=%async_computation.19 | async-start | bytes 5898240 | tf_op jit(solution)/shard_map/reduce_scatter | solution.py:446
  1433.1 311.7 %all-to-all-start = ((bf16[8,170,1536]{1,0,2:T(8,128)(2,1)}), bf16[8,170,1536]{1,0,2:T(8,128)(2,1)}, u32[]{:S(2)}, u32[]{:S(2)}) async-start(bf16[8,170,1536]{1,0,2:T(8,128)(2,1)} %copy.151), calls=%async_computation.6 | async-start | bytes 12582912 | tf_op jit(solution)/shard_map/all_to_all | solution.py:247
  1744.8 126.2 %all-to-all-start.1 = ((bf16[8,170,768]{1,0,2:T(8,128)(2,1)}), bf16[8,170,768]{1,0,2:T(8,128)(2,1)}, u32[]{:S(2)}, u32[]{:S(2)}) async-start(bf16[8,170,768]{1,0,2:T(8,128)(2,1)} %copy.160), calls=%async_computation.7 | async-start | bytes 6291456 | tf_op jit(solution)/shard_map/all_to_all | solution.py:248
  1749.5 691.3 %reduce-scatter.22.cloned.1.call-start = ((), (), s32[]{:S(2)}) async-start(), calls=%async_computation.23 | async-start | bytes 491520
  1768.2 899.3 %all-reduce.7.cloned.1.call-start = ((), (), s32[]{:S(2)}) async-start(), calls=%async_computation.24 | async-start | bytes 33816576 | tf_op jit(solution)/shard_map/psum | solution.py:452
  2420.6 21.1 copy-start.18
  2425.6 18.1 copy-start.30
  2425.6 18.1 copy-start.48
  2443.7 25.7 copy-start.14
  2667.6 7.3 copy-start.22
  2667.6 11.9 slice-start.2
  (38 other events, 133.3 us)
Sparse Core Ops, SparseCore 0:
  9.6 115.8 all-gather.10
  127.0 95.7 all-gather.12
  224.4 321.4 all-gather.14
  547.4 321.3 all-gather.16
  870.2 321.3 all-gather.18
  1353.1 30.7 reduce-scatter.9
  1386.2 19.8 reduce-scatter.11
  1407.6 485.8 all-gather.24
  1895.1 147.2 all-gather.20
  2044.4 147.3 all-gather.22
  2194.6 21.5 reduce-scatter.15
  2218.3 22.5 reduce-scatter.17
  2243.8 84.5 reduce-scatter.13
  2331.1 85.7 reduce-scatter.19
  2419.6 21.0 reduce-scatter.21
  2447.1 220.4 all-reduce.6
where the time goes:
time: 2700 us
  waiting for transfers between devices  2070 us (77%)
  local copies, waits for them, and re-layouts  194 us (7%)
  matrix products  185 us (7%)
  blocking collectives  152 us (6%)
  other arithmetic  68.5 us (3%)
    all_gather x1, waiting for transfers between devices, gather_mixture(): lax.all_gather(w_up, 'cp', axis=1, tiled=True)  309 us
    all_gather x1, waiting for transfers between devices, gather_mixture(): lax.all_gather(w_down, 'cp', axis=1, tiled=True)  309 us
    all_to_all x1, waiting for transfers between devices, local(): lax.all_to_all(expert_in, 'cp', split_axis=2, concat_axis=1, tiled=True)  301 us
    all_gather x1, waiting for transfers between devices, gather_mixture(): lax.all_gather(w_gate, 'cp', axis=1, tiled=True)  289 us
    psum x1, waiting for transfers between devices, local(): lax.psum(attn_sums[1].astype(jnp.bfloat16), 'dp').astype(jnp.float32)  195 us
    all_gather x1, waiting for transfers between devices, local(): lax.all_gather(up_pre_grad, 'cp', axis=1, tiled=True)  137 us
    all_gather x1, waiting for transfers between devices, local(): lax.all_gather(gate_pre_grad, 'cp', axis=1, tiled=True)  128 us
    all_to_all x1, waiting for transfers between devices, local(): lax.all_to_all(active_low, 'cp', split_axis=2, concat_axis=1, tiled=True)  103 us
  transfers between devices with their start and end apart: 18, of which 17 were waited for; matrix products, arithmetic and copies ran while one was open for 10% of the time, Pallas kernels for 0%

commit v1 on v0

v1 whole, which is shorter than its diff:
```python
import functools
import math

import jax
import jax.numpy as jnp
from jax import lax
from jax.experimental import pallas as pl
from jax.experimental.pallas import tpu as pltpu
from jax.sharding import PartitionSpec as P

MODEL_WIDTH = 1536
QUERY_HEADS = 12
KEY_VALUE_HEADS = 2
HEAD_WIDTH = 128
EXPERTS = 8
TOPK = 4
BLK = 256

norm_eps = 1e-06
rope_base = 1000000.0
mask_fill = -1e30
score_scale = 1.0 / math.sqrt(HEAD_WIDTH)
query_columns = QUERY_HEADS * HEAD_WIDTH
key_columns = KEY_VALUE_HEADS * HEAD_WIDTH
group_heads = QUERY_HEADS // KEY_VALUE_HEADS

f32 = jnp.float32
bf16 = jnp.bfloat16


def dot_nn(a, b):
    return lax.dot_general(a, b, (((1,), (0,)), ((), ())), preferred_element_type=f32)


def dot_nt(a, b):
    return lax.dot_general(a, b, (((1,), (1,)), ((), ())), preferred_element_type=f32)


def dot_tn(a, b):
    return lax.dot_general(a, b, (((0,), (0,)), ((), ())), preferred_element_type=f32)


def params(megabytes):
    return pltpu.CompilerParams(vmem_limit_bytes=megabytes * 1024 * 1024)


def project_kernel(chunk_heads, slot_ref, h_ref, w_ref, cos_ref, sin_ref, out_ref):
    j = pl.program_id(0)
    full = dot_nn(h_ref[...], w_ref[0])
    for k in range(chunk_heads):
        u = full[:, k * HEAD_WIDTH : (k + 1) * HEAD_WIDTH]
        turned = u * cos_ref[...] + pltpu.roll(u, HEAD_WIDTH // 2, 1) * sin_ref[...]
        is_value = j * chunk_heads + k >= QUERY_HEADS + KEY_VALUE_HEADS
        out_ref[:, k * HEAD_WIDTH : (k + 1) * HEAD_WIDTH] = jnp.where(is_value, u, turned).astype(bf16)


def project(slot_of, h, w_rel, cos, sin):
    m, d, cw = w_rel.shape
    t = h.shape[0]
    return pl.pallas_call(
        functools.partial(project_kernel, cw // HEAD_WIDTH),
        grid_spec=pltpu.PrefetchScalarGridSpec(
            num_scalar_prefetch=1,
            grid=(m,),
            in_specs=[
                pl.BlockSpec((t, d), lambda j, s: (0, 0)),
                pl.BlockSpec((1, d, cw), lambda j, s: (s[j], 0, 0)),
                pl.BlockSpec((t, HEAD_WIDTH), lambda j, s: (0, 0)),
                pl.BlockSpec((t, HEAD_WIDTH), lambda j, s: (0, 0)),
            ],
            out_specs=pl.BlockSpec((t, cw), lambda j, s: (0, j)),
        ),
        out_shape=jax.ShapeDtypeStruct((t, m * cw), bf16),
        compiler_params=params(24),
        cost_estimate=pl.CostEstimate(
            flops=2 * t * d * m * cw, bytes_accessed=2 * d * m * cw, transcendentals=0
        ),
        name="project",
    )(slot_of, h, w_rel, cos, sin)


def project_back_kernel(chunk_ref, h_ref, g_ref, w_ref, dh_ref, gw_ref):
    @pl.when(pl.program_id(0) == 0)
    def _():
        dh_ref[...] = jnp.zeros_like(dh_ref)

    dh_ref[...] += dot_nt(g_ref[...], w_ref[0])
    gw_ref[0] = dot_tn(h_ref[...], g_ref[...]).astype(bf16)


def project_back(chunk_of, h, grad, w_rel):
    m, d, cw = w_rel.shape
    t = h.shape[0]
    return pl.pallas_call(
        project_back_kernel,
        grid_spec=pltpu.PrefetchScalarGridSpec(
            num_scalar_prefetch=1,
            grid=(m,),
            in_specs=[
                pl.BlockSpec((t, d), lambda j, c: (0, 0)),
                pl.BlockSpec((t, cw), lambda j, c: (0, c[j])),
                pl.BlockSpec((1, d, cw), lambda j, c: (j, 0, 0)),
            ],
            out_specs=[
                pl.BlockSpec((t, d), lambda j, c: (0, 0)),
                pl.BlockSpec((1, d, cw), lambda j, c: (j, 0, 0)),
            ],
        ),
        out_shape=[
            jax.ShapeDtypeStruct((t, d), f32),
            jax.ShapeDtypeStruct((m, d, cw), bf16),
        ],
        compiler_params=params(32),
        cost_estimate=pl.CostEstimate(
            flops=4 * t * d * m * cw, bytes_accessed=4 * d * m * cw, transcendentals=0
        ),
        name="project_back",
    )(chunk_of, h, grad, w_rel)


def attend_kernel(seen_ref, q_ref, k_ref, v_ref, out_ref):
    s = dot_nt(q_ref[...], k_ref[...]) * score_scale
    col = lax.broadcasted_iota(jnp.int32, s.shape, 1)
    s = jnp.where(col < seen_ref[0], s, mask_fill)
    e = jnp.exp(s - jnp.max(s, 1, keepdims=True))
    p = (e / jnp.sum(e, 1, keepdims=True)).astype(bf16)
    out_ref[...] = dot_nn(p, v_ref[...]).astype(bf16)


def attend(seen, qkv, kv):
    t, rows = qkv.shape[0], kv.shape[0]
    return pl.pallas_call(
        attend_kernel,
        grid_spec=pltpu.PrefetchScalarGridSpec(
            num_scalar_prefetch=1,
            grid=(QUERY_HEADS,),
            in_specs=[
                pl.BlockSpec((t, HEAD_WIDTH), lambda j, s: (0, j)),
                pl.BlockSpec((rows, HEAD_WIDTH), lambda j, s: (0, j // group_heads)),
                pl.BlockSpec((rows, HEAD_WIDTH), lambda j, s: (0, KEY_VALUE_HEADS + j // group_heads)),
            ],
            out_specs=pl.BlockSpec((t, HEAD_WIDTH), lambda j, s: (0, j)),
        ),
        out_shape=jax.ShapeDtypeStruct((t, query_columns), bf16),
        compiler_params=params(40),
        cost_estimate=pl.CostEstimate(
            flops=4 * t * rows * query_columns,
            bytes_accessed=4 * t * query_columns,
            transcendentals=t * rows * QUERY_HEADS,
        ),
        name="attend",
    )(seen, qkv, kv, kv)


def attend_back_kernel(seen_ref, q_ref, k_ref, v_ref, g_ref, cos_ref, sin_ref, dq_ref, dkv_ref, dk_acc, dv_acc):
    j = pl.program_id(0)
    q, k, g = q_ref[...], k_ref[...], g_ref[...]
    s = dot_nt(k, q) * score_scale
    row = lax.broadcasted_iota(jnp.int32, s.shape, 0)
    s = jnp.where(row < seen_ref[0], s, mask_fill)
    e = jnp.exp(s - jnp.max(s, 0, keepdims=True))
    p = e / jnp.sum(e, 0, keepdims=True)
    pb = p.astype(bf16)
    dp = dot_nt(v_ref[...], g)
    delta = jnp.sum(p * dp, 0, keepdims=True)
    ds = (p * (dp - delta)).astype(bf16)
    dq = dot_tn(ds, k) * score_scale
    dq_ref[...] = (dq * cos_ref[...] - pltpu.roll(dq, HEAD_WIDTH // 2, 1) * sin_ref[...]).astype(bf16)

    @pl.when(j % group_heads == 0)
    def _():
        dk_acc[...] = jnp.zeros_like(dk_acc)
        dv_acc[...] = jnp.zeros_like(dv_acc)

    dk_acc[...] += dot_nn(ds, q) * score_scale
    dv_acc[...] += dot_nn(pb, g)

    @pl.when(j % group_heads == group_heads - 1)
    def _():
        dkv_ref[0] = dk_acc[...].astype(bf16)
        dkv_ref[1] = dv_acc[...].astype(bf16)


def attend_back(seen, qkv, kv, grad, cos, sin):
    t, rows = qkv.shape[0], kv.shape[0]
    return pl.pallas_call(
        attend_back_kernel,
        grid_spec=pltpu.PrefetchScalarGridSpec(
            num_scalar_prefetch=1,
            grid=(QUERY_HEADS,),
            in_specs=[
                pl.BlockSpec((t, HEAD_WIDTH), lambda j, s: (0, j)),
                pl.BlockSpec((rows, HEAD_WIDTH), lambda j, s: (0, j // group_heads)),
                pl.BlockSpec((rows, HEAD_WIDTH), lambda j, s: (0, KEY_VALUE_HEADS + j // group_heads)),
                pl.BlockSpec((t, HEAD_WIDTH), lambda j, s: (0, j)),
                pl.BlockSpec((t, HEAD_WIDTH), lambda j, s: (0, 0)),
                pl.BlockSpec((t, HEAD_WIDTH), lambda j, s: (0, 0)),
            ],
            out_specs=[
                pl.BlockSpec((t, HEAD_WIDTH), lambda j, s: (0, j)),
                pl.BlockSpec((2, rows, HEAD_WIDTH), lambda j, s: (0, 0, j // group_heads)),
            ],
            scratch_shapes=[pltpu.VMEM((rows, HEAD_WIDTH), f32)] * 2,
        ),
        out_shape=[
            jax.ShapeDtypeStruct((t, query_columns), bf16),
            jax.ShapeDtypeStruct((2, rows, key_columns), bf16),
        ],
        compiler_params=params(56),
        cost_estimate=pl.CostEstimate(
            flops=10 * t * rows * query_columns,
            bytes_accessed=8 * t * query_columns,
            transcendentals=t * rows * QUERY_HEADS,
        ),
        name="attend_back",
    )(seen, qkv, kv, kv, grad, cos, sin)


def experts_kernel(
    fc, h_ref, z_ref, gate_ref, wg_ref, wu_ref, wd_ref,
    a_ref, dg_ref, du_ref, eo_ref, dh_ref, dgate_ref, eo_acc, dh_acc, dgate_acc,
):
    step = pl.program_id(0)
    ct = a_ref.shape[1]
    wg = wg_ref[...].reshape(ct, wg_ref.shape[-1])
    wu = wu_ref[...].reshape(ct, wu_ref.shape[-1])
    wd = wd_ref[...].reshape(ct, wd_ref.shape[-1])
    slot_row = lax.broadcasted_iota(jnp.int32, (gate_ref.shape[0], ct), 0)
    slot_col = lax.broadcasted_iota(jnp.int32, (gate_ref.shape[0], ct), 1) + step * ct
    low = slot_row * fc
    pick = jnp.where((slot_col >= low) & (slot_col < low + fc), 1.0, 0.0).astype(bf16)
    gates = gate_ref[...]
    gates_high = gates.astype(bf16)
    gates_low = (gates - gates_high.astype(f32)).astype(bf16)
    wide = dot_tn(gates_high, pick) + dot_tn(gates_low, pick)
    g = dot_nt(h_ref[...], wg)
    u = dot_nt(h_ref[...], wu)
    e = dot_nt(z_ref[...], wd)
    sig = 1.0 / (1.0 + jnp.exp(-g))
    swish = g * sig
    a = swish * u
    da = e * wide
    ab = (a * wide).astype(bf16)
    dg = (da * u * (sig * (1.0 + g * (1.0 - sig)))).astype(bf16)
    du = (da * swish).astype(bf16)
    a_ref[...] = ab
    dg_ref[...] = dg
    du_ref[...] = du

    @pl.when(step == 0)
    def _():
        eo_acc[...] = jnp.zeros_like(eo_acc)
        dh_acc[...] = jnp.zeros_like(dh_acc)
        dgate_acc[...] = jnp.zeros_like(dgate_acc)

    dgate_acc[...] += dot_nt(pick, (a * e).astype(bf16))
    eo_acc[...] += dot_nn(ab, wd)
    dh_acc[...] += dot_nn(dg, wg) + dot_nn(du, wu)

    @pl.when(step == pl.num_programs(0) - 1)
    def _():
        eo_ref[...] = eo_acc[...].astype(eo_ref.dtype)
        dh_ref[...] = dh_acc[...].astype(dh_ref.dtype)
        dgate_ref[...] = dgate_acc[...]


def experts(h, z, gates, wg, wu, wd, sent_type):
    t, d = h.shape
    m, fc = wg.shape[0], wg.shape[1]
    width = m * fc
    ct = min(width, 384)
    per = ct // fc
    w_spec = pl.BlockSpec((per, fc, d), lambda j: (j, 0, 0))
    rows = pl.BlockSpec((t, d), lambda j: (0, 0))
    tile = pl.BlockSpec((t, ct), lambda j: (0, j))
    slots = pl.BlockSpec(gates.shape, lambda j: (0, 0))
    return pl.pallas_call(
        functools.partial(experts_kernel, fc),
        grid=(width // ct,),
        in_specs=[rows, rows, slots, w_spec, w_spec, w_spec],
        out_specs=[tile, tile, tile, rows, rows, slots],
        out_shape=[
            jax.ShapeDtypeStruct((t, width), bf16),
            jax.ShapeDtypeStruct((t, width), bf16),
            jax.ShapeDtypeStruct((t, width), bf16),
            jax.ShapeDtypeStruct((t, d), sent_type),
            jax.ShapeDtypeStruct((t, d), sent_type),
            jax.ShapeDtypeStruct(gates.shape, f32),
        ],
        scratch_shapes=[
            pltpu.VMEM((t, d), f32),
            pltpu.VMEM((t, d), f32),
            pltpu.VMEM(gates.shape, f32),
        ],
        compiler_params=params(44),
        cost_estimate=pl.CostEstimate(
            flops=12 * t * d * width, bytes_accessed=6 * d * width, transcendentals=t * width
        ),
        name="experts",
    )(h, z, gates, wg, wu, wd)


def expert_grads_kernel(n, fc, *refs):
    a, dg, du = refs[:n], refs[n : 2 * n], refs[2 * n : 3 * n]
    h, z, out_ref = refs[3 * n : 4 * n], refs[4 * n : 5 * n], refs[5 * n]
    per = out_ref.shape[0]
    for which, (left, right) in enumerate(((dg, h), (du, h), (a, z))):
        total = dot_tn(left[0][...], right[0][...])
        for s in range(1, n):
            total += dot_tn(left[s][...], right[s][...])
        out_ref[:, which] = total.astype(bf16).reshape(per, fc, total.shape[-1])


def expert_grads(fc, a, dg, du, h, z):
    n = len(a)
    t, width = a[0].shape
    d = h[0].shape[1]
    ct = min(width, 384)
    per = ct // fc
    tile = pl.BlockSpec((t, ct), lambda j: (0, j))
    rows = pl.BlockSpec((t, d), lambda j: (0, 0))
    return pl.pallas_call(
        functools.partial(expert_grads_kernel, n, fc),
        grid=(width // ct,),
        in_specs=[tile] * (3 * n) + [rows] * (2 * n),
        out_specs=pl.BlockSpec((per, 3, fc, d), lambda j: (j, 0, 0, 0)),
        out_shape=jax.ShapeDtypeStruct((width // fc, 3, fc, d), bf16),
        compiler_params=params(58),
        cost_estimate=pl.CostEstimate(
            flops=6 * n * t * d * width, bytes_accessed=6 * d * width, transcendentals=0
        ),
        name="expert_grads",
    )(*a, *dg, *du, *h, *z)


def pick_kernel(where_ref, in_ref, out_ref):
    out_ref[...] = in_ref[...].reshape(out_ref.shape).astype(out_ref.dtype)


def reorder(where, stacked):
    m = stacked.shape[0]
    block = (1,) + stacked.shape[1:]
    tail = (0,) * (stacked.ndim - 1)
    return pl.pallas_call(
        pick_kernel,
        grid_spec=pltpu.PrefetchScalarGridSpec(
            num_scalar_prefetch=1,
            grid=(m,),
            in_specs=[pl.BlockSpec(block, lambda j, w: (w[j],) + tail)],
            out_specs=pl.BlockSpec(block, lambda j, w: (j,) + tail),
        ),
        out_shape=jax.ShapeDtypeStruct(stacked.shape, stacked.dtype),
        compiler_params=params(16),
        cost_estimate=pl.CostEstimate(flops=0, bytes_accessed=4 * stacked.size, transcendentals=0),
        name="reorder",
    )(where, stacked)


def reorder_rows(where, stacked, inner_first):
    m, n, c, d = stacked.shape if inner_first else (stacked.shape[1], stacked.shape[0]) + stacked.shape[2:]
    one, two = (1, n, c, d), (n, 1, c, d)
    pick_m, put_m = (lambda j, w: (w[j], 0, 0, 0)), (lambda j, w: (j, 0, 0, 0))
    pick_n, put_n = (lambda j, w: (0, w[j], 0, 0)), (lambda j, w: (0, j, 0, 0))
    return pl.pallas_call(
        pick_kernel,
        grid_spec=pltpu.PrefetchScalarGridSpec(
            num_scalar_prefetch=1,
            grid=(m,),
            in_specs=[pl.BlockSpec(one, pick_m) if inner_first else pl.BlockSpec(two, pick_n)],
            out_specs=pl.BlockSpec(two, put_n) if inner_first else pl.BlockSpec(one, put_m),
        ),
        out_shape=jax.ShapeDtypeStruct((n, m, c, d) if inner_first else (m, n, c, d), stacked.dtype),
        compiler_params=params(16),
        cost_estimate=pl.CostEstimate(flops=0, bytes_accessed=4 * stacked.size, transcendentals=0),
        name="reorder_rows",
    )(where, stacked)


def spread_kernel(half, slot_ref, near_ref, far_ref, out_ref):
    near = slot_ref[pl.program_id(0)] < half

    @pl.when(near)
    def _():
        out_ref[...] = near_ref[...].astype(f32)

    @pl.when(jnp.logical_not(near))
    def _():
        out_ref[...] = far_ref[...].astype(f32)


def spread(slot_of, near, far):
    half = near.shape[0]
    block = (1,) + near.shape[1:]
    tail = (0,) * (near.ndim - 1)
    return pl.pallas_call(
        functools.partial(spread_kernel, half),
        grid_spec=pltpu.PrefetchScalarGridSpec(
            num_scalar_prefetch=1,
            grid=(2 * half,),
            in_specs=[
                pl.BlockSpec(block, lambda j, s: (jnp.minimum(s[j], half - 1),) + tail),
                pl.BlockSpec(block, lambda j, s: (jnp.maximum(s[j] - half, 0),) + tail),
            ],
            out_specs=pl.BlockSpec(block, lambda j, s: (j,) + tail),
        ),
        out_shape=jax.ShapeDtypeStruct((2 * half,) + near.shape[1:], f32),
        compiler_params=params(16),
        cost_estimate=pl.CostEstimate(flops=0, bytes_accessed=12 * near.size, transcendentals=0),
        name="spread",
    )(slot_of, near, far)


class Along:
    def __init__(self):
        self.n, self.m = lax.axis_size("cp"), lax.axis_size("dp")
        self.r, self.i = lax.axis_index("cp"), lax.axis_index("dp")
        self.bits = self.m.bit_length() - 1
        assert 1 << self.bits == self.m and self.bits > 1
        self.inner = self.bits - 1
        slots = jnp.arange(self.m, dtype=jnp.int32)
        self.chunk_of = self.i ^ (((slots & (self.m // 2 - 1)) << 1) | (slots >> self.inner))
        offset = slots ^ self.i
        self.slot_of = (offset >> 1) | ((offset & 1) << self.inner)

    def swap(self, x, bit):
        mask = 1 if bit == self.inner else 2 << bit
        return lax.ppermute(x, "dp", [(k, k ^ mask) for k in range(self.m)])

    def shift(self, x, s):
        return lax.ppermute(x, "cp", [(k, (k + s) % self.n) for k in range(self.n)])

    def shift_up(self, x, s):
        return lax.ppermute(x, "cp", [(k, k + s) for k in range(self.n - s)])

    def shift_down(self, x, s):
        return lax.ppermute(x, "cp", [(k + s, k) for k in range(self.n - s)])

    def orders(self):
        up = list(range(self.inner))
        return up, up[::-1]

    def gather_dp(self, x, order):
        buffer, held = x[None], [0]
        for bit in order:
            got = self.swap(buffer, bit)
            buffer = jnp.concatenate([buffer, got], 0)
            held = held + [h | 1 << bit for h in held]
        if held != sorted(held):
            buffer = jnp.concatenate([buffer[held.index(h)][None] for h in sorted(held)], 0)
        return buffer, self.swap(buffer, self.inner)

    def halve_core(self, x):
        half = self.m // 2
        return (x[:half].astype(f32) + self.swap(x[half:], self.inner).astype(f32)).astype(bf16)

    def halve(self, x, order):
        held = list(range(self.m // 2))
        parts = {h: x[h] for h in held}
        for bit in order:
            sent = [h for h in held if h >> bit & 1]
            held = [h for h in held if not h >> bit & 1]
            got = self.swap(jnp.stack([parts[h].astype(bf16) for h in sent]), bit)
            for k, h in enumerate(held):
                parts[h] = parts[h].astype(f32) + got[k].astype(f32)
        return parts[0]

    def pieces(self, x, s):
        return lax.dynamic_index_in_dim(x, (self.r + s) % self.n, 0, keepdims=False)

    def scatter_cp(self, x):
        return [self.pieces(x, 0)] + [self.shift(self.pieces(x, s), s) for s in range(1, self.n)]

    def ranked(self, slots):
        back = slots[::-1]
        line = jnp.stack(back + back[:-1])
        return lax.dynamic_slice_in_dim(line, self.n - 1 - self.r, self.n, 0)

    def gather_cp(self, x):
        return self.ranked([x] + [self.shift(x, s) for s in range(1, self.n)])


def norm_forward(values, gain_vec):
    inverse = lax.rsqrt(jnp.mean(values * values, -1, keepdims=True) + norm_eps)
    scaled = values * inverse
    return (scaled * gain_vec, scaled, inverse)


def norm_backward(gradient, gain_vec, scaled, inverse):
    gain_grad = jnp.sum(gradient * scaled, 0)
    inner_vals = gradient * gain_vec
    return (
        inverse * (inner_vals - scaled * jnp.mean(inner_vals * scaled, -1, keepdims=True)),
        gain_grad,
    )


def rotary(positions):
    half = HEAD_WIDTH // 2
    frequency = rope_base ** (-2.0 * jnp.arange(half, dtype=f32) / HEAD_WIDTH)
    angles = positions.astype(f32)[:, None] * frequency[None, :]
    cos, sin = jnp.cos(angles), jnp.sin(angles)
    return jnp.concatenate([cos, cos], 1), jnp.concatenate([-sin, sin], 1)


def local(
    tokens, routes, out_grad, norm_attn, w_query, key_weight, value_weight, w_out,
    norm_mix, w_router, w_gate, w_up, w_down,
):
    along = Along()
    n, m, r, i = along.n, along.m, along.r, along.i
    t, d = tokens.shape[1], tokens.shape[2]
    assert t == BLK
    dl, ff, fs = w_query.shape[0], w_gate.shape[2], w_down.shape[1]
    sub = m // EXPERTS
    fc = fs // sub
    rc = dl // m
    up_order, down_order = along.orders()
    inputs = tokens[0].astype(f32)
    route_rows = routes[0]
    dz = out_grad[0]

    w_qkv = jnp.concatenate([w_query, key_weight, value_weight], 1)
    cw = w_qkv.shape[1] // m
    own_qkv = along.gather_cp(lax.dynamic_slice_in_dim(w_qkv, i * cw, cw, 1)).reshape(d, cw)
    small = jnp.concatenate([norm_attn[None], norm_mix[None], w_router.T], 0)
    small = jnp.swapaxes(along.gather_cp(small), 0, 1).reshape(2 + EXPERTS, d)
    gain_one, gain_two = small[0].astype(f32), small[1].astype(f32)
    router = small[2:]
    qkv_a = along.gather_dp(own_qkv[: d // 2], up_order)
    qkv_b = along.gather_dp(own_qkv[d // 2 :], down_order)
    w_rel = jnp.concatenate([jnp.concatenate(qkv_a, 0), jnp.concatenate(qkv_b, 0)], 1)

    normed_one, scaled_one, inverse_one = norm_forward(inputs, gain_one)
    h1 = normed_one.astype(bf16)
    cos, sin = rotary(r * t + jnp.arange(t, dtype=jnp.int32))
    qkv = project(along.slot_of, h1, w_rel, cos, sin)
    own_kv = qkv[:, query_columns:]
    kv = jnp.concatenate([own_kv] + [along.shift_up(own_kv, s) for s in range(1, n)], 0)
    seen = ((r + 1) * t).reshape(1)
    ob = attend(seen, qkv, kv)

    expert_chunk = i // sub
    flipped = [
        lax.dynamic_index_in_dim(w, expert_chunk, 0, keepdims=False).T.reshape(n, sub, fc, dl)
        for w in (w_gate, w_up)
    ]
    flipped = jnp.stack(flipped, 1)
    flipped = lax.dynamic_index_in_dim(flipped, i % sub, 2, keepdims=False)
    gate_up = along.ranked(along.scatter_cp(flipped))
    gate_up = jnp.transpose(gate_up, (1, 2, 0, 3)).reshape(2, fc, d)
    own_out = along.gather_cp(lax.dynamic_slice_in_dim(w_out, i * rc, rc, 0))
    own_out = own_out.reshape(2, n * rc // 2, d)
    mix_a = along.gather_dp(jnp.concatenate([gate_up[0], own_out[0]], 0), up_order)
    mix_b = along.gather_dp(jnp.concatenate([gate_up[1], own_out[1]], 0), down_order)
    wg = jnp.concatenate([x[:, :fc] for x in mix_a], 0)
    wu = jnp.concatenate([x[:, :fc] for x in mix_b], 0)
    out_rel = jnp.concatenate(
        [jnp.concatenate([a[:, fc:], b[:, fc:]], 1) for a, b in zip(mix_a, mix_b)], 0
    ).reshape(m, n, rc, d)
    full_out = reorder_rows(along.slot_of, out_rel, True).reshape(n * dl, d)
    wd = reorder(along.chunk_of, w_down.reshape(m, fc, d))

    middle = inputs + dot_nn(ob, full_out)
    normed_two, scaled_two, inverse_two = norm_forward(middle, gain_two)
    h2 = normed_two.astype(bf16)
    logits = dot_nt(h2, router)
    experts_range = jnp.arange(EXPERTS, dtype=jnp.int32)
    route_flags = (route_rows[:, :, None] == experts_range).astype(f32)
    chosen = jnp.sum(logits[:, None, :] * route_flags, -1)
    raised = jnp.exp(chosen - jnp.max(chosen, -1, keepdims=True))
    gate_vals = raised / jnp.sum(raised, -1, keepdims=True)
    slot_flags = (route_rows[:, :, None] == along.chunk_of // sub).astype(f32)
    gates = jnp.sum(gate_vals[:, :, None] * slot_flags, 1).T
    padded = max(m, 16)
    gates = jnp.concatenate([gates, jnp.zeros((padded - m, t), f32)], 0)

    z_slots = [dz] + [along.shift(dz, s) for s in range(1, n)]
    h_slots = [h2] + [along.shift(h2, s) for s in range(1, n)]
    gate_slots = [gates] + [along.shift(gates, s) for s in range(1, n)]
    done = [
        experts(h_slots[s], z_slots[s], gate_slots[s], wg, wu, wd, f32 if s == 0 else bf16)
        for s in range(n)
    ]
    mixed, h2_grad, slot_gate_grad = done[0][3], done[0][4], done[0][5]
    for s in range(1, n):
        h2_grad = h2_grad + along.shift(done[s][4], -s).astype(f32)
        slot_gate_grad = slot_gate_grad + along.shift(done[s][5], -s)
    for s in range(1, n):
        mixed = mixed + along.shift(done[s][3], -s).astype(f32)
    output = (middle + mixed).astype(bf16)[None]
    mix_grads = expert_grads(fc, *([x[k] for x in done] for k in range(3)), h_slots, z_slots)

    gate_grad = jnp.sum(slot_gate_grad[:m].T[:, None, :] * slot_flags, -1)
    weighted = gate_vals * gate_grad
    chosen_grad = weighted - gate_vals * jnp.sum(weighted, -1, keepdims=True)
    logit_grad = jnp.sum(chosen_grad[:, :, None] * route_flags, 1).astype(bf16)
    router_grad = dot_tn(logit_grad, h2)
    h2_grad = h2_grad + dot_nn(logit_grad, router)
    middle_norm_grad, gain_two_grad = norm_backward(h2_grad, gain_two, scaled_two, inverse_two)
    middle_grad = dz.astype(f32) + middle_norm_grad
    branch = middle_grad.astype(bf16)

    dob = dot_nt(branch, full_out).astype(bf16)
    out_grads = dot_tn(ob, branch).astype(bf16)
    out_grads = reorder_rows(along.chunk_of, out_grads.reshape(n, m, rc, d), False)
    dq, dkv = attend_back(seen, qkv, kv, dob, cos, sin)
    dkv_own = dkv[:, :t].astype(f32)
    for s in range(1, n):
        dkv_own = dkv_own + along.shift_down(dkv[:, s * t : (s + 1) * t], s).astype(f32)
    dk = dkv_own[0].reshape(t, KEY_VALUE_HEADS, HEAD_WIDTH)
    half = HEAD_WIDTH // 2
    dk = dk * cos[:, None] - jnp.concatenate([dk[..., half:], dk[..., :half]], -1) * sin[:, None]
    dqkv = jnp.concatenate([dq, dk.reshape(t, key_columns).astype(bf16), dkv_own[1].astype(bf16)], 1)
    h1_grad, qkv_grads = project_back(along.chunk_of, h1, dqkv, w_rel)
    input_norm_grad, gain_one_grad = norm_backward(h1_grad, gain_one, scaled_one, inverse_one)
    input_grad = (middle_grad + input_norm_grad).astype(bf16)[None]

    mix_grads = along.halve_core(mix_grads.reshape(m, 3 * fc, d))
    cut = 3 * fc // 2
    own_mix = jnp.concatenate(
        [along.halve(mix_grads[:, :cut], down_order), along.halve(mix_grads[:, cut:], up_order)], 0
    ).astype(bf16)
    down_half = fc // 2
    down_a = along.gather_dp(own_mix[2 * fc : 2 * fc + down_half], up_order)
    down_b = along.gather_dp(own_mix[2 * fc + down_half :], down_order)
    down_near = jnp.concatenate([down_a[0], down_b[0]], 1)
    down_far = jnp.concatenate([down_a[1], down_b[1]], 1)
    grad_w_down = spread(along.slot_of, down_near, down_far).reshape(EXPERTS, fs, d)
    back = jnp.transpose(own_mix[: 2 * fc].reshape(2 * fc, n, dl), (1, 0, 2))
    back = along.ranked(along.scatter_cp(back)).reshape(n, 2, fc, dl)
    back = jnp.transpose(back, (1, 3, 0, 2)).reshape(2, dl, n * fc)
    grads = []
    for k, order in ((0, up_order), (1, down_order)):
        near, far = along.gather_dp(back[k], order)
        g = spread(along.slot_of, near, far)
        if sub > 1:
            g = g.reshape(EXPERTS, sub, dl, n, fc)
            g = jnp.transpose(g, (0, 2, 3, 1, 4))
        grads.append(g.reshape(EXPERTS, dl, ff))
    grad_w_gate, grad_w_up = grads

    def sum_all(x):
        x = along.halve_core(x)
        cut = x.shape[1] // 2
        own = jnp.concatenate([along.halve(x[:, :cut], down_order), along.halve(x[:, cut:], up_order)], 0)
        return own.astype(bf16)

    own_out = along.scatter_cp(sum_all(out_grads.reshape(m, n * rc, d)).reshape(n, rc, d))
    own_out = functools.reduce(jnp.add, [x.astype(f32) for x in own_out]).astype(bf16)
    near, far = along.gather_dp(own_out, up_order)
    grad_w_out = spread(along.slot_of, near, far).reshape(dl, d)
    own_qkv = along.scatter_cp(sum_all(qkv_grads).reshape(n, dl, cw))
    own_qkv = functools.reduce(jnp.add, [x.astype(f32) for x in own_qkv]).astype(bf16)
    near, far = along.gather_dp(own_qkv, down_order)
    qkv_grad = jnp.transpose(spread(along.slot_of, near, far), (1, 0, 2)).reshape(dl, m * cw)
    grad_w_query = qkv_grad[:, :query_columns]
    grad_w_key = qkv_grad[:, query_columns : query_columns + key_columns]
    grad_w_value = qkv_grad[:, query_columns + key_columns :]

    small_grads = jnp.concatenate([gain_one_grad[None], gain_two_grad[None], router_grad], 0)
    small_grads = jnp.transpose(small_grads.reshape(2 + EXPERTS, n, dl), (1, 0, 2))
    small_grads = functools.reduce(jnp.add, along.scatter_cp(small_grads))
    for bit in range(along.bits):
        small_grads = small_grads + along.swap(small_grads, bit)
    return (
        output,
        input_grad,
        small_grads[0],
        grad_w_query,
        grad_w_key,
        grad_w_value,
        grad_w_out,
        small_grads[1],
        small_grads[2:].T,
        grad_w_gate,
        grad_w_up,
        grad_w_down,
    )


def solution(mesh):
    seq = P("dp", "cp", None)
    row, mid = P("cp", None), P(None, "cp", None)
    in_specs = (seq, seq, seq, P("cp"), row, row, row, row, P("cp"), row, mid, mid, mid)
    out_specs = (seq, seq, P("cp"), row, row, row, row, P("cp"), row, mid, mid, mid)
    return jax.shard_map(local, mesh=mesh, in_specs=in_specs, out_specs=out_specs, check_vma=False)
```

time: 2700 us -> 942 us (0.35)
  waiting for transfers between devices: 2070 us -> 371 us
  starting transfers between devices: 10.8 us -> 209 us
  matrix products: 185 us -> 7.96 us
  Pallas kernels: 0 us -> 159 us
  blocking collectives: 152 us -> 0 us
  local copies, waits for them, and re-layouts: 194 us -> 98.5 us
    all_gather x8 -> x0, waiting for transfers between devices: 1200 us -> none  [the longest x1 309 us: gather_mixture(): lax.all_gather(w_up, 'cp', axis=1, tiled=True)]
    all_to_all x2 -> x0, waiting for transfers between devices: 404 us -> none  [the longest x1 301 us: local(): lax.all_to_all(expert_in, 'cp', split_axis=2, concat_axis=1, tiled=True)]
    ppermute x0 -> x96, waiting for transfers between devices: none -> 371 us  [the longest x48 215 us: swap(): return lax.ppermute(x, 'dp', [(k, k ^ mask) for k in range(self.m)])]
    reduce_scatter x6 -> x0, waiting for transfers between devices: 247 us -> none  [the longest x1 88.5 us: local(): lax.psum_scatter(out_w_grad.astype(jnp.bfloat16), 'cp', scatter_dimension...]
    ppermute x0 -> x96, starting transfers between devices: none -> 209 us  [the longest x42 159 us: shift(): return lax.ppermute(x, 'cp', [(k, (k + s) % self.n) for k in range(self.n)])]
    psum x1 -> x0, waiting for transfers between devices: 195 us -> none  [local(): lax.psum(attn_sums[1].astype(jnp.bfloat16), 'dp').astype(jnp.float32)]
    dot_general x30 -> x6, matrix products: 179 us -> 7.96 us  [the longest x2 3.74 us: dot_nn(): lax.dot_general(a, b, (((1,), (0,)), ((), ())), preferred_element_type=f32)]
    pallas_call x0 -> x17, Pallas kernels: none -> 159 us  [the longest x4 62.3 us: experts(): pl.pallas_call(functools.partial(experts_kernel, fc), grid=(width // ct,)...]
  transfers between devices with their start and end apart: 18 -> 96, of which waited for: 17 -> 35; matrix products, arithmetic and copies ran while one was open for 10% -> 17% of each run, Pallas kernels for 0% -> 16%
where the time goes in v1:
time: 942 us; the launch traced here: 928 us
  waiting for transfers between devices  371 us (39%)
  starting transfers between devices  209 us (22%)
  Pallas kernels  159 us (17%)
  local copies, waits for them, and re-layouts  98.5 us (10%)
  other arithmetic  79.3 us (8%)
    ppermute x48, waiting for transfers between devices, swap(): return lax.ppermute(x, 'dp', [(k, k ^ mask) for k in range(self.m)])  215 us
    ppermute x42, starting transfers between devices, shift(): return lax.ppermute(x, 'cp', [(k, (k + s) % self.n) for k in range(self.n)])  159 us
    ppermute x42, waiting for transfers between devices, shift(): return lax.ppermute(x, 'cp', [(k, (k + s) % self.n) for k in range(self.n)])  132 us
    pallas_call x4, Pallas kernels, experts(): pl.pallas_call(functools.partial(experts_kernel, fc), grid=(width // ct,)...  62.3 us
    ppermute x48, starting transfers between devices, swap(): return lax.ppermute(x, 'dp', [(k, k ^ mask) for k in range(self.m)])  40.2 us
    unnamed x207, local copies, waits for them, and re-layouts  35.7 us
    pallas_call x5, Pallas kernels, spread(): pl.pallas_call(functools.partial(spread_kernel, half), grid_spec=pltpu.Pr...  27.4 us
    ppermute x3, waiting for transfers between devices, shift_down(): return lax.ppermute(x, 'cp', [(k + s, k) for k in range(self.n - s)])  24.6 us
  transfers between devices with their start and end apart: 96, of which 35 were waited for; matrix products, arithmetic and copies ran while one was open for 17% of the time, Pallas kernels for 16%

profile of v1, /device:TPU:0, one launch (start us, length us, event | category | flops | bytes accessed | tf_op | source)
XLA Modules:
  0.0 927.6 jit_solution(15184858512485904944)
XLA Ops:
  2.8 5.1 collective-permute-start
  19.9 5.9 collective-permute-done.18
  25.8 4.3 collective-permute-start.19
  30.1 3.9 collective-permute-done.19
  34.1 4.5 collective-permute-start.20
  38.6 4.4 collective-permute-done.20
  48.2 4.5 collective-permute-done.5
  52.7 5.6 collective-permute-start.17
  58.4 13.9 %collective-permute-done.16 = bf16[2,192,384]{2,1,0:T(8,128)(2,1)S(1)} collective-permute-done((bf16[2,192,384]{2,1,0:T(8,128)(2,1)S(1)}, bf16[2,192,384]{2,1,0:T(8,128)(2,1)S(1)}, u32[]{:S(2)}, u32[]{:S(2)}) %collective-permute-start.16) | collective-permute-done | bytes 294944 | tf_op jit(solution)/shard_map/ppermute | solution.py:430
  77.3 14.5 %collective-permute-done.23 = bf16[1,288,1536]{2,1,0:T(8,128)(2,1)S(1)} collective-permute-done((bf16[1,288,1536]{2,1,0:T(8,128)(2,1)S(1)}, bf16[1,288,1536]{2,1,0:T(8,128)(2,1)S(1)}, u32[]{:S(2)}, u32[]{:S(2)}) %collective-permute-start.23) | collective-permute-done | bytes 884768 | tf_op jit(solution)/shard_map/ppermute | solution.py:427
  96.2 8.4 collective-permute-done.9
  107.6 35.8 %collective-permute-done.6 = bf16[1,768,256]{2,1,0:T(8,128)(2,1)S(1)} collective-permute-done((bf16[1,768,256]{2,1,0:T(8,128)(2,1)S(1)}, bf16[1,768,256]{2,1,0:T(8,128)(2,1)S(1)}, u32[]{:S(2)}, u32[]{:S(2)}) %collective-permute-start.6) | collective-permute-done | bytes 393248 | tf_op jit(solution)/shard_map/ppermute | solution.py:427
  144.1 12.7 %collective-permute-done.10 = bf16[2,768,256]{2,1,0:T(8,128)(2,1)S(1)} collective-permute-done((bf16[2,768,256]{2,1,0:T(8,128)(2,1)S(1)}, bf16[2,768,256]{2,1,0:T(8,128)(2,1)S(1)}, u32[]{:S(2)}, u32[]{:S(2)}) %collective-permute-start.10) | collective-permute-done | bytes 786464 | tf_op jit(solution)/shard_map/ppermute | solution.py:427
  169.3 4.4 collective-permute-done.11
  176.4 10.4 %pad_maximum_fusion.w_ref = bf16[8,1536,256]{2,1,0:T(8,128)(2,1)S(1)} fusion(bf16[8,768,256]{2,1,0:T(8,128)(2,1)} %constant_dynamic-update-slice_fusion.7, bf16[4,768,256]{2,1,0:T(8,128)(2,1)} %collective-permute-done.8, bf16[2,768,256]{2,1,0:T(8,128)(2,1)S(1)} %copy-done.55, bf16[1,768,256]{2,1,0:T(8,128)(2,1)S(1)} %collective-permute-done.6, ...), kind=kLoop, calls=%fused_computation.3 | loop fusion | flops 31457280 | bytes 12582912 | tf_op jit(solution)/shard_map/concatenate | solution.py:531
  186.8 4.3 project.1.q_ref
  213.4 10.3 %attend.1 = bf16[256,1536]{1,0:T(8,128)(2,1)S(1)} custom-call(s32[1]{0:T(128)} %bitcast.1.seen_ref, bf16[256,2048]{1,0:T(8,128)(2,1)S(1)} %project.1.q_ref, bf16[1024,512]{1,0:T(8,128)(2,1)S(1)} %pad_maximum_fusion.18.k_ref.v_ref, bf16[1024,512]{1,0:T(8,128)(2,1)S(1)} %pad_maximum_fusion.18.k_ref.v_ref), custom_call_target="tpu_custom_call" | custom-call | flops 1610612736 | bytes 1572864 | tf_op jit(solution)/shard_map/attend/pallas_call | solution.py:132
  233.9 52.8 %collective-permute-start.31 = (bf16[256,1536]{1,0:T(8,128)(2,1)S(1)}, bf16[256,1536]{1,0:T(8,128)(2,1)}, u32[]{:S(2)}, u32[]{:S(2)}) collective-permute-start(bf16[256,1536]{1,0:T(8,128)(2,1)S(1)} %multiply_convert_fusion.h_ref.refs_12_), channel_id=1, source_target_pairs={{0,2},{1,3},{2,0},{3,1},{4,6},{5,7},{6,4},{7,5},{8,10},{9,11},{10,... | collective-permute-start | bytes 2359304 | tf_op jit(solution)/shard_map/ppermute | solution.py:430
  298.3 15.7 %experts.4 = (bf16[256,1536]{1,0:T(8,128)(2,1)S(1)}, bf16[256,1536]{1,0:T(8,128)(2,1)S(1)}, bf16[256,1536]{1,0:T(8,128)(2,1)S(1)}, f32[256,1536]{1,0:T(8,128)S(1...) custom-call(bf16[256,1536]{1,0:T(8,128)(2,1)S(1)} %multiply_convert_fusion.h_ref.refs_12_, ...), custom_call_target="tpu_custom_call" | custom-call | flops 7247757312 | bytes 14155776 | tf_op jit(solution)/shard_map/experts/pallas_call | solution.py:277
  317.8 36.4 %collective-permute-start.33 = (f32[16,256]{1,0:T(8,128)S(1)}, f32[16,256]{1,0:T(8,128)S(1)}, u32[]{:S(2)}, u32[]{:S(2)}) collective-permute-start(f32[16,256]{1,0:T(8,128)S(1)} %concatenate.170.gate_ref), channel_id=1, source_target_pairs={{0,2},{1,3},{2,0},{3,1},{4,6},{5,7},{6,4},{7,5},{8,10},{9,11},{10,... | collective-permute-start | bytes 49160 | tf_op jit(solution)/shard_map/ppermute | solution.py:430
  357.3 15.6 %experts.7 = (bf16[256,1536]{1,0:T(8,128)(2,1)S(1)}, bf16[256,1536]{1,0:T(8,128)(2,1)S(1)}, bf16[256,1536]{1,0:T(8,128)(2,1)S(1)}, bf16[256,1536]{1,0:T(8,128)(2...) custom-call(bf16[256,1536]{1,0:T(8,128)(2,1)S(1)} %copy-done.19, ...), custom_call_target="tpu_custom_call" | custom-call | flops 7247757312 | bytes 14155776 | tf_op jit(solution)/shard_map/experts/pallas_call | solution.py:277
  373.8 3.9 collective-permute-start.44
  377.7 15.9 %experts.6 = (bf16[256,1536]{1,0:T(8,128)(2,1)S(1)}, bf16[256,1536]{1,0:T(8,128)(2,1)S(1)}, bf16[256,1536]{1,0:T(8,128)(2,1)S(1)}, bf16[256,1536]{1,0:T(8,128)(2...) custom-call(bf16[256,1536]{1,0:T(8,128)(2,1)} %collective-permute-done.31.h_ref.refs_14_, ...), custom_call_target="tpu_custom_call" | custom-call | flops 7247757312 | bytes 14155776 | tf_op jit(solution)/shard_map/experts/pallas_call | solution.py:277
  398.0 15.1 %experts.5 = (bf16[256,1536]{1,0:T(8,128)(2,1)S(1)}, bf16[256,1536]{1,0:T(8,128)(2,1)S(1)}, bf16[256,1536]{1,0:T(8,128)(2,1)S(1)}, bf16[256,1536]{1,0:T(8,128)(2...) custom-call(bf16[256,1536]{1,0:T(8,128)(2,1)S(1)} %collective-permute-done.27.h_ref.refs_13_, ...), custom_call_target="tpu_custom_call" | custom-call | flops 7247757312 | bytes 14155776 | tf_op jit(solution)/shard_map/experts/pallas_call | solution.py:277
  421.6 21.3 %expert_grads.1 = bf16[8,3,192,1536]{3,2,1,0:T(8,128)(2,1)} custom-call(bf16[256,1536]{1,0:T(8,128)(2,1)} %copy-done.26, bf16[256,1536]{1,0:T(8,128)(2,1)} %copy-done.35, bf16[256,1536]{1,0:T(8,128)(2,1)} %copy-done.32, bf16[256,1536]{1,0:T(8,128)(2,1)} %copy-done.29, bf16[256,1536]{1,0:T(8,128)(2,1)} %copy-done.27, bf16[256,1536]{1,0:T(8,128)(2,1)} %copy-done.36, ...), custom_call_target="tpu_custom_call" | custom-call | flops 14495514624 | bytes 14155776 | tf_op jit(solution)/shard_map/expert_grads/pallas_call | solution.py:322
  443.0 11.4 %fusion.65 = (bf16[4,3,192,1536]{3,2,1,0:T(8,128)(2,1)}, bf16[4,3,192,1536]{3,2,1,0:T(8,128)(2,1)}) fusion(bf16[8,3,192,1536]{3,2,1,0:T(8,128)(2,1)} %expert_grads.1), kind=kLoop, calls=%fused_computation.240 | loop fusion | bytes 28311552 | tf_op jit(solution)/shard_map/slice | solution.py:454
  461.5 40.6 %collective-permute-done.40 = bf16[256,1536]{1,0:T(8,128)(2,1)} collective-permute-done((bf16[256,1536]{1,0:T(8,128)(2,1)}, bf16[256,1536]{1,0:T(8,128)(2,1)}, u32[]{:S(2)}, u32[]{:S(2)}) %collective-permute-start.40) | collective-permute-done | bytes 786464 | tf_op jit(solution)/shard_map/ppermute | solution.py:430
  506.7 32.5 %collective-permute-done.34 = bf16[256,1536]{1,0:T(8,128)(2,1)S(1)} collective-permute-done((bf16[256,1536]{1,0:T(8,128)(2,1)S(1)}, bf16[256,1536]{1,0:T(8,128)(2,1)S(1)}, u32[]{:S(2)}, u32[]{:S(2)}) %collective-permute-start.34) | collective-permute-done | bytes 786464 | tf_op jit(solution)/shard_map/ppermute | solution.py:430
  546.1 23.8 %attend_back.1 = (bf16[256,1536]{1,0:T(8,128)(2,1)}, bf16[2,1024,256]{2,1,0:T(8,128)(2,1)}) custom-call(s32[1]{0:T(128)} %bitcast.1.seen_ref, bf16[256,2048]{1,0:T(8,128)(2,1)} %copy-done.8, bf16[1024,512]{1,0:T(8,128)(2,1)} %copy-done.15, bf16[1024,512]{1,0:T(8,128)(2,1)} %copy-done.15, bf16[256,1536]{1,0:T(8,128)(2,1)} %convolution_convert_fusion.1.g_ref, ...), custom_call_target="tpu_custom_call" | custom-call | flops 4026531840 | bytes 3145728 | tf_op jit(solution)/shard_map/attend_back/pallas_call | solution.py:186
  579.3 14.2 %collective-permute-done.47 = bf16[2,256,256]{2,1,0:T(8,128)(2,1)S(1)} collective-permute-done((bf16[2,256,256]{2,1,0:T(8,128)(2,1)S(1)}, bf16[2,256,256]{2,1,0:T(8,128)(2,1)S(1)}, u32[]{:S(2)}, u32[]{:S(2)}) %collective-permute-start.47) | collective-permute-done | bytes 262176 | tf_op jit(solution)/shard_map/ppermute | solution.py:436
  593.5 10.4 %collective-permute-done.46 = bf16[2,256,256]{2,1,0:T(8,128)(2,1)S(1)} collective-permute-done((bf16[2,256,256]{2,1,0:T(8,128)(2,1)S(1)}, bf16[2,256,256]{2,1,0:T(8,128)(2,1)S(1)}, u32[]{:S(2)}, u32[]{:S(2)}) %collective-permute-start.46) | collective-permute-done | bytes 262176 | tf_op jit(solution)/shard_map/ppermute | solution.py:436
  609.0 5.9 project_back.1
  619.2 5.8 collective-permute-start.49
  629.2 14.2 %collective-permute-done.66 = bf16[2,96,1536]{2,1,0:T(8,128)(2,1)S(1)} collective-permute-done((bf16[2,96,1536]{2,1,0:T(8,128)(2,1)S(1)}, bf16[2,96,1536]{2,1,0:T(8,128)(2,1)S(1)}, u32[]{:S(2)}, u32[]{:S(2)}) %collective-permute-start.66) | collective-permute-done | bytes 589856 | tf_op jit(solution)/shard_map/ppermute | solution.py:427
  647.2 17.4 %collective-permute-done.51 = f32[10,384]{1,0:T(8,128)S(1)} collective-permute-done((f32[10,384]{1,0:T(8,128)S(1)}, f32[10,384]{1,0:T(8,128)S(1)}, u32[]{:S(2)}, u32[]{:S(2)}) %collective-permute-start.51) | collective-permute-done | bytes 15392 | tf_op jit(solution)/shard_map/ppermute | solution.py:427
  677.5 10.1 %fusion = bf16[4,576,1536]{2,1,0:T(8,128)(2,1)} fusion(bf16[4,576,1536]{2,1,0:T(8,128)(2,1)} %collective-permute-done.76, bf16[4,3,192,1536]{3,2,1,0:T(8,128)(2,1)} %get-tuple-element.102), kind=kLoop, calls=%fused_computation.1 | loop fusion | flops 14155776 | bytes 21233664 | tf_op jit(solution)/shard_map/convert_element_type | solution.py:454
  695.6 36.2 %collective-permute-done.77 = bf16[2,288,1536]{2,1,0:T(8,128)(2,1)S(1)} collective-permute-done((bf16[2,288,1536]{2,1,0:T(8,128)(2,1)S(1)}, bf16[2,288,1536]{2,1,0:T(8,128)(2,1)S(1)}, u32[]{:S(2)}, u32[]{:S(2)}) %collective-permute-start.77) | collective-permute-done | bytes 1769504 | tf_op jit(solution)/shard_map/ppermute | solution.py:427
  736.8 4.1 collective-permute-done.71
  743.1 19.3 %collective-permute-done.56 = bf16[1,768,256]{2,1,0:T(8,128)(2,1)S(1)} collective-permute-done((bf16[1,768,256]{2,1,0:T(8,128)(2,1)S(1)}, bf16[1,768,256]{2,1,0:T(8,128)(2,1)S(1)}, u32[]{:S(2)}, u32[]{:S(2)}) %collective-permute-start.56) | collective-permute-done | bytes 393248 | tf_op jit(solution)/shard_map/ppermute | solution.py:427
  766.6 9.4 %collective-permute-done.58 = bf16[1,768,256]{2,1,0:T(8,128)(2,1)S(1)} collective-permute-done((bf16[1,768,256]{2,1,0:T(8,128)(2,1)S(1)}, bf16[1,768,256]{2,1,0:T(8,128)(2,1)S(1)}, u32[]{:S(2)}, u32[]{:S(2)}) %collective-permute-start.58) | collective-permute-done | bytes 393248 | tf_op jit(solution)/shard_map/ppermute | solution.py:427
  784.2 5.6 collective-permute-done.60
  809.4 8.6 collective-permute-done.82
  830.2 8.0 collective-permute-done.84
  852.9 11.4 %collective-permute-done.93 = bf16[2,96,1536]{2,1,0:T(8,128)(2,1)S(1)} collective-permute-done((bf16[2,96,1536]{2,1,0:T(8,128)(2,1)S(1)}, bf16[2,96,1536]{2,1,0:T(8,128)(2,1)S(1)}, u32[]{:S(2)}, u32[]{:S(2)}) %collective-permute-start.93) | collective-permute-done | bytes 589856 | tf_op jit(solution)/shard_map/ppermute | solution.py:427
  867.4 9.5 %collective-permute-done.88 = bf16[2,384,768]{2,1,0:T(8,128)(2,1)S(1)} collective-permute-done((bf16[2,384,768]{2,1,0:T(8,128)(2,1)S(1)}, bf16[2,384,768]{2,1,0:T(8,128)(2,1)S(1)}, u32[]{:S(2)}, u32[]{:S(2)}) %collective-permute-start.88) | collective-permute-done | bytes 1179680 | tf_op jit(solution)/shard_map/ppermute | solution.py:427
  904.3 5.3 spread.9
  909.7 8.8 spread.7
  918.4 8.8 spread.8
  (537 shorter events, 274.0 us)
Async XLA Ops:
  7.9 88.2 %collective-permute-start.1 = (bf16[10,384]{1,0:T(8,128)(2,1)S(1)}, bf16[10,384]{1,0:T(8,128)(2,1)S(1)}, u32[]{:S(2)}, u32[]{:S(2)}) collective-permute-start(bf16[10,384]{1,0:T(8,128)(2,1)S(1)} %pad_maximum_fusion.35), channel_id=1, source_target_pairs={{0,2},{1,3},{2,0},{3,1},{4,6},{5,7},{6,4},{7,5},{8,10},{9,11},{10,... | collective-permute-start | bytes 23048 | tf_op jit(solution)/shard_map/ppermute | solution.py:430
  7.9 88.2 %collective-permute-start.2 = (bf16[10,384]{1,0:T(8,128)(2,1)S(1)}, bf16[10,384]{1,0:T(8,128)(2,1)S(1)}, u32[]{:S(2)}, u32[]{:S(2)}) collective-permute-start(bf16[10,384]{1,0:T(8,128)(2,1)S(1)} %pad_maximum_fusion.35), channel_id=1, source_target_pairs={{0,1},{1,2},{2,3},{3,0},{4,5},{5,6},{6,7},{7,4},{8,9},{9,10},{10,1... | collective-permute-start | bytes 23048 | tf_op jit(solution)/shard_map/ppermute | solution.py:430
  10.0 35.9 %collective-permute-start.3 = (bf16[384,256]{1,0:T(8,128)(2,1)S(1)}, bf16[384,256]{1,0:T(8,128)(2,1)S(1)}, u32[]{:S(2)}, u32[]{:S(2)}) collective-permute-start(bf16[384,256]{1,0:T(8,128)(2,1)S(1)} %fusion.41), channel_id=1, source_target_pairs={{0,3},{1,0},{2,1},{3,2},{4,7},{5,4},{6,5},{7,6},{8,11},{9,8},{10,9... | collective-permute-start | bytes 589832 | tf_op jit(solution)/shard_map/ppermute | solution.py:430
  12.8 35.1 %collective-permute-start.4 = (bf16[384,256]{1,0:T(8,128)(2,1)S(1)}, bf16[384,256]{1,0:T(8,128)(2,1)S(1)}, u32[]{:S(2)}, u32[]{:S(2)}) collective-permute-start(bf16[384,256]{1,0:T(8,128)(2,1)S(1)} %fusion.41), channel_id=1, source_target_pairs={{0,2},{1,3},{2,0},{3,1},{4,6},{5,7},{6,4},{7,5},{8,10},{9,11},{10,... | collective-permute-start | bytes 589832 | tf_op jit(solution)/shard_map/ppermute | solution.py:430
  75.8 29.0 %collective-permute-start.21 = (bf16[1,288,1536]{2,1,0:T(8,128)(2,1)S(1)}, bf16[1,288,1536]{2,1,0:T(8,128)(2,1)S(1)}, u32[]{:S(2)}, u32[]{:S(2)}) collective-permute-start(bf16[1,288,1536]{2,1,0:T(8,128)(2,1)S(1)} %maximum_bitcast_fusion), channel_id=1, source_target_pairs={{0,8},{4,12},{8,0},{12,4},{16,24},{20,28},{24,16},{28,20},{1,9},{5... | collective-permute-start | bytes 2654216 | tf_op jit(solution)/shard_map/ppermute | solution.py:427
  92.0 65.7 %collective-permute-start.24 = (bf16[2,288,1536]{2,1,0:T(8,128)(2,1)S(1)}, bf16[2,288,1536]{2,1,0:T(8,128)(2,1)S(1)}, u32[]{:S(2)}, u32[]{:S(2)}) collective-permute-start(bf16[2,288,1536]{2,1,0:T(8,128)(2,1)S(1)} %pad_maximum_fusion.9), channel_id=1, source_target_pairs={{0,8},{4,12},{8,0},{12,4},{16,24},{20,28},{24,16},{28,20},{1,9},{5... | collective-permute-start | bytes 5308424 | tf_op jit(solution)/shard_map/ppermute | solution.py:427
  96.1 47.3 %collective-permute-start.6 = (bf16[1,768,256]{2,1,0:T(8,128)(2,1)S(1)}, bf16[1,768,256]{2,1,0:T(8,128)(2,1)S(1)}, u32[]{:S(2)}, u32[]{:S(2)}) collective-permute-start(bf16[1,768,256]{2,1,0:T(8,128)(2,1)S(1)} %bitcast.233), channel_id=1, source_target_pairs={{0,8},{4,12},{8,0},{12,4},{16,24},{20,28},{24,16},{28,20},{1,9},{5... | collective-permute-start | bytes 1179656 | tf_op jit(solution)/shard_map/ppermute | solution.py:427
  104.7 52.0 %collective-permute-start.10 = (bf16[2,768,256]{2,1,0:T(8,128)(2,1)S(1)}, bf16[2,768,256]{2,1,0:T(8,128)(2,1)S(1)}, u32[]{:S(2)}, u32[]{:S(2)}) collective-permute-start(bf16[2,768,256]{2,1,0:T(8,128)(2,1)S(1)} %pad_maximum_fusion.21), channel_id=1, source_target_pairs={{0,8},{4,12},{8,0},{12,4},{16,24},{20,28},{24,16},{28,20},{1,9},{5... | collective-permute-start | bytes 2359304 | tf_op jit(solution)/shard_map/ppermute | solution.py:427
  105.0 54.9 %collective-permute-start.22 = (bf16[2,288,1536]{2,1,0:T(8,128)(2,1)S(1)}, bf16[2,288,1536]{2,1,0:T(8,128)(2,1)S(1)}, u32[]{:S(2)}, u32[]{:S(2)}) collective-permute-start(bf16[2,288,1536]{2,1,0:T(8,128)(2,1)S(1)} %pad_maximum_fusion.8), channel_id=1, source_target_pairs={{0,16},{4,20},{8,24},{12,28},{16,0},{20,4},{24,8},{28,12},{1,17},{... | collective-permute-start | bytes 5308424 | tf_op jit(solution)/shard_map/ppermute | solution.py:427
  159.8 63.9 %collective-permute-start.26 = (bf16[4,288,1536]{2,1,0:T(8,128)(2,1)}, bf16[4,288,1536]{2,1,0:T(8,128)(2,1)}, u32[]{:S(2)}, u32[]{:S(2)}) collective-permute-start(bf16[4,288,1536]{2,1,0:T(8,128)(2,1)} %pad_maximum_fusion.4), channel_id=1, source_target_pairs={{0,4},{4,0},{8,12},{12,8},{16,20},{20,16},{24,28},{28,24},{1,5},{5... | collective-permute-start | bytes 10616840 | tf_op jit(solution)/shard_map/ppermute | solution.py:427
  161.8 63.3 %collective-permute-start.25 = (bf16[4,288,1536]{2,1,0:T(8,128)(2,1)}, bf16[4,288,1536]{2,1,0:T(8,128)(2,1)}, u32[]{:S(2)}, u32[]{:S(2)}) collective-permute-start(bf16[4,288,1536]{2,1,0:T(8,128)(2,1)} %pad_maximum_fusion.3), channel_id=1, source_target_pairs={{0,4},{4,0},{8,12},{12,8},{16,20},{20,16},{24,28},{28,24},{1,5},{5... | collective-permute-start | bytes 10616840 | tf_op jit(solution)/shard_map/ppermute | solution.py:427
  211.3 105.4 %collective-permute-start.36 = (bf16[256,1536]{1,0:T(8,128)(2,1)}, bf16[256,1536]{1,0:T(8,128)(2,1)}, u32[]{:S(2)}, u32[]{:S(2)}) collective-permute-start(bf16[256,1536]{1,0:T(8,128)(2,1)} %bitcast.39.z_ref.refs_16_), channel_id=1, source_target_pairs={{0,3},{1,0},{2,1},{3,2},{4,7},{5,4},{6,5},{7,6},{8,11},{9,8},{10,9... | collective-permute-start | bytes 2359304 | tf_op jit(solution)/shard_map/ppermute | solution.py:430
  211.3 162.4 %collective-permute-start.32 = (bf16[256,1536]{1,0:T(8,128)(2,1)}, bf16[256,1536]{1,0:T(8,128)(2,1)}, u32[]{:S(2)}, u32[]{:S(2)}) collective-permute-start(bf16[256,1536]{1,0:T(8,128)(2,1)} %bitcast.39.z_ref.refs_16_), channel_id=1, source_target_pairs={{0,2},{1,3},{2,0},{3,1},{4,6},{5,7},{6,4},{7,5},{8,10},{9,11},{10,... | collective-permute-start | bytes 2359304 | tf_op jit(solution)/shard_map/ppermute | solution.py:430
  231.5 122.7 %collective-permute-start.35 = (bf16[256,1536]{1,0:T(8,128)(2,1)S(1)}, bf16[256,1536]{1,0:T(8,128)(2,1)S(1)}, u32[]{:S(2)}, u32[]{:S(2)}) collective-permute-start(bf16[256,1536]{1,0:T(8,128)(2,1)S(1)} %multiply_convert_fusion.h_ref.refs_12_), channel_id=1, source_target_pairs={{0,3},{1,0},{2,1},{3,2},{4,7},{5,4},{6,5},{7,6},{8,11},{9,8},{10,9... | collective-permute-start | bytes 2359304 | tf_op jit(solution)/shard_map/ppermute | solution.py:430
  233.9 143.7 %collective-permute-start.31 = (bf16[256,1536]{1,0:T(8,128)(2,1)S(1)}, bf16[256,1536]{1,0:T(8,128)(2,1)}, u32[]{:S(2)}, u32[]{:S(2)}) collective-permute-start(bf16[256,1536]{1,0:T(8,128)(2,1)S(1)} %multiply_convert_fusion.h_ref.refs_12_), channel_id=1, source_target_pairs={{0,2},{1,3},{2,0},{3,1},{4,6},{5,7},{6,4},{7,5},{8,10},{9,11},{10,... | collective-permute-start | bytes 2359304 | tf_op jit(solution)/shard_map/ppermute | solution.py:430
  287.2 30.6 %collective-permute-start.37 = (f32[16,256]{1,0:T(8,128)S(1)}, f32[16,256]{1,0:T(8,128)S(1)}, u32[]{:S(2)}, u32[]{:S(2)}) collective-permute-start(f32[16,256]{1,0:T(8,128)S(1)} %concatenate.170.gate_ref), channel_id=1, source_target_pairs={{0,3},{1,0},{2,1},{3,2},{4,7},{5,4},{6,5},{7,6},{8,11},{9,8},{10,9... | collective-permute-start | bytes 49160 | tf_op jit(solution)/shard_map/ppermute | solution.py:430
  316.7 81.2 %collective-permute-start.28 = (bf16[256,1536]{1,0:T(8,128)(2,1)}, bf16[256,1536]{1,0:T(8,128)(2,1)S(1)}, u32[]{:S(2)}, u32[]{:S(2)}) collective-permute-start(bf16[256,1536]{1,0:T(8,128)(2,1)} %bitcast.39.z_ref.refs_16_), channel_id=1, source_target_pairs={{0,1},{1,2},{2,3},{3,0},{4,5},{5,6},{6,7},{7,4},{8,9},{9,10},{10,1... | collective-permute-start | bytes 2359304 | tf_op jit(solution)/shard_map/ppermute | solution.py:430
  317.8 56.0 %collective-permute-start.33 = (f32[16,256]{1,0:T(8,128)S(1)}, f32[16,256]{1,0:T(8,128)S(1)}, u32[]{:S(2)}, u32[]{:S(2)}) collective-permute-start(f32[16,256]{1,0:T(8,128)S(1)} %concatenate.170.gate_ref), channel_id=1, source_target_pairs={{0,2},{1,3},{2,0},{3,1},{4,6},{5,7},{6,4},{7,5},{8,10},{9,11},{10,... | collective-permute-start | bytes 49160 | tf_op jit(solution)/shard_map/ppermute | solution.py:430
  355.1 42.9 %collective-permute-start.27 = (bf16[256,1536]{1,0:T(8,128)(2,1)S(1)}, bf16[256,1536]{1,0:T(8,128)(2,1)S(1)}, u32[]{:S(2)}, u32[]{:S(2)}) collective-permute-start(bf16[256,1536]{1,0:T(8,128)(2,1)S(1)} %multiply_convert_fusion.h_ref.refs_12_), channel_id=1, source_target_pairs={{0,1},{1,2},{2,3},{3,0},{4,5},{5,6},{6,7},{7,4},{8,9},{9,10},{10,1... | collective-permute-start | bytes 2359304 | tf_op jit(solution)/shard_map/ppermute | solution.py:430
  373.8 80.6 %collective-permute-start.44 = (f32[16,256]{1,0:T(8,128)S(1)}, f32[16,256]{1,0:T(8,128)S(1)}, u32[]{:S(2)}, u32[]{:S(2)}) collective-permute-start(f32[16,256]{1,0:T(8,128)S(1)} %get-tuple-element.51), channel_id=1, source_target_pairs={{0,1},{1,2},{2,3},{3,0},{4,5},{5,6},{6,7},{7,4},{8,9},{9,10},{10,1... | collective-permute-start | bytes 49160 | tf_op jit(solution)/shard_map/ppermute | solution.py:430
  397.1 59.1 %collective-permute-start.43 = (f32[16,256]{1,0:T(8,128)S(1)}, f32[16,256]{1,0:T(8,128)S(1)}, u32[]{:S(2)}, u32[]{:S(2)}) collective-permute-start(f32[16,256]{1,0:T(8,128)S(1)} %get-tuple-element.50), channel_id=1, source_target_pairs={{0,2},{1,3},{2,0},{3,1},{4,6},{5,7},{6,4},{7,5},{8,10},{9,11},{10,... | collective-permute-start | bytes 49160 | tf_op jit(solution)/shard_map/ppermute | solution.py:430
  417.5 39.2 %collective-permute-start.42 = (f32[16,256]{1,0:T(8,128)S(1)}, f32[16,256]{1,0:T(8,128)S(1)}, u32[]{:S(2)}, u32[]{:S(2)}) collective-permute-start(f32[16,256]{1,0:T(8,128)S(1)} %get-tuple-element.49), channel_id=1, source_target_pairs={{0,3},{1,0},{2,1},{3,2},{4,7},{5,4},{6,5},{7,6},{8,11},{9,8},{10,9... | collective-permute-start | bytes 49160 | tf_op jit(solution)/shard_map/ppermute | solution.py:430
  419.4 38.9 %collective-permute-start.41 = (bf16[256,1536]{1,0:T(8,128)(2,1)}, bf16[256,1536]{1,0:T(8,128)(2,1)S(1)}, u32[]{:S(2)}, u32[]{:S(2)}) collective-permute-start(bf16[256,1536]{1,0:T(8,128)(2,1)} %get-tuple-element.47), channel_id=1, source_target_pairs={{0,1},{1,2},{2,3},{3,0},{4,5},{5,6},{6,7},{7,4},{8,9},{9,10},{10,1... | collective-permute-start | bytes 2359304 | tf_op jit(solution)/shard_map/ppermute | solution.py:430
  419.6 82.5 %collective-permute-start.40 = (bf16[256,1536]{1,0:T(8,128)(2,1)}, bf16[256,1536]{1,0:T(8,128)(2,1)}, u32[]{:S(2)}, u32[]{:S(2)}) collective-permute-start(bf16[256,1536]{1,0:T(8,128)(2,1)} %get-tuple-element.46), channel_id=1, source_target_pairs={{0,2},{1,3},{2,0},{3,1},{4,6},{5,7},{6,4},{7,5},{8,10},{9,11},{10,... | collective-permute-start | bytes 2359304 | tf_op jit(solution)/shard_map/ppermute | solution.py:430
  454.4 50.0 %collective-permute-start.39 = (bf16[256,1536]{1,0:T(8,128)(2,1)S(1)}, bf16[256,1536]{1,0:T(8,128)(2,1)S(1)}, u32[]{:S(2)}, u32[]{:S(2)}) collective-permute-start(bf16[256,1536]{1,0:T(8,128)(2,1)S(1)} %copy-done.23), channel_id=1, source_target_pairs={{0,3},{1,0},{2,1},{3,2},{4,7},{5,4},{6,5},{7,6},{8,11},{9,8},{10,9... | collective-permute-start | bytes 2359304 | tf_op jit(solution)/shard_map/ppermute | solution.py:430
  456.1 50.6 %collective-permute-start.38 = (bf16[256,1536]{1,0:T(8,128)(2,1)S(1)}, bf16[256,1536]{1,0:T(8,128)(2,1)S(1)}, u32[]{:S(2)}, u32[]{:S(2)}) collective-permute-start(bf16[256,1536]{1,0:T(8,128)(2,1)S(1)} %get-tuple-element.43), channel_id=1, source_target_pairs={{0,1},{1,2},{2,3},{3,0},{4,5},{5,6},{6,7},{7,4},{8,9},{9,10},{10,1... | collective-permute-start | bytes 2359304 | tf_op jit(solution)/shard_map/ppermute | solution.py:430
  456.8 82.5 %collective-permute-start.34 = (bf16[256,1536]{1,0:T(8,128)(2,1)S(1)}, bf16[256,1536]{1,0:T(8,128)(2,1)S(1)}, u32[]{:S(2)}, u32[]{:S(2)}) collective-permute-start(bf16[256,1536]{1,0:T(8,128)(2,1)S(1)} %copy-done.17), channel_id=1, source_target_pairs={{0,2},{1,3},{2,0},{3,1},{4,6},{5,7},{6,4},{7,5},{8,10},{9,11},{10,... | collective-permute-start | bytes 2359304 | tf_op jit(solution)/shard_map/ppermute | solution.py:430
  458.4 80.8 %collective-permute-start.30 = (bf16[256,1536]{1,0:T(8,128)(2,1)S(1)}, bf16[256,1536]{1,0:T(8,128)(2,1)S(1)}, u32[]{:S(2)}, u32[]{:S(2)}) collective-permute-start(bf16[256,1536]{1,0:T(8,128)(2,1)S(1)} %copy-done.21), channel_id=1, source_target_pairs={{0,3},{1,0},{2,1},{3,2},{4,7},{5,4},{6,5},{7,6},{8,11},{9,8},{10,9... | collective-permute-start | bytes 2359304 | tf_op jit(solution)/shard_map/ppermute | solution.py:430
  502.1 175.4 %collective-permute-start.76 = (bf16[4,576,1536]{2,1,0:T(8,128)(2,1)}, bf16[4,576,1536]{2,1,0:T(8,128)(2,1)}, u32[]{:S(2)}, u32[]{:S(2)}) collective-permute-start(bf16[4,576,1536]{2,1,0:T(8,128)(2,1)} %bitcast.77), channel_id=1, source_target_pairs={{0,4},{4,0},{8,12},{12,8},{16,20},{20,16},{24,28},{28,24},{1,5},{5... | collective-permute-start | bytes 21233672 | tf_op jit(solution)/shard_map/ppermute | solution.py:427
  572.3 31.5 %collective-permute-start.46 = (bf16[2,256,256]{2,1,0:T(8,128)(2,1)S(1)}, bf16[2,256,256]{2,1,0:T(8,128)(2,1)S(1)}, u32[]{:S(2)}, u32[]{:S(2)}) collective-permute-start(bf16[2,256,256]{2,1,0:T(8,128)(2,1)S(1)} %get-tuple-element.141), channel_id=1, source_target_pairs={{2,0},{3,1},{6,4},{7,5},{10,8},{11,9},{14,12},{15,13},{18,16},{19,... | collective-permute-start | bytes 786440 | tf_op jit(solution)/shard_map/ppermute | solution.py:436
  573.6 30.2 %collective-permute-start.45 = (bf16[2,256,256]{2,1,0:T(8,128)(2,1)S(1)}, bf16[2,256,256]{2,1,0:T(8,128)(2,1)S(1)}, u32[]{:S(2)}, u32[]{:S(2)}) collective-permute-start(bf16[2,256,256]{2,1,0:T(8,128)(2,1)S(1)} %get-tuple-element.139), channel_id=1, source_target_pairs={{1,0},{2,1},{3,2},{5,4},{6,5},{7,6},{9,8},{10,9},{11,10},{13,12},{... | collective-permute-start | bytes 786440 | tf_op jit(solution)/shard_map/ppermute | solution.py:436
  579.0 46.0 %collective-permute-start.65 = (bf16[4,192,1536]{2,1,0:T(8,128)(2,1)}, bf16[4,192,1536]{2,1,0:T(8,128)(2,1)}, u32[]{:S(2)}, u32[]{:S(2)}) collective-permute-start(bf16[4,192,1536]{2,1,0:T(8,128)(2,1)} %bitcast.65), channel_id=1, source_target_pairs={{0,4},{4,0},{8,12},{12,8},{16,20},{20,16},{24,28},{28,24},{1,5},{5... | collective-permute-start | bytes 7077896 | tf_op jit(solution)/shard_map/ppermute | solution.py:427
  618.5 52.1 %collective-permute-start.54 = (bf16[4,1536,256]{2,1,0:T(8,128)(2,1)}, bf16[4,1536,256]{2,1,0:T(8,128)(2,1)}, u32[]{:S(2)}, u32[]{:S(2)}) collective-permute-start(bf16[4,1536,256]{2,1,0:T(8,128)(2,1)} %slice.355), channel_id=1, source_target_pairs={{0,4},{4,0},{8,12},{12,8},{16,20},{20,16},{24,28},{28,24},{1,5},{5... | collective-permute-start | bytes 9437192 | tf_op jit(solution)/shard_map/ppermute | solution.py:427
  674.3 59.8 %collective-permute-start.55 = (bf16[2,768,256]{2,1,0:T(8,128)(2,1)}, bf16[2,768,256]{2,1,0:T(8,128)(2,1)}, u32[]{:S(2)}, u32[]{:S(2)}) collective-permute-start(bf16[2,768,256]{2,1,0:T(8,128)(2,1)} %stack.143), channel_id=1, source_target_pairs={{0,16},{4,20},{8,24},{12,28},{16,0},{20,4},{24,8},{28,12},{1,17},{... | collective-permute-start | bytes 2359304 | tf_op jit(solution)/shard_map/ppermute | solution.py:427
  676.0 66.6 %collective-permute-start.57 = (bf16[2,768,256]{2,1,0:T(8,128)(2,1)S(1)}, bf16[2,768,256]{2,1,0:T(8,128)(2,1)}, u32[]{:S(2)}, u32[]{:S(2)}) collective-permute-start(bf16[2,768,256]{2,1,0:T(8,128)(2,1)S(1)} %pad_maximum_fusion.22), channel_id=1, source_target_pairs={{0,8},{4,12},{8,0},{12,4},{16,24},{20,28},{24,16},{28,20},{1,9},{5... | collective-permute-start | bytes 2359304 | tf_op jit(solution)/shard_map/ppermute | solution.py:427
  689.4 42.4 %collective-permute-start.77 = (bf16[2,288,1536]{2,1,0:T(8,128)(2,1)S(1)}, bf16[2,288,1536]{2,1,0:T(8,128)(2,1)S(1)}, u32[]{:S(2)}, u32[]{:S(2)}) collective-permute-start(bf16[2,288,1536]{2,1,0:T(8,128)(2,1)S(1)} %stack.145), channel_id=1, source_target_pairs={{0,16},{4,20},{8,24},{12,28},{16,0},{20,4},{24,8},{28,12},{1,17},{... | collective-permute-start | bytes 5308424 | tf_op jit(solution)/shard_map/ppermute | solution.py:427
  693.3 71.9 %collective-permute-start.79 = (bf16[2,288,1536]{2,1,0:T(8,128)(2,1)S(1)}, bf16[2,288,1536]{2,1,0:T(8,128)(2,1)S(1)}, u32[]{:S(2)}, u32[]{:S(2)}) collective-permute-start(bf16[2,288,1536]{2,1,0:T(8,128)(2,1)S(1)} %pad_maximum_fusion.10), channel_id=1, source_target_pairs={{0,8},{4,12},{8,0},{12,4},{16,24},{20,28},{24,16},{28,20},{1,9},{5... | collective-permute-start | bytes 5308424 | tf_op jit(solution)/shard_map/ppermute | solution.py:427
  693.9 38.6 %collective-permute-start.72 = (bf16[48,1536]{1,0:T(8,128)(2,1)S(1)}, bf16[48,1536]{1,0:T(8,128)(2,1)S(1)}, u32[]{:S(2)}, u32[]{:S(2)}) collective-permute-start(bf16[48,1536]{1,0:T(8,128)(2,1)S(1)} %get-tuple-element.155), channel_id=1, source_target_pairs={{0,3},{1,0},{2,1},{3,2},{4,7},{5,4},{6,5},{7,6},{8,11},{9,8},{10,9... | collective-permute-start | bytes 442376 | tf_op jit(solution)/shard_map/ppermute | solution.py:430
  734.2 31.0 %collective-permute-start.78 = (bf16[1,288,1536]{2,1,0:T(8,128)(2,1)S(1)}, bf16[1,288,1536]{2,1,0:T(8,128)(2,1)S(1)}, u32[]{:S(2)}, u32[]{:S(2)}) collective-permute-start(bf16[1,288,1536]{2,1,0:T(8,128)(2,1)S(1)} %add_convert_fusion.4), channel_id=1, source_target_pairs={{0,8},{4,12},{8,0},{12,4},{16,24},{20,28},{24,16},{28,20},{1,9},{5... | collective-permute-start | bytes 2654216 | tf_op jit(solution)/shard_map/ppermute | solution.py:427
  740.9 142.7 %collective-permute-start.53 = (f32[10,384]{1,0:T(8,128)}, f32[10,384]{1,0:T(8,128)}, u32[]{:S(2)}, u32[]{:S(2)}) collective-permute-start(f32[10,384]{1,0:T(8,128)} %add.357), channel_id=1, source_target_pairs={{0,4},{4,0},{8,12},{12,8},{16,20},{20,16},{24,28},{28,24},{1,5},{5... | collective-permute-start | bytes 46088 | tf_op jit(solution)/shard_map/ppermute | solution.py:427
  742.5 37.3 %collective-permute-start.73 = (bf16[1,48,1536]{2,1,0:T(8,128)(2,1)S(1)}, bf16[1,48,1536]{2,1,0:T(8,128)(2,1)S(1)}, u32[]{:S(2)}, u32[]{:S(2)}) collective-permute-start(bf16[1,48,1536]{2,1,0:T(8,128)(2,1)S(1)} %fusion.43), channel_id=1, source_target_pairs={{0,8},{4,12},{8,0},{12,4},{16,24},{20,28},{24,16},{28,20},{1,9},{5... | collective-permute-start | bytes 442376 | tf_op jit(solution)/shard_map/ppermute | solution.py:427
  765.7 27.9 %collective-permute-start.80 = (bf16[1,288,1536]{2,1,0:T(8,128)(2,1)S(1)}, bf16[1,288,1536]{2,1,0:T(8,128)(2,1)S(1)}, u32[]{:S(2)}, u32[]{:S(2)}) collective-permute-start(bf16[1,288,1536]{2,1,0:T(8,128)(2,1)S(1)} %get-tuple-element.105), channel_id=1, source_target_pairs={{0,16},{4,20},{8,24},{12,28},{16,0},{20,4},{24,8},{28,12},{1,17},{... | collective-permute-start | bytes 2654216 | tf_op jit(solution)/shard_map/ppermute | solution.py:427
  782.9 41.5 %collective-permute-start.74 = (bf16[2,48,1536]{2,1,0:T(8,128)(2,1)}, bf16[2,48,1536]{2,1,0:T(8,128)(2,1)}, u32[]{:S(2)}, u32[]{:S(2)}) collective-permute-start(bf16[2,48,1536]{2,1,0:T(8,128)(2,1)} %pad_maximum_fusion.31), channel_id=1, source_target_pairs={{0,16},{4,20},{8,24},{12,28},{16,0},{20,4},{24,8},{28,12},{1,17},{... | collective-permute-start | bytes 884744 | tf_op jit(solution)/shard_map/ppermute | solution.py:427
  790.6 35.1 %collective-permute-start.62 = (bf16[1,384,256]{2,1,0:T(8,128)(2,1)}, bf16[1,384,256]{2,1,0:T(8,128)(2,1)}, u32[]{:S(2)}, u32[]{:S(2)}) collective-permute-start(bf16[1,384,256]{2,1,0:T(8,128)(2,1)} %fusion.42), channel_id=1, source_target_pairs={{0,16},{4,20},{8,24},{12,28},{16,0},{20,4},{24,8},{28,12},{1,17},{... | collective-permute-start | bytes 589832 | tf_op jit(solution)/shard_map/ppermute | solution.py:427
  846.5 30.4 %collective-permute-start.88 = (bf16[2,384,768]{2,1,0:T(8,128)(2,1)S(1)}, bf16[2,384,768]{2,1,0:T(8,128)(2,1)S(1)}, u32[]{:S(2)}, u32[]{:S(2)}) collective-permute-start(bf16[2,384,768]{2,1,0:T(8,128)(2,1)S(1)} %pad_maximum_fusion.15), channel_id=1, source_target_pairs={{0,8},{4,12},{8,0},{12,4},{16,24},{20,28},{24,16},{28,20},{1,9},{5... | collective-permute-start | bytes 3538952 | tf_op jit(solution)/shard_map/ppermute | solution.py:427
  852.8 31.2 %collective-permute-start.75 = (bf16[4,48,1536]{2,1,0:T(8,128)(2,1)S(1)}, bf16[4,48,1536]{2,1,0:T(8,128)(2,1)S(1)}, u32[]{:S(2)}, u32[]{:S(2)}) collective-permute-start(bf16[4,48,1536]{2,1,0:T(8,128)(2,1)S(1)} %pad_maximum_fusion.27.near_ref), channel_id=1, source_target_pairs={{0,4},{4,0},{8,12},{12,8},{16,20},{20,16},{24,28},{28,24},{1,5},{5... | collective-permute-start | bytes 1769480 | tf_op jit(solution)/shard_map/ppermute | solution.py:427
  876.9 32.8 %collective-permute-start.86 = (bf16[4,384,768]{2,1,0:T(8,128)(2,1)}, bf16[4,384,768]{2,1,0:T(8,128)(2,1)}, u32[]{:S(2)}, u32[]{:S(2)}) collective-permute-start(bf16[4,384,768]{2,1,0:T(8,128)(2,1)} %pad_maximum_fusion.5.near_ref), channel_id=1, source_target_pairs={{0,4},{4,0},{8,12},{12,8},{16,20},{20,16},{24,28},{28,24},{1,5},{5... | collective-permute-start | bytes 7077896 | tf_op jit(solution)/shard_map/ppermute | solution.py:427
  880.1 38.3 %collective-permute-start.89 = (bf16[4,384,768]{2,1,0:T(8,128)(2,1)}, bf16[4,384,768]{2,1,0:T(8,128)(2,1)}, u32[]{:S(2)}, u32[]{:S(2)}) collective-permute-start(bf16[4,384,768]{2,1,0:T(8,128)(2,1)} %pad_maximum_fusion.6.near_ref), channel_id=1, source_target_pairs={{0,4},{4,0},{8,12},{12,8},{16,20},{20,16},{24,28},{28,24},{1,5},{5... | collective-permute-start | bytes 7077896 | tf_op jit(solution)/shard_map/ppermute | solution.py:427
  (132 other events, 2409.9 us)

commit v2 on v1

v2 whole, which is shorter than its diff:
```python
import functools
import math

import jax
import jax.numpy as jnp
from jax import lax
from jax.experimental import pallas as pl
from jax.experimental.pallas import tpu as pltpu
from jax.sharding import PartitionSpec as P

MODEL_WIDTH = 1536
QUERY_HEADS = 12
KEY_VALUE_HEADS = 2
HEAD_WIDTH = 128
EXPERTS = 8
TOPK = 4
BLK = 256

norm_eps = 1e-06
rope_base = 1000000.0
mask_fill = -1e30
score_scale = 1.0 / math.sqrt(HEAD_WIDTH)
query_columns = QUERY_HEADS * HEAD_WIDTH
key_columns = KEY_VALUE_HEADS * HEAD_WIDTH
group_heads = QUERY_HEADS // KEY_VALUE_HEADS

COST = 100000
EXTRA = 16
f32 = jnp.float32
bf16 = jnp.bfloat16


def dot_nn(a, b):
    return lax.dot_general(a, b, (((1,), (0,)), ((), ())), preferred_element_type=f32)


def dot_nt(a, b):
    return lax.dot_general(a, b, (((1,), (1,)), ((), ())), preferred_element_type=f32)


def dot_tn(a, b):
    return lax.dot_general(a, b, (((0,), (0,)), ((), ())), preferred_element_type=f32)


def params(megabytes):
    return pltpu.CompilerParams(vmem_limit_bytes=megabytes * 1024 * 1024)


def cost(flops, moved, raised=0):
    return pl.CostEstimate(flops=flops // COST, bytes_accessed=moved // COST, transcendentals=raised // COST)


def after(x, *deps):
    return lax.optimization_barrier((x, deps))[0]


def project_kernel(chunk_heads, half, slot_ref, h_ref, an_ref, af_ref, bn_ref, bf_ref, cos_ref, sin_ref, out_ref):
    j = pl.program_id(0)
    near = slot_ref[j] < half
    cut = an_ref.shape[1]

    def run(a_ref, b_ref):
        full = dot_nn(h_ref[:, :cut], a_ref[0]) + dot_nn(h_ref[:, cut:], b_ref[0])
        for k in range(chunk_heads):
            at = slice(k * HEAD_WIDTH, (k + 1) * HEAD_WIDTH)
            u = full[:, at]
            turned = u * cos_ref[...] + pltpu.roll(u, HEAD_WIDTH // 2, 1) * sin_ref[...]
            is_value = j * chunk_heads + k >= QUERY_HEADS + KEY_VALUE_HEADS
            out_ref[:, at] = jnp.where(is_value, u, turned).astype(bf16)

    pl.when(near)(lambda: run(an_ref, bn_ref))
    pl.when(jnp.logical_not(near))(lambda: run(af_ref, bf_ref))


def project(slot_of, h, w_a, w_b, cos, sin):
    half, cut, cw = w_a[0].shape
    t, d = h.shape
    m = 2 * half
    w_spec = pl.BlockSpec((1, cut, cw), lambda j, s: (s[j] % half, 0, 0))
    table = pl.BlockSpec((t, HEAD_WIDTH), lambda j, s: (0, 0))
    return pl.pallas_call(
        functools.partial(project_kernel, cw // HEAD_WIDTH, half),
        grid_spec=pltpu.PrefetchScalarGridSpec(
            num_scalar_prefetch=1,
            grid=(m,),
            in_specs=[pl.BlockSpec((t, d), lambda j, s: (0, 0))] + [w_spec] * 4 + [table] * 2,
            out_specs=pl.BlockSpec((t, cw), lambda j, s: (0, j)),
        ),
        out_shape=jax.ShapeDtypeStruct((t, m * cw), bf16),
        compiler_params=params(24),
        cost_estimate=cost(2 * t * d * m * cw, 2 * d * m * cw),
        name="project",
    )(slot_of, h, *w_a, *w_b, cos, sin)


def project_back_kernel(half, chunk_ref, h_ref, g_ref, an_ref, af_ref, bn_ref, bf_ref, dh_ref, gn_ref, gf_ref):
    j = pl.program_id(0)
    cut = an_ref.shape[1]

    @pl.when(j == 0)
    def _():
        dh_ref[...] = jnp.zeros_like(dh_ref)

    def run(a_ref, b_ref, gw_ref):
        dh_ref[:, :cut] += dot_nt(g_ref[...], a_ref[0])
        dh_ref[:, cut:] += dot_nt(g_ref[...], b_ref[0])
        gw_ref[0] = dot_tn(h_ref[...], g_ref[...]).astype(bf16)

    pl.when(j < half)(lambda: run(af_ref, bf_ref, gf_ref))
    pl.when(j >= half)(lambda: run(an_ref, bn_ref, gn_ref))


def project_back(chunk_of, h, grad, w_a, w_b):
    half, cut, cw = w_a[0].shape
    t, d = h.shape
    m = 2 * half
    first = lambda j, c: (jnp.minimum(j, half - 1), 0, 0)
    second = lambda j, c: (jnp.maximum(j - half, 0), 0, 0)
    near, far = pl.BlockSpec((1, cut, cw), second), pl.BlockSpec((1, cut, cw), first)
    return pl.pallas_call(
        functools.partial(project_back_kernel, half),
        grid_spec=pltpu.PrefetchScalarGridSpec(
            num_scalar_prefetch=1,
            grid=(m,),
            in_specs=[
                pl.BlockSpec((t, d), lambda j, c: (0, 0)),
                pl.BlockSpec((t, cw), lambda j, c: (0, c[(j + half) % m])),
                near,
                far,
                near,
                far,
            ],
            out_specs=[
                pl.BlockSpec((t, d), lambda j, c: (0, 0)),
                pl.BlockSpec((1, d, cw), second),
                pl.BlockSpec((1, d, cw), first),
            ],
        ),
        out_shape=[
            jax.ShapeDtypeStruct((t, d), f32),
            jax.ShapeDtypeStruct((half, d, cw), bf16),
            jax.ShapeDtypeStruct((half, d, cw), bf16),
        ],
        compiler_params=params(32),
        cost_estimate=cost(4 * t * d * m * cw, 4 * d * m * cw),
        name="project_back",
    )(chunk_of, h, grad, *w_a, *w_b)


def visible(rank, shape, dim):
    slot = lax.shift_right_logical(lax.broadcasted_iota(jnp.int32, shape, dim), BLK.bit_length() - 1)
    return (slot ^ rank) <= rank


def attend_kernel(rank_ref, q_ref, k_ref, v_ref, out_ref):
    s = dot_nt(q_ref[...], k_ref[...]) * score_scale
    s = jnp.where(visible(rank_ref[0], s.shape, 1), s, mask_fill)
    e = jnp.exp(s - jnp.max(s, 1, keepdims=True))
    p = (e / jnp.sum(e, 1, keepdims=True)).astype(bf16)
    out_ref[...] = dot_nn(p, v_ref[...]).astype(bf16)


def attend(rank, qkv, kv):
    t, rows = qkv.shape[0], kv.shape[0]
    return pl.pallas_call(
        attend_kernel,
        grid_spec=pltpu.PrefetchScalarGridSpec(
            num_scalar_prefetch=1,
            grid=(QUERY_HEADS,),
            in_specs=[
                pl.BlockSpec((t, HEAD_WIDTH), lambda j, s: (0, j)),
                pl.BlockSpec((rows, HEAD_WIDTH), lambda j, s: (0, j // group_heads)),
                pl.BlockSpec((rows, HEAD_WIDTH), lambda j, s: (0, KEY_VALUE_HEADS + j // group_heads)),
            ],
            out_specs=pl.BlockSpec((t, HEAD_WIDTH), lambda j, s: (0, j)),
        ),
        out_shape=jax.ShapeDtypeStruct((t, query_columns), bf16),
        compiler_params=params(40),
        cost_estimate=cost(4 * t * rows * query_columns, 4 * t * query_columns, t * rows * QUERY_HEADS),
        name="attend",
    )(rank, qkv, kv, kv)


def attend_back_kernel(rank_ref, q_ref, k_ref, v_ref, g_ref, cos_ref, sin_ref, dq_ref, dkv_ref, dk_acc, dv_acc):
    j = pl.program_id(0)
    q, k, g = q_ref[...], k_ref[...], g_ref[...]
    s = dot_nt(k, q) * score_scale
    s = jnp.where(visible(rank_ref[0], s.shape, 0), s, mask_fill)
    e = jnp.exp(s - jnp.max(s, 0, keepdims=True))
    p = e / jnp.sum(e, 0, keepdims=True)
    pb = p.astype(bf16)
    dp = dot_nt(v_ref[...], g)
    delta = jnp.sum(p * dp, 0, keepdims=True)
    ds = (p * (dp - delta)).astype(bf16)
    dq = dot_tn(ds, k) * score_scale
    dq_ref[...] = (dq * cos_ref[...] - pltpu.roll(dq, HEAD_WIDTH // 2, 1) * sin_ref[...]).astype(bf16)

    @pl.when(j % group_heads == 0)
    def _():
        dk_acc[...] = jnp.zeros_like(dk_acc)
        dv_acc[...] = jnp.zeros_like(dv_acc)

    dk_acc[...] += dot_nn(ds, q) * score_scale
    dv_acc[...] += dot_nn(pb, g)

    @pl.when(j % group_heads == group_heads - 1)
    def _():
        dkv_ref[0] = dk_acc[...].astype(bf16)
        dkv_ref[1] = dv_acc[...].astype(bf16)


def attend_back(rank, qkv, kv, grad, cos, sin):
    t, rows = qkv.shape[0], kv.shape[0]
    return pl.pallas_call(
        attend_back_kernel,
        grid_spec=pltpu.PrefetchScalarGridSpec(
            num_scalar_prefetch=1,
            grid=(QUERY_HEADS,),
            in_specs=[
                pl.BlockSpec((t, HEAD_WIDTH), lambda j, s: (0, j)),
                pl.BlockSpec((rows, HEAD_WIDTH), lambda j, s: (0, j // group_heads)),
                pl.BlockSpec((rows, HEAD_WIDTH), lambda j, s: (0, KEY_VALUE_HEADS + j // group_heads)),
                pl.BlockSpec((t, HEAD_WIDTH), lambda j, s: (0, j)),
                pl.BlockSpec((t, HEAD_WIDTH), lambda j, s: (0, 0)),
                pl.BlockSpec((t, HEAD_WIDTH), lambda j, s: (0, 0)),
            ],
            out_specs=[
                pl.BlockSpec((t, HEAD_WIDTH), lambda j, s: (0, j)),
                pl.BlockSpec((2, rows, HEAD_WIDTH), lambda j, s: (0, 0, j // group_heads)),
            ],
            scratch_shapes=[pltpu.VMEM((rows, HEAD_WIDTH), f32)] * 2,
        ),
        out_shape=[
            jax.ShapeDtypeStruct((t, query_columns), bf16),
            jax.ShapeDtypeStruct((2, rows, key_columns), bf16),
        ],
        compiler_params=params(56),
        cost_estimate=cost(10 * t * rows * query_columns, 8 * t * query_columns, t * rows * QUERY_HEADS),
        name="attend_back",
    )(rank, qkv, kv, kv, grad, cos, sin)


def experts_kernel(
    chunk_ref, h_ref, z_ref, gn_ref, gf_ref, un_ref, uf_ref, wd_ref,
    a_ref, dg_ref, du_ref, eo_ref, dh_ref, weights, eo_acc, dh_acc, dgate_acc, sems,
):
    per, fc, d = weights.shape[2:]
    ct = per * fc

    def copies(side):
        moves = [
            pltpu.make_async_copy((gn_ref, gf_ref)[side], weights.at[side, 0], sems.at[side, 0]),
            pltpu.make_async_copy((un_ref, uf_ref)[side], weights.at[side, 1], sems.at[side, 1]),
        ]
        for k in range(per):
            moves.append(
                pltpu.make_async_copy(
                    wd_ref.at[chunk_ref[side * per + k]], weights.at[side, 2, k], sems.at[side, 2 + k]
                )
            )
        return moves

    for side in range(2):
        for move in copies(side):
            move.start()
    t = z_ref.shape[0]
    gates_high = h_ref[t:, :t]
    gates_low = h_ref[t:, t : 2 * t]
    for side in range(2):
        moves = copies(side)
        slot_row = lax.broadcasted_iota(jnp.int32, (EXTRA, ct), 0)
        slot_col = lax.broadcasted_iota(jnp.int32, (EXTRA, ct), 1) + side * ct
        low = slot_row * fc
        pick = jnp.where((slot_col >= low) & (slot_col < low + fc), 1.0, 0.0).astype(bf16)
        wide = dot_tn(gates_high, pick) + dot_tn(gates_low, pick)
        moves[0].wait()
        wg = weights[side, 0].reshape(ct, d)
        g = dot_nt(h_ref[:t], wg)
        moves[1].wait()
        wu = weights[side, 1].reshape(ct, d)
        u = dot_nt(h_ref[:t], wu)
        for move in moves[2:]:
            move.wait()
        wd = weights[side, 2].reshape(ct, d)
        e = dot_nt(z_ref[...], wd)
        sig = 1.0 / (1.0 + jnp.exp(-g))
        swish = g * sig
        a = swish * u
        da = e * wide
        at = slice(side * ct, (side + 1) * ct)
        ab = (a * wide).astype(bf16)
        dg = (da * u * (sig * (1.0 + g * (1.0 - sig)))).astype(bf16)
        du = (da * swish).astype(bf16)
        a_ref[:, at] = ab
        dg_ref[:, at] = dg
        du_ref[:, at] = du
        dgate = dot_nt(pick, (a * e).astype(bf16))
        if side == 0:
            dgate_acc[...] = dgate
            dh_acc[...] = dot_nn(dg, wg)
            dh_acc[...] += dot_nn(du, wu)
            eo_acc[...] = dot_nn(ab, wd)
        else:
            dgate = dgate_acc[...] + dgate
            high = dgate.astype(dh_ref.dtype)
            dh_ref[t:] = jnp.zeros((EXTRA, d), dh_ref.dtype)
            dh_ref[t:, :t] = high
            dh_ref[t:, t : 2 * t] = (dgate - high.astype(f32)).astype(dh_ref.dtype)
            dh_acc[...] += dot_nn(dg, wg)
            dh_ref[:t] = (dh_acc[...] + dot_nn(du, wu)).astype(dh_ref.dtype)
            eo_ref[...] = (eo_acc[...] + dot_nn(ab, wd)).astype(eo_ref.dtype)


def experts(chunk_of, h, z, wg, wu, wd, sent_type):
    t, d = z.shape
    per, fc = wg[0].shape[0], wg[0].shape[1]
    width = 2 * per * fc
    vmem, hbm = pl.BlockSpec(memory_space=pltpu.VMEM), pl.BlockSpec(memory_space=pl.ANY)
    return pl.pallas_call(
        experts_kernel,
        in_specs=[pl.BlockSpec(memory_space=pltpu.SMEM)] + [vmem] * 2 + [hbm] * 5,
        out_specs=[vmem] * 5,
        out_shape=[
            jax.ShapeDtypeStruct((t, width), bf16),
            jax.ShapeDtypeStruct((t, width), bf16),
            jax.ShapeDtypeStruct((t, width), bf16),
            jax.ShapeDtypeStruct((t, d), sent_type),
            jax.ShapeDtypeStruct((t + EXTRA, d), sent_type),
        ],
        scratch_shapes=[
            pltpu.VMEM((2, 3, per, fc, d), bf16),
            pltpu.VMEM((t, d), f32),
            pltpu.VMEM((t, d), f32),
            pltpu.VMEM((EXTRA, t), f32),
            pltpu.SemaphoreType.DMA((2, 2 + per)),
        ],
        compiler_params=params(48),
        cost_estimate=cost(12 * t * d * width, 6 * d * width),
        name="experts",
    )(chunk_of, h, z, *wg, *wu, wd)


def expert_grads_kernel(n, fc, *refs):
    a, dg, du = refs[:n], refs[n : 2 * n], refs[2 * n : 3 * n]
    h, z, out_ref = refs[3 * n : 4 * n], refs[4 * n : 5 * n], refs[5 * n]
    per = out_ref.shape[0]
    for which, (left, right) in enumerate(((dg, h), (du, h), (a, z))):
        total = dot_tn(left[0][...], right[0][...])
        for s in range(1, n):
            total += dot_tn(left[s][...], right[s][...])
        out_ref[:, which] = total.astype(bf16).reshape(per, fc, total.shape[-1])


def expert_grads(side, fc, a, dg, du, h, z):
    n = len(a)
    t, width = a[0].shape
    width = width // 2
    d = h[0].shape[1]
    ct = min(width, 384)
    per = ct // fc
    steps = width // ct
    tile = pl.BlockSpec((t, ct), lambda j: (0, side * steps + j))
    rows = pl.BlockSpec((t, d), lambda j: (0, 0))
    if width % HEAD_WIDTH:
        a, dg, du = ([x[:, side * width : (side + 1) * width] for x in xs] for xs in (a, dg, du))
        tile = pl.BlockSpec((t, width), lambda j: (0, 0))
    return pl.pallas_call(
        functools.partial(expert_grads_kernel, n, fc),
        grid=(steps,),
        in_specs=[tile] * (3 * n) + [rows] * (2 * n),
        out_specs=pl.BlockSpec((per, 3, fc, d), lambda j: (j, 0, 0, 0)),
        out_shape=jax.ShapeDtypeStruct((width // fc, 3, fc, d), bf16),
        compiler_params=params(58),
        cost_estimate=cost(6 * n * t * d * width, 6 * d * width),
        name="expert_grads",
    )(*a, *dg, *du, *h, *z)


def join_kernel(half, slot_ref, *refs):
    out_ref = refs[-1]
    near = slot_ref[pl.program_id(0)] < half

    def run(side):
        at = 0
        for k in range(side, len(refs) - 1, 2):
            block = refs[k][0]
            rows = block.shape[0]
            if out_ref.ndim == 4:
                out_ref[at : at + rows, 0] = block.astype(out_ref.dtype)
            else:
                out_ref[0, at : at + rows] = block.astype(out_ref.dtype)
            at += rows

    pl.when(near)(lambda: run(0))
    pl.when(jnp.logical_not(near))(lambda: run(1))


def join(slot_of, parts, dtype, spread_out=False):
    half = parts[0][0].shape[0]
    m = 2 * half
    tail = parts[0][0].shape[2:]
    rows = sum(near.shape[1] for near, far in parts)
    zeros = (0,) * len(tail)
    specs, flat = [], []
    for pair in parts:
        for x in pair:
            specs.append(pl.BlockSpec((1,) + x.shape[1:], lambda j, s: (s[j] % half, 0) + zeros))
            flat.append(x)
    if spread_out:
        out_spec = pl.BlockSpec((rows, 1) + tail, lambda j, s: (0, j) + zeros)
        shape = (rows, m) + tail
    else:
        out_spec = pl.BlockSpec((1, rows) + tail, lambda j, s: (j, 0) + zeros)
        shape = (m, rows) + tail
    return pl.pallas_call(
        functools.partial(join_kernel, half),
        grid_spec=pltpu.PrefetchScalarGridSpec(
            num_scalar_prefetch=1, grid=(m,), in_specs=specs, out_specs=out_spec
        ),
        out_shape=jax.ShapeDtypeStruct(shape, dtype),
        compiler_params=params(24),
        cost_estimate=cost(0, 6 * math.prod(shape)),
        name="join",
    )(slot_of, *flat)


def split_kernel(half, chunk_ref, in_ref, near_ref, far_ref):
    j = pl.program_id(0)

    @pl.when(j < half)
    def _():
        far_ref[0] = in_ref[:, 0]

    @pl.when(j >= half)
    def _():
        near_ref[0] = in_ref[:, 0]


def split(chunk_of, x):
    n, m, c, d = x.shape
    half = m // 2
    return pl.pallas_call(
        functools.partial(split_kernel, half),
        grid_spec=pltpu.PrefetchScalarGridSpec(
            num_scalar_prefetch=1,
            grid=(m,),
            in_specs=[pl.BlockSpec((n, 1, c, d), lambda j, s: (0, s[(j + half) % m], 0, 0))],
            out_specs=[
                pl.BlockSpec((1, n, c, d), lambda j, s: (jnp.maximum(j - half, 0), 0, 0, 0)),
                pl.BlockSpec((1, n, c, d), lambda j, s: (jnp.minimum(j, half - 1), 0, 0, 0)),
            ],
        ),
        out_shape=[jax.ShapeDtypeStruct((half, n, c, d), x.dtype)] * 2,
        compiler_params=params(16),
        cost_estimate=cost(0, 4 * x.size),
        name="split",
    )(chunk_of, x)


def columns_kernel(half, counts, slot_ref, near_ref, far_ref, *out_refs):
    j = pl.program_id(0)
    near = slot_ref[j] < half
    at = 0
    for count, out_ref in zip(counts, out_refs):
        mine = (j >= at) & (j < at + count)

        @pl.when(mine & near)
        def _(out_ref=out_ref):
            out_ref[...] = near_ref[0].astype(f32)

        @pl.when(mine & jnp.logical_not(near))
        def _(out_ref=out_ref):
            out_ref[...] = far_ref[0].astype(f32)

        at += count


def columns(slot_of, near, far, widths):
    half, rows, cw = near.shape
    counts = [w // cw for w in widths]
    specs, at = [], 0
    for count in counts:
        specs.append(
            pl.BlockSpec((rows, cw), lambda j, s, at=at, top=count - 1: (0, jnp.clip(j - at, 0, top)))
        )
        at += count
    in_spec = pl.BlockSpec((1, rows, cw), lambda j, s: (s[j] % half, 0, 0))
    return pl.pallas_call(
        functools.partial(columns_kernel, half, counts),
        grid_spec=pltpu.PrefetchScalarGridSpec(
            num_scalar_prefetch=1, grid=(2 * half,), in_specs=[in_spec] * 2, out_specs=specs
        ),
        out_shape=[jax.ShapeDtypeStruct((rows, w), f32) for w in widths],
        compiler_params=params(16),
        cost_estimate=cost(0, 12 * near.size),
        name="columns",
    )(slot_of, near, far)


def arrange_kernel(n, fc, rc, rank_ref, *refs):
    slots, (gate_ref, up_ref, a_ref, b_ref) = refs[:n], refs[n:]
    dl = slots[0].shape[1]

    def run(rank):
        for q in range(n):
            block = slots[q ^ rank]
            gate_ref[:, q * dl : (q + 1) * dl] = block[:fc]
            up_ref[:, q * dl : (q + 1) * dl] = block[fc : 2 * fc]
            out_ref = (a_ref, b_ref)[q // (n // 2)]
            for b in range(n):
                at = 2 * fc + b * rc
                out_ref[q % (n // 2), :, b * dl : (b + 1) * dl] = block[at : at + rc]

    for rank in range(n):
        pl.when(rank_ref[0] == rank)(functools.partial(run, rank))


def arrange(rank, slots, fc, rc):
    n, d = len(slots), len(slots) * slots[0].shape[1]
    vmem = pl.BlockSpec(memory_space=pltpu.VMEM)
    return pl.pallas_call(
        functools.partial(arrange_kernel, n, fc, rc),
        in_specs=[pl.BlockSpec(memory_space=pltpu.SMEM)] + [vmem] * n,
        out_specs=[vmem] * 4,
        out_shape=[jax.ShapeDtypeStruct((fc, d), bf16)] * 2 + [jax.ShapeDtypeStruct((n // 2, rc, d), bf16)] * 2,
        compiler_params=params(16),
        cost_estimate=cost(0, 8 * fc * d),
        name="arrange",
    )(rank, *slots)


class Rounds:
    def __init__(self):
        self.gate, self.made, self.later = (), [], []

    def enter(self, x):
        return after(x, *self.gate) if self.gate else x

    def leave(self, *xs):
        self.made.extend(xs)
        return xs[0]

    def leave_late(self, *xs):
        self.later.extend(xs)
        return xs[0]

    def turn(self):
        self.gate, self.made, self.later = tuple(self.made), self.later, []


class Along:
    def __init__(self, rounds):
        self.rounds = rounds
        self.n, self.m = lax.axis_size("cp"), lax.axis_size("dp")
        self.r, self.i = lax.axis_index("cp"), lax.axis_index("dp")
        self.bits = self.m.bit_length() - 1
        assert 1 << self.bits == self.m and self.bits > 1
        self.inner = self.bits - 1
        slots = jnp.arange(self.m, dtype=jnp.int32)
        self.chunk_of = self.i ^ (((slots & (self.m // 2 - 1)) << 1) | (slots >> self.inner))
        offset = slots ^ self.i
        self.slot_of = (offset >> 1) | ((offset & 1) << self.inner)

    def send(self, x, axis, pairs, late=False):
        leave = self.rounds.leave_late if late else self.rounds.leave
        return leave(lax.ppermute(self.rounds.enter(x), axis, pairs))

    def swap(self, x, bit, late=False):
        mask = 1 if bit == self.inner else 2 << bit
        return self.send(x, "dp", [(k, k ^ mask) for k in range(self.m)], late)

    def cross(self, x, s, keep=None, late=False):
        pairs = [(k, k ^ s) for k in range(self.n)]
        return self.send(x, "cp", [p for p in pairs if keep is None or keep(*p)], late)

    def orders(self):
        up = list(range(self.inner))
        return up, up[::-1]

    def pieces(self, x, s):
        return lax.dynamic_index_in_dim(x, self.r ^ s, 0, keepdims=False)

    def scatter_cp(self, x):
        return [self.pieces(x, 0)] + [self.cross(self.pieces(x, s), s) for s in range(1, self.n)]

    def ranked(self, slots):
        for bit in range(self.n.bit_length() - 1):
            turned = (self.r >> bit & 1) == 1
            slots = [jnp.where(turned, slots[k ^ 1 << bit], slots[k]) for k in range(self.n)]
        return jnp.stack(slots)

    def gather_cp(self, x):
        return [x] + [self.cross(x, s) for s in range(1, self.n)]


class Gather:
    def __init__(self, along, *xs):
        self.along, self.parts, self.at = along, [{0: x} for x in xs], 0

    def step(self, late=False):
        for k, held in enumerate(self.parts):
            bit = self.along.orders()[k % 2][self.at]
            slots = sorted(held)
            got = self.along.swap(jnp.stack([held[h] for h in slots]), bit, late)
            for p, h in enumerate(slots):
                held[h | 1 << bit] = got[p]
        self.at += 1

    def rest(self, late=False):
        while self.at < self.along.inner:
            self.step(late)

    def finish(self, late=False):
        self.rest(late)
        near = [jnp.stack([held[h] for h in sorted(held)]) for held in self.parts]
        return [(x, self.along.swap(x, self.along.inner, late)) for x in near]


class Reduce:
    def __init__(self, along, far):
        self.along, self.at = along, 0
        self.got = along.swap(far, along.inner)

    def add(self, near):
        cut = near.shape[1] // 2
        self.parts = [
            {h: near[h, at].astype(f32) + self.got[h, at].astype(f32) for h in range(self.along.m // 2)}
            for at in (slice(0, cut), slice(cut, None))
        ]

    def step(self, late=False):
        for k, held in enumerate(self.parts):
            bit = self.along.orders()[1 - k][self.at]
            sent = jnp.stack([held[h].astype(bf16) for h in sorted(held) if h >> bit & 1])
            more = self.along.swap(sent, bit, late)
            kept = [h for h in sorted(held) if not h >> bit & 1]
            self.parts[k] = {h: held[h] + more[p].astype(f32) for p, h in enumerate(kept)}
        self.at += 1

    def rest(self, late=False):
        while self.at < self.along.inner:
            self.step(late)

    def finish(self):
        self.rest()
        return jnp.concatenate([p[0] for p in self.parts], 0).astype(bf16)


class Relay:
    inside, outside, turned = [(1, 2), (2, 1)], [(1, 0), (2, 3)], [(0, 1), (3, 2)]

    def __init__(self, along, x):
        self.along, self.x, self.four = along, x, along.n == 4

    def one(self):
        self.first = self.along.cross(self.x, 1)

    def middle(self):
        if self.four:
            self.third = self.along.send(self.x, "cp", self.inside)

    def two(self, late=False):
        self.second = self.along.cross(self.x, 2, late=late)

    def ends(self):
        along = self.along
        if self.four:
            outer = along.send(self.second, "cp", self.outside)
            self.third = [jnp.where((along.r == 1) | (along.r == 2), self.third, outer)]
        else:
            self.third = [along.cross(self.x, s) for s in range(3, along.n)]

    def slots(self):
        return [self.x, self.first, self.second, *self.third]


def norm_forward(values, gain_vec):
    inverse = lax.rsqrt(jnp.mean(values * values, -1, keepdims=True) + norm_eps)
    scaled = values * inverse
    return (scaled * gain_vec, scaled, inverse)


def norm_backward(gradient, gain_vec, scaled, inverse):
    gain_grad = jnp.sum(gradient * scaled, 0)
    inner_vals = gradient * gain_vec
    return (
        inverse * (inner_vals - scaled * jnp.mean(inner_vals * scaled, -1, keepdims=True)),
        gain_grad,
    )


def rotary(positions):
    half = HEAD_WIDTH // 2
    frequency = rope_base ** (-2.0 * jnp.arange(half, dtype=f32) / HEAD_WIDTH)
    angles = positions.astype(f32)[:, None] * frequency[None, :]
    cos, sin = jnp.cos(angles), jnp.sin(angles)
    return jnp.concatenate([cos, cos], 1), jnp.concatenate([-sin, sin], 1)


def local(
    tokens, routes, out_grad, norm_attn, w_query, key_weight, value_weight, w_out,
    norm_mix, w_router, w_gate, w_up, w_down,
):
    rounds = Rounds()
    along = Along(rounds)
    n, m, r, i = along.n, along.m, along.r, along.i
    t, d = tokens.shape[1], tokens.shape[2]
    assert t == BLK
    dl, ff, fs = w_query.shape[0], w_gate.shape[2], w_down.shape[1]
    sub = m // EXPERTS
    fc = fs // sub
    rc = dl // m
    inputs = tokens[0].astype(f32)
    route_rows = routes[0]
    dz = out_grad[0]
    up = lambda a, b: b > a
    down = lambda a, b: b < a

    w_qkv = jnp.concatenate([w_query, key_weight, value_weight], 1)
    cw = w_qkv.shape[1] // m
    small = jnp.concatenate([norm_attn[None], norm_mix[None], w_router.T], 0).reshape(-1)
    tail = -(-small.shape[0] // (16 * cw)) * 16
    small = jnp.concatenate([small, jnp.zeros((tail * cw - small.shape[0],), bf16)]).reshape(tail, cw)
    sent = jnp.concatenate([lax.dynamic_slice_in_dim(w_qkv, i * cw, cw, 1), small], 0)
    got = along.ranked(along.gather_cp(sent))
    own_qkv = got[:, :dl].reshape(d, cw)
    small = got[:, dl:].reshape(n, tail * cw)[:, : (2 + EXPERTS) * dl].reshape(n, 2 + EXPERTS, dl)
    small = jnp.swapaxes(small, 0, 1).reshape(2 + EXPERTS, d)
    gain_one, gain_two = small[0].astype(f32), small[1].astype(f32)
    router = small[2:]
    flipped = [
        lax.dynamic_index_in_dim(w, i // sub, 0, keepdims=False).T.reshape(n, sub, fc, dl)
        for w in (w_gate, w_up)
    ]
    flipped = lax.dynamic_index_in_dim(jnp.stack(flipped, 1), i % sub, 2, keepdims=False).reshape(n, 2 * fc, dl)
    out_rows = lax.dynamic_slice_in_dim(w_out, i * rc, rc, 0).reshape(rc, n, dl)
    out_rows = jnp.swapaxes(out_rows, 0, 1).reshape(1, n * rc, dl)
    flipped = jnp.concatenate([flipped, jnp.broadcast_to(out_rows, (n, n * rc, dl))], 1)
    flipped = rounds.leave(flipped)
    cos, sin = rotary(r * t + jnp.arange(t, dtype=jnp.int32))
    rounds.leave(cos, sin)

    rounds.turn()
    qkv_gather = Gather(along, own_qkv[: d // 2], own_qkv[d // 2 :])
    qkv_gather.step()
    mix = [along.pieces(flipped, 0), along.cross(along.pieces(flipped, 1), 1)]
    normed_one, scaled_one, inverse_one = norm_forward(inputs, gain_one)
    h1 = rounds.leave(normed_one.astype(bf16))
    rounds.turn()
    qkv_gather.rest()
    mix.append(along.cross(along.pieces(flipped, 2), 2))
    rounds.turn()
    qkv_a, qkv_b = qkv_gather.finish()
    mix.extend(along.cross(along.pieces(flipped, s), s, late=True) for s in range(3, n))
    rounds.turn()
    rank = r.reshape(1)
    qkv = rounds.leave(project(along.slot_of, rounds.enter(h1), qkv_a, qkv_b, cos, sin))
    rounds.turn()

    own_kv = qkv[:, query_columns:]
    kv = jnp.concatenate([own_kv] + [along.cross(own_kv, s, up) for s in range(1, n)], 0)
    if dl % HEAD_WIDTH == 0:
        gate_rows, up_rows, out_first, out_second = arrange(rank, [rounds.enter(x) for x in mix], fc, rc)
    else:
        got = along.ranked(mix)
        gate_rows, up_rows = jnp.swapaxes(got[:, : 2 * fc], 0, 1).reshape(2, fc, d)
        own_out = jnp.swapaxes(got[:, 2 * fc :].reshape(n, n, rc, dl), 1, 2).reshape(n, rc, d)
        out_first, out_second = own_out[: n // 2], own_out[n // 2 :]
    out_gather = Gather(along, out_first, out_second)
    out_gather.step()
    mix_gather = Gather(along, gate_rows, up_rows)
    mix_gather.step()
    rounds.turn()
    z_relay = Relay(along, dz)
    z_relay.two()
    out_gather.rest()
    mix_gather.rest()
    ob = rounds.leave(attend(rank, qkv, rounds.enter(kv)))
    rounds.turn()
    z_relay.one()
    z_relay.middle()
    out_a, out_b = out_gather.finish()
    wg, wu = mix_gather.finish()
    wd = w_down.reshape(m, fc, d)
    full_out = join(along.slot_of, [out_a, out_b], bf16, True).reshape(n * dl, d)

    middle = inputs + dot_nn(rounds.enter(ob), full_out)
    normed_two, scaled_two, inverse_two = norm_forward(middle, gain_two)
    h2 = normed_two.astype(bf16)
    logits = dot_nt(h2, router)
    experts_range = jnp.arange(EXPERTS, dtype=jnp.int32)
    route_flags = (route_rows[:, :, None] == experts_range).astype(f32)
    chosen = jnp.sum(logits[:, None, :] * route_flags, -1)
    raised = jnp.exp(chosen - jnp.max(chosen, -1, keepdims=True))
    gate_vals = raised / jnp.sum(raised, -1, keepdims=True)
    slot_flags = (route_rows[:, :, None] == along.chunk_of // sub).astype(f32)
    gates = jnp.sum(gate_vals[:, :, None] * slot_flags, 1).T
    gates = jnp.concatenate([gates, jnp.zeros((EXTRA - m, t), f32)], 0)
    gates_high = gates.astype(bf16)
    gates_low = (gates - gates_high.astype(f32)).astype(bf16)
    gates = jnp.concatenate([gates_high, gates_low, jnp.zeros((EXTRA, d - 2 * t), bf16)], 1)
    h_sent = rounds.leave(jnp.concatenate([h2, gates], 0))
    rounds.turn()

    h_relay = Relay(along, h_sent)
    h_relay.one()
    h_relay.middle()

    def run(h, z, sent_type=bf16):
        results = experts(along.chunk_of, rounds.enter(h), z, wg, wu, wd, sent_type)
        rounds.leave(*results)
        return results

    done = [run(h_sent, dz, f32)]
    rounds.turn()
    h_relay.two()
    z_relay.ends()
    done.append(run(h_relay.first, z_relay.first))
    rounds.turn()
    h_relay.ends()
    done.append(run(h_relay.second, z_relay.second))
    rounds.turn()
    h_slots, z_slots = h_relay.slots(), z_relay.slots()
    h2_back = done[0][4] + along.cross(done[1][4], 1).astype(f32)
    done.extend(run(h_slots[s], z_slots[s]) for s in range(3, n))
    rounds.turn()
    triples = [[rounds.enter(x[k]) for x in done] for k in range(3)]
    second = done[2][4]
    if n == 4:
        h2_back = h2_back + along.send(done[3][4], "cp", Relay.inside).astype(f32)
        second = (second.astype(f32) + along.send(done[3][4], "cp", Relay.turned).astype(f32)).astype(bf16)
    else:
        for s in range(3, n):
            h2_back = h2_back + along.cross(done[s][4], s).astype(f32)
    mix_far = rounds.leave(expert_grads(1, fc, *triples, h_slots, z_slots).reshape(m // 2, 3 * fc, d))
    rounds.turn()
    h2_back = h2_back + along.cross(second, 2).astype(f32)
    mix_reduce = Reduce(along, mix_far)
    triples = [[rounds.enter(x) for x in xs] for xs in triples]
    mix_near = rounds.leave(expert_grads(0, fc, *triples, h_slots, z_slots).reshape(m // 2, 3 * fc, d))
    rounds.turn()
    mix_reduce.add(mix_near)
    mix_reduce.step()

    mixed = done[0][3] + along.cross(done[1][3], 1).astype(f32)
    second_out = done[2][3]
    if n == 4:
        mixed = mixed + along.send(done[3][3], "cp", Relay.inside).astype(f32)
        second_out = second_out.astype(f32) + along.send(done[3][3], "cp", Relay.turned).astype(f32)
        second_out = second_out.astype(bf16)
    h2_back = rounds.enter(h2_back)
    slot_gate_grad = h2_back[t : t + m, :t] + h2_back[t : t + m, t : 2 * t]
    gate_grad = jnp.sum(slot_gate_grad.T[:, None, :] * slot_flags, -1)
    weighted = gate_vals * gate_grad
    chosen_grad = weighted - gate_vals * jnp.sum(weighted, -1, keepdims=True)
    logit_grad = jnp.sum(chosen_grad[:, :, None] * route_flags, 1).astype(bf16)
    router_grad = dot_tn(logit_grad, h2)
    h2_grad = h2_back[:t] + dot_nn(logit_grad, router)
    middle_norm_grad, gain_two_grad = norm_backward(h2_grad, gain_two, scaled_two, inverse_two)
    middle_grad = dz.astype(f32) + middle_norm_grad
    branch = middle_grad.astype(bf16)

    dob = dot_nt(branch, full_out).astype(bf16)
    out_grads = dot_tn(ob, branch).astype(bf16)
    out_near, out_far = split(along.chunk_of, out_grads.reshape(n, m, rc, d))
    dq, dkv = attend_back(rank, qkv, kv, dob, cos, sin)
    rounds.leave(dkv, out_near, out_far)
    rounds.turn()
    dkv_own = dkv[:, :t].astype(f32)
    for s in range(1, n):
        dkv_own = dkv_own + along.cross(dkv[:, s * t : (s + 1) * t], s, down).astype(f32)
    mix_reduce.rest()
    out_reduce = Reduce(along, out_far)
    rounds.turn()
    out_reduce.add(out_near)
    out_reduce.step()
    dkv_own = rounds.enter(dkv_own)
    dk = dkv_own[0].reshape(t, KEY_VALUE_HEADS, HEAD_WIDTH)
    half = HEAD_WIDTH // 2
    dk = dk * cos[:, None] - jnp.concatenate([dk[..., half:], dk[..., :half]], -1) * sin[:, None]
    dqkv = jnp.concatenate([dq, dk.reshape(t, key_columns).astype(bf16), dkv_own[1].astype(bf16)], 1)
    own_mix = mix_reduce.finish()
    back = [lax.dynamic_slice_in_dim(own_mix[: 2 * fc], (r ^ s) * dl, dl, 1) for s in range(n)]
    back = [back[0]] + [along.cross(back[s], s) for s in range(1, n)]
    own_down = own_mix[2 * fc :]
    down_gather = Gather(along, own_down[: fc // 2], own_down[fc // 2 :])
    down_gather.step()
    h1_grad, qkv_near, qkv_far = project_back(along.chunk_of, h1, dqkv, qkv_a, qkv_b)
    rounds.leave(h1_grad, qkv_near, qkv_far)
    rounds.turn()

    def sum_cp(x):
        return functools.reduce(jnp.add, [y.astype(f32) for y in along.scatter_cp(x)]).astype(bf16)

    qkv_reduce = Reduce(along, qkv_far)
    out_reduce.rest()
    down_gather.rest()
    input_norm_grad, gain_one_grad = norm_backward(h1_grad, gain_one, scaled_one, inverse_one)
    input_grad = (middle_grad + input_norm_grad).astype(bf16)[None]
    small_grads = jnp.concatenate([gain_one_grad[None], gain_two_grad[None], router_grad], 0)
    small_grads = rounds.leave(jnp.transpose(small_grads.reshape(2 + EXPERTS, n, dl), (1, 0, 2)))
    back = along.ranked(back).reshape(n, 2, fc, dl)
    back = rounds.leave(jnp.transpose(back, (1, 3, 0, 2)).reshape(2, dl, n * fc))
    rounds.turn()
    qkv_reduce.add(qkv_near)
    qkv_reduce.step()
    own_out = sum_cp(out_reduce.finish())
    small_grads = functools.reduce(jnp.add, along.scatter_cp(small_grads))
    rounds.turn()
    qkv_reduce.rest()
    back_gather = Gather(along, back[0], back[1])
    back_gather.step()
    out_gather = Gather(along, own_out)
    out_gather.step()
    small_grads = small_grads + along.swap(small_grads, along.inner)
    mixed = mixed + along.cross(second_out, 2).astype(f32)
    rounds.turn()
    back_gather.rest()
    out_gather.rest()
    own_qkv = sum_cp(qkv_reduce.finish().reshape(n, dl, cw))
    small_grads = small_grads + along.swap(small_grads, 0)
    if n != 4:
        for s in range(3, n):
            mixed = mixed + along.cross(done[s][3], s).astype(f32)
    rounds.turn()
    qkv_gather = Gather(along, own_qkv)
    qkv_gather.step()
    back_slots = back_gather.finish()
    (out_slots,) = out_gather.finish()
    down_a, down_b = down_gather.finish()
    for bit in range(1, along.inner):
        small_grads = small_grads + along.swap(small_grads, bit)
    output = (middle + mixed).astype(bf16)[None]
    rounds.turn()
    qkv_gather.rest()
    grad_w_down = join(along.slot_of, [down_a, down_b], f32)
    rounds.leave(grad_w_down)
    grad_w_down = grad_w_down.reshape(EXPERTS, fs, d)
    rounds.turn()
    (qkv_slots,) = qkv_gather.finish()
    grads = []
    for slots in back_slots:
        g = join(along.slot_of, [slots], f32)
        if sub > 1:
            g = g.reshape(EXPERTS, sub, dl, n, fc)
            g = jnp.transpose(g, (0, 2, 3, 1, 4))
        grads.append(g.reshape(EXPERTS, dl, ff))
    grad_w_gate, grad_w_up = grads
    grad_w_out = join(along.slot_of, [out_slots], f32).reshape(dl, d)
    grad_w_query, grad_w_key, grad_w_value = columns(
        along.slot_of, *qkv_slots, (query_columns, key_columns, key_columns)
    )
    return (
        output,
        input_grad,
        small_grads[0],
        grad_w_query,
        grad_w_key,
        grad_w_value,
        grad_w_out,
        small_grads[1],
        small_grads[2:].T,
        grad_w_gate,
        grad_w_up,
        grad_w_down,
    )


def solution(mesh):
    seq = P("dp", "cp", None)
    row, mid = P("cp", None), P(None, "cp", None)
    in_specs = (seq, seq, seq, P("cp"), row, row, row, row, P("cp"), row, mid, mid, mid)
    out_specs = (seq, seq, P("cp"), row, row, row, row, P("cp"), row, mid, mid, mid)
    return jax.shard_map(local, mesh=mesh, in_specs=in_specs, out_specs=out_specs, check_vma=False)
```

time: 942 us -> 675 us (0.72)
  waiting for transfers between devices: 371 us -> 235 us
  starting transfers between devices: 209 us -> 135 us
  local copies, waits for them, and re-layouts: 98.5 us -> 46.4 us
    ppermute x96 -> x94, waiting for transfers between devices: 371 us -> 235 us  [send(): return leave(lax.ppermute(self.rounds.enter(x), axis, pairs))]
    ppermute x96 -> x94, starting transfers between devices: 209 us -> 135 us  [send(): return leave(lax.ppermute(self.rounds.enter(x), axis, pairs))]
    concatenate x31 -> x6, other arithmetic: 42.7 us -> 2.66 us  [the longest x2 1.13 us: finish(): return jnp.concatenate([p[0] for p in self.parts], 0).astype(bf16)]
    slice x30 -> x10, local copies, waits for them, and re-layouts: 42.2 us -> 4.15 us  [the longest x5 2.77 us: step(): held[h | 1 << bit] = got[p]]
    another operation x4 -> x36, other arithmetic: 0.62 us -> 33.3 us  [the longest x13 14.6 us: finish(): near = [jnp.stack([held[h] for h in sorted(held)]) for held in self.parts]]
    convert_element_type x7 -> x10, other arithmetic: 17.6 us -> 19.3 us  [the longest x6 16.4 us: step(): held[h].astype(bf16)]
    unnamed x207 -> x247, local copies, waits for them, and re-layouts: 35.7 us -> 34.4 us
    pallas_call x15 -> x16, Pallas kernels: 125 us -> 126 us  [the longest x4 53.3 us: experts(): pl.pallas_call(experts_kernel, in_specs=[pl.BlockSpec(memory_space=pltpu....]
  transfers between devices with their start and end apart: 96 -> 94, of which waited for: 35 -> 37; matrix products, arithmetic and copies ran while one was open for 17% -> 14% of each run, Pallas kernels for 16% -> 23%
where the time goes in v2:
time: 675 us; the launch traced here: 664 us
  waiting for transfers between devices  235 us (35%)
  Pallas kernels  160 us (24%)
  starting transfers between devices  135 us (20%)
  other arithmetic  78.9 us (12%)
  local copies, waits for them, and re-layouts  46.4 us (7%)
    ppermute x94, waiting for transfers between devices, send(): return leave(lax.ppermute(self.rounds.enter(x), axis, pairs))  235 us
    ppermute x94, starting transfers between devices, send(): return leave(lax.ppermute(self.rounds.enter(x), axis, pairs))  135 us
    pallas_call x4, Pallas kernels, experts(): pl.pallas_call(experts_kernel, in_specs=[pl.BlockSpec(memory_space=pltpu....  53.3 us
    unnamed x247, local copies, waits for them, and re-layouts  34.4 us
    pallas_call x2, Pallas kernels, expert_grads(): pl.pallas_call(functools.partial(expert_grads_kernel, n, fc), grid=(steps...  26.8 us
    pallas_call x5, Pallas kernels, join(): pl.pallas_call(functools.partial(join_kernel, half), grid_spec=pltpu.Pref...  25.8 us
    pallas_call x1, Pallas kernels, attend_back(): pl.pallas_call(attend_back_kernel, grid_spec=pltpu.PrefetchScalarGridSpec...  23.8 us
    convert_element_type x6, other arithmetic, step(): held[h].astype(bf16)  16.4 us
  transfers between devices with their start and end apart: 94, of which 37 were waited for; matrix products, arithmetic and copies ran while one was open for 14% of the time, Pallas kernels for 23%

profile of v2, /device:TPU:0, one launch (start us, length us, event | category | flops | bytes accessed | tf_op | source)
XLA Modules:
  0.0 664.4 jit_solution(14570360691201282037)
XLA Ops:
  4.6 5.0 collective-permute-start
  17.4 10.0 %collective-permute-done.1 = bf16[400,256]{1,0:T(8,128)(2,1)} collective-permute-done((bf16[400,256]{1,0:T(8,128)(2,1)}, bf16[400,256]{1,0:T(8,128)(2,1)}, u32[]{:S(2)}, u32[]{:S(2)}) %collective-permute-start.1) | collective-permute-done | bytes 204832 | tf_op jit(solution)/shard_map/ppermute | solution.py:566
  32.4 6.8 %collective-permute-done.4 = bf16[1,768,256]{2,1,0:T(8,128)(2,1)} collective-permute-done((bf16[1,768,256]{2,1,0:T(8,128)(2,1)S(1)}, bf16[1,768,256]{2,1,0:T(8,128)(2,1)}, u32[]{:S(2)}, u32[]{:S(2)}) %collective-permute-start.4) | collective-permute-done | bytes 393248 | tf_op jit(solution)/shard_map/ppermute | solution.py:566
  45.3 14.8 %collective-permute-done.7 = bf16[2,768,256]{2,1,0:T(8,128)(2,1)S(1)} collective-permute-done((bf16[2,768,256]{2,1,0:T(8,128)(2,1)S(1)}, bf16[2,768,256]{2,1,0:T(8,128)(2,1)S(1)}, u32[]{:S(2)}, u32[]{:S(2)}) %collective-permute-start.7) | collective-permute-done | bytes 786464 | tf_op jit(solution)/shard_map/ppermute | solution.py:566
  69.4 4.5 project.1.q_ref
  74.0 4.6 collective-permute-done.11.refs_3_
  82.9 8.8 %collective-permute-start.12 = (bf16[256,512]{1,0:T(8,128)(2,1)S(1)}, bf16[256,512]{1,0:T(8,128)(2,1)S(1)}, u32[]{:S(2)}, u32[]{:S(2)}) collective-permute-start(bf16[256,512]{1,0:T(8,128)(2,1)S(1)} %slice.445), channel_id=1, source_target_pairs={{0,1},{2,3},{4,5},{6,7},{8,9},{10,11},{12,13},{14,15},{16,17},{18,... | collective-permute-start | bytes 786440 | tf_op jit(solution)/shard_map/ppermute | solution.py:566
  91.7 6.1 collective-permute-start.13
  99.3 4.8 collective-permute-done.13
  111.9 11.4 %collective-permute-start.19 = (bf16[256,1536]{1,0:T(8,128)(2,1)S(1)}, bf16[256,1536]{1,0:T(8,128)(2,1)S(1)}, u32[]{:S(2)}, u32[]{:S(2)}) collective-permute-start(bf16[256,1536]{1,0:T(8,128)(2,1)S(1)} %bitcast.163), channel_id=1, source_target_pairs={{0,2},{1,3},{2,0},{3,1},{4,6},{5,7},{6,4},{7,5},{8,10},{9,11},{10,... | collective-permute-start | bytes 2359304 | tf_op jit(solution)/shard_map/ppermute | solution.py:566
  123.3 10.3 %attend.1 = bf16[256,1536]{1,0:T(8,128)(2,1)S(1)} custom-call(s32[1]{0:T(128)} %bitcast.1.rank_ref, bf16[256,2048]{1,0:T(8,128)(2,1)S(1)} %project.1.q_ref, bf16[1024,512]{1,0:T(8,128)(2,1)S(1)} %pad_maximum_fusion.19.k_ref.v_ref, bf16[1024,512]{1,0:T(8,128)(2,1)S(1)} %pad_maximum_fusion.19.k_ref.v_ref), custom_call_target="tpu_custom_call" | custom-call | flops 16106 | bytes 15 | tf_op jit(solution)/shard_map/attend/pallas_call | solution.py:165
  134.9 10.7 %collective-permute-done.21 = bf16[2,2,48,1536]{3,2,1,0:T(8,128)(2,1)S(1)} collective-permute-done((bf16[2,2,48,1536]{3,2,1,0:T(8,128)(2,1)S(1)}, bf16[2,2,48,1536]{3,2,1,0:T(8,128)(2,1)S(1)}, u32[]{:S(2)}, u32[]{:S(2)}) %collective-permute-start.21) | collective-permute-done | bytes 589856 | tf_op jit(solution)/shard_map/ppermute | solution.py:566
  146.8 6.9 %collective-permute-done.19.z_ref.refs_18_ = bf16[256,1536]{1,0:T(8,128)(2,1)S(1)} collective-permute-done((bf16[256,1536]{1,0:T(8,128)(2,1)S(1)}, bf16[256,1536]{1,0:T(8,128)(2,1)S(1)}, u32[]{:S(2)}, u32[]{:S(2)}) %collective-permute-start.19) | collective-permute-done | bytes 786464 | tf_op jit(solution)/shard_map/ppermute | solution.py:566
  167.1 6.2 join.5
  177.0 4.0 collective-permute-start.30
  181.9 13.6 %experts.4 = (bf16[256,1536]{1,0:T(8,128)(2,1)S(1)}, bf16[256,1536]{1,0:T(8,128)(2,1)S(1)}, bf16[256,1536]{1,0:T(8,128)(2,1)S(1)}, f32[256,1536]{1,0:T(8,128)S(1)}, f32[272,1536]{1,0:T(8,128)}) custom-call(s32[8]{0:T(128)S(1)} %fusion.72.chunk_ref, bf16[272,1536]{1,0:T(8,128)(2,1)S(1)} %maximum_maximum_fusion.h_ref.refs_12_, ...), custom_call_target="tpu_custom_call" | custom-call | flops 72477 | bytes 141 | tf_op jit(solution)/shard_map/experts/pallas_call | solution.py:319
  199.4 4.5 collective-permute-start.32
  205.5 13.6 %experts.5 = (bf16[256,1536]{1,0:T(8,128)(2,1)S(1)}, bf16[256,1536]{1,0:T(8,128)(2,1)S(1)}, bf16[256,1536]{1,0:T(8,128)(2,1)S(1)}, bf16[256,1536]{1,0:T(8,128)(2,1)S(1)}, bf16[272,1536]{1,0:T(8,128)(2,1)S(1)}) custom-call(s32[8]{0:T(128)S(1)} %fusion.72.chunk_ref, bf16[272,1536]{1,0:T(8,128)(2,1)S(1)} %collective-permute-done.30.h_ref.refs_13_, ...), custom_call_target="tpu_custom_call" | custom-call | flops 72477 | bytes 141 | tf_op jit(solution)/shard_map/experts/pallas_call | solution.py:319
  223.7 15.8 %collective-permute-done.33 = bf16[256,1536]{1,0:T(8,128)(2,1)S(1)} collective-permute-done((bf16[256,1536]{1,0:T(8,128)(2,1)S(1)}, bf16[256,1536]{1,0:T(8,128)(2,1)S(1)}, u32[]{:S(2)}, u32[]{:S(2)}) %collective-permute-start.33) | collective-permute-done | bytes 786464 | tf_op jit(solution)/shard_map/ppermute | solution.py:566
  242.1 13.0 %experts.6 = (bf16[256,1536]{1,0:T(8,128)(2,1)S(1)}, bf16[256,1536]{1,0:T(8,128)(2,1)S(1)}, bf16[256,1536]{1,0:T(8,128)(2,1)S(1)}, bf16[256,1536]{1,0:T(8,128)(2,1)S(1)}, bf16[272,1536]{1,0:T(8,128)(2,1)S(1)}) custom-call(s32[8]{0:T(128)S(1)} %fusion.72.chunk_ref, bf16[272,1536]{1,0:T(8,128)(2,1)S(1)} %collective-permute-done.32.h_ref.refs_14_, ...), custom_call_target="tpu_custom_call" | custom-call | flops 72477 | bytes 141 | tf_op jit(solution)/shard_map/experts/pallas_call | solution.py:319
  262.2 13.2 %experts.7 = (bf16[256,1536]{1,0:T(8,128)(2,1)S(1)}, bf16[256,1536]{1,0:T(8,128)(2,1)S(1)}, bf16[256,1536]{1,0:T(8,128)(2,1)S(1)}, bf16[256,1536]{1,0:T(8,128)(2,1)S(1)}, bf16[272,1536]{1,0:T(8,128)(2,1)S(1)}) custom-call(s32[8]{0:T(128)S(1)} %fusion.72.chunk_ref, bf16[272,1536]{1,0:T(8,128)(2,1)S(1)} %broadcast_select_fusion.h_ref.refs_15_, ...), custom_call_target="tpu_custom_call" | custom-call | flops 72477 | bytes 141 | tf_op jit(solution)/shard_map/experts/pallas_call | solution.py:319
  284.0 13.2 %expert_grads.2 = bf16[4,3,192,1536]{3,2,1,0:T(8,128)(2,1)} custom-call(bf16[256,1536]{1,0:T(8,128)(2,1)} %copy-done.29, bf16[256,1536]{1,0:T(8,128)(2,1)} %copy-done.32, bf16[256,1536]{1,0:T(8,128)(2,1)} %copy-done.35, bf16[256,1536]{1,0:T(8,128)(2,1)} %copy-done.38, bf16[256,1536]{1,0:T(8,128)(2,1)} %copy-done.30, bf16[256,1536]{1,0:T(8,128)(2,1)} %copy-done.33, ...), custom_call_target="tpu_custom_call" | custom-call | flops 72477 | bytes 70 | tf_op jit(solution)/shard_map/expert_grads/pallas_call | solution.py:367
  298.6 4.1 collective-permute-start.38
  302.7 13.5 %expert_grads.3 = bf16[4,3,192,1536]{3,2,1,0:T(8,128)(2,1)} custom-call(bf16[256,1536]{1,0:T(8,128)(2,1)} %copy-done.29, bf16[256,1536]{1,0:T(8,128)(2,1)} %copy-done.32, bf16[256,1536]{1,0:T(8,128)(2,1)} %copy-done.35, bf16[256,1536]{1,0:T(8,128)(2,1)} %copy-done.38, bf16[256,1536]{1,0:T(8,128)(2,1)} %copy-done.30, bf16[256,1536]{1,0:T(8,128)(2,1)} %copy-done.33, ...), custom_call_target="tpu_custom_call" | custom-call | flops 72477 | bytes 70 | tf_op jit(solution)/shard_map/expert_grads/pallas_call | solution.py:367
  316.3 23.7 %collective-permute-done.38 = bf16[272,1536]{1,0:T(8,128)(2,1)} collective-permute-done((bf16[272,1536]{1,0:T(8,128)(2,1)S(1)}, bf16[272,1536]{1,0:T(8,128)(2,1)}, u32[]{:S(2)}, u32[]{:S(2)}) %collective-permute-start.38) | collective-permute-done | bytes 835616 | tf_op jit(solution)/shard_map/ppermute | solution.py:566
  347.2 4.1 add_convert_fusion.5
  359.8 23.8 %attend_back.1 = (bf16[256,1536]{1,0:T(8,128)(2,1)}, bf16[2,1024,256]{2,1,0:T(8,128)(2,1)}) custom-call(s32[1]{0:T(128)} %bitcast.1.rank_ref, bf16[256,2048]{1,0:T(8,128)(2,1)} %copy-done.10, bf16[1024,512]{1,0:T(8,128)(2,1)} %copy-done.2, bf16[1024,512]{1,0:T(8,128)(2,1)} %copy-done.2, bf16[256,1536]{1,0:T(8,128)(2,1)} %convolution_convert_fusion.1.g_ref, ...), custom_call_target="tpu_custom_call" | custom-call | flops 40265 | bytes 31 | tf_op jit(solution)/shard_map/attend_back/pallas_call | solution.py:214
  385.0 3.6 split.1
  395.4 4.5 add_convert_fusion.2
  403.6 10.6 %collective-permute-done.45 = bf16[2,256,256]{2,1,0:T(8,128)(2,1)S(1)} collective-permute-done((bf16[2,256,256]{2,1,0:T(8,128)(2,1)S(1)}, bf16[2,256,256]{2,1,0:T(8,128)(2,1)S(1)}, u32[]{:S(2)}, u32[]{:S(2)}) %collective-permute-start.45) | collective-permute-done | bytes 262176 | tf_op jit(solution)/shard_map/ppermute | solution.py:566
  415.5 10.0 %collective-permute-done.46 = bf16[2,256,256]{2,1,0:T(8,128)(2,1)S(1)} collective-permute-done((bf16[2,256,256]{2,1,0:T(8,128)(2,1)S(1)}, bf16[2,256,256]{2,1,0:T(8,128)(2,1)S(1)}, u32[]{:S(2)}, u32[]{:S(2)}) %collective-permute-start.46) | collective-permute-done | bytes 262176 | tf_op jit(solution)/shard_map/ppermute | solution.py:566
  427.5 4.1 add_convert_fusion
  434.2 6.0 collective-permute-start.54
  448.0 13.9 %collective-permute-done.54 = bf16[384,384]{1,0:T(8,128)(2,1)S(1)} collective-permute-done((bf16[384,384]{1,0:T(8,128)(2,1)}, bf16[384,384]{1,0:T(8,128)(2,1)S(1)}, u32[]{:S(2)}, u32[]{:S(2)}) %collective-permute-start.54) | collective-permute-done | bytes 294944 | tf_op jit(solution)/shard_map/ppermute | solution.py:566
  470.0 7.5 %project_back.1 = (f32[256,1536]{1,0:T(8,128)S(1)}, bf16[4,1536,256]{2,1,0:T(8,128)(2,1)S(1)}, bf16[4,1536,256]{2,1,0:T(8,128)(2,1)}) custom-call(s32[8]{0:T(128)S(1)} %fusion.72.chunk_ref, bf16[256,1536]{1,0:T(8,128)(2,1)S(1)} %copy-done.17, bf16[256,2048]{1,0:T(8,128)(2,1)S(1)} %copy-done.28, bf16[4,768,256]{2,1,0:T(8,128)(2,1)S(1)} %copy-done.4, ...), custom_call_target="tpu_custom_call" | custom-call | flops 32212 | bytes 125 | tf_op jit(solution)/shard_map/project_back/pallas_call | solution.py:120
  496.6 14.8 %collective-permute-done.60 = bf16[1,2,48,1536]{3,2,1,0:T(8,128)(2,1)S(1)} collective-permute-done((bf16[1,2,48,1536]{3,2,1,0:T(8,128)(2,1)S(1)}, bf16[1,2,48,1536]{3,2,1,0:T(8,128)(2,1)S(1)}, u32[]{:S(2)}, u32[]{:S(2)}) %collective-permute-start.60) | collective-permute-done | bytes 294944 | tf_op jit(solution)/shard_map/ppermute | solution.py:566
  516.2 4.3 collective-permute-start.68
  522.3 5.9 collective-permute-start.65
  530.0 4.1 collective-permute-done.66
  545.0 8.5 %collective-permute-done.76 = bf16[1,384,768]{2,1,0:T(8,128)(2,1)} collective-permute-done((bf16[1,384,768]{2,1,0:T(8,128)(2,1)}, bf16[1,384,768]{2,1,0:T(8,128)(2,1)}, u32[]{:S(2)}, u32[]{:S(2)}) %collective-permute-start.76) | collective-permute-done | bytes 589856 | tf_op jit(solution)/shard_map/ppermute | solution.py:566
  556.7 6.2 collective-permute-done.77
  562.9 13.0 %collective-permute-done.71 = bf16[256,1536]{1,0:T(8,128)(2,1)} collective-permute-done((bf16[256,1536]{1,0:T(8,128)(2,1)}, bf16[256,1536]{1,0:T(8,128)(2,1)}, u32[]{:S(2)}, u32[]{:S(2)}) %collective-permute-start.71) | collective-permute-done | bytes 786464 | tf_op jit(solution)/shard_map/ppermute | solution.py:566
  586.6 17.6 %collective-permute-done.80 = bf16[2,384,768]{2,1,0:T(8,128)(2,1)} collective-permute-done((bf16[2,384,768]{2,1,0:T(8,128)(2,1)}, bf16[2,384,768]{2,1,0:T(8,128)(2,1)}, u32[]{:S(2)}, u32[]{:S(2)}) %collective-permute-start.80) | collective-permute-done | bytes 1179680 | tf_op jit(solution)/shard_map/ppermute | solution.py:566
  609.4 4.3 collective-permute-done.82
  633.1 5.3 join.6
  649.4 5.3 join.9
  654.8 5.3 join.8
  660.1 4.1 columns.1
  (556 shorter events, 231.8 us)
Async XLA Ops:
  43.6 20.1 %collective-permute-start.6 = (bf16[2,768,256]{2,1,0:T(8,128)(2,1)S(1)}, bf16[2,768,256]{2,1,0:T(8,128)(2,1)S(1)}, u32[]{:S(2)}, u32[]{:S(2)}) collective-permute-start(bf16[2,768,256]{2,1,0:T(8,128)(2,1)S(1)} %pad_maximum_fusion.21), channel_id=1, source_target_pairs={{0,16},{4,20},{8,24},{12,28},{16,0},{20,4},{24,8},{28,12},{1,17},{... | collective-permute-start | bytes 2359304 | tf_op jit(solution)/shard_map/ppermute | solution.py:566
  44.2 19.6 %collective-permute-start.8 = (bf16[576,384]{1,0:T(8,128)(2,1)S(1)}, bf16[576,384]{1,0:T(8,128)(2,1)S(1)}, u32[]{:S(2)}, u32[]{:S(2)}) collective-permute-start(bf16[576,384]{1,0:T(8,128)(2,1)S(1)} %copy-done.111), channel_id=1, source_target_pairs={{0,2},{1,3},{2,0},{3,1},{4,6},{5,7},{6,4},{7,5},{8,10},{9,11},{10,... | collective-permute-start | bytes 1327112 | tf_op jit(solution)/shard_map/ppermute | solution.py:566
  81.8 25.0 %collective-permute-start.18 = (bf16[1,192,1536]{2,1,0:T(8,128)(2,1)S(1)}, bf16[1,192,1536]{2,1,0:T(8,128)(2,1)S(1)}, u32[]{:S(2)}, u32[]{:S(2)}) collective-permute-start(bf16[1,192,1536]{2,1,0:T(8,128)(2,1)S(1)} %bitcast.174), channel_id=1, source_target_pairs={{0,16},{4,20},{8,24},{12,28},{16,0},{20,4},{24,8},{28,12},{1,17},{... | collective-permute-start | bytes 1769480 | tf_op jit(solution)/shard_map/ppermute | solution.py:566
  82.3 24.5 %collective-permute-start.17 = (bf16[1,192,1536]{2,1,0:T(8,128)(2,1)S(1)}, bf16[1,192,1536]{2,1,0:T(8,128)(2,1)S(1)}, u32[]{:S(2)}, u32[]{:S(2)}) collective-permute-start(bf16[1,192,1536]{2,1,0:T(8,128)(2,1)S(1)} %bitcast.171), channel_id=1, source_target_pairs={{0,8},{4,12},{8,0},{12,4},{16,24},{20,28},{24,16},{28,20},{1,9},{5... | collective-permute-start | bytes 1769480 | tf_op jit(solution)/shard_map/ppermute | solution.py:566
  106.8 26.8 %collective-permute-start.20 = (bf16[2,2,48,1536]{3,2,1,0:T(8,128)(2,1)S(1)}, bf16[2,2,48,1536]{3,2,1,0:T(8,128)(2,1)S(1)}, u32[]{:S(2)}, u32[]{:S(2)}) collective-permute-start(bf16[2,2,48,1536]{3,2,1,0:T(8,128)(2,1)S(1)} %pad_maximum_fusion.27), channel_id=1, source_target_pairs={{0,16},{4,20},{8,24},{12,28},{16,0},{20,4},{24,8},{28,12},{1,17},{... | collective-permute-start | bytes 1769480 | tf_op jit(solution)/shard_map/ppermute | solution.py:566
  108.5 46.1 %collective-permute-start.23 = (bf16[2,192,1536]{2,1,0:T(8,128)(2,1)S(1)}, bf16[2,192,1536]{2,1,0:T(8,128)(2,1)S(1)}, u32[]{:S(2)}, u32[]{:S(2)}) collective-permute-start(bf16[2,192,1536]{2,1,0:T(8,128)(2,1)S(1)} %pad_maximum_fusion.11), channel_id=1, source_target_pairs={{0,8},{4,12},{8,0},{12,4},{16,24},{20,28},{24,16},{28,20},{1,9},{5... | collective-permute-start | bytes 3538952 | tf_op jit(solution)/shard_map/ppermute | solution.py:566
  110.1 35.6 %collective-permute-start.21 = (bf16[2,2,48,1536]{3,2,1,0:T(8,128)(2,1)S(1)}, bf16[2,2,48,1536]{3,2,1,0:T(8,128)(2,1)S(1)}, u32[]{:S(2)}, u32[]{:S(2)}) collective-permute-start(bf16[2,2,48,1536]{3,2,1,0:T(8,128)(2,1)S(1)} %pad_maximum_fusion.28), channel_id=1, source_target_pairs={{0,8},{4,12},{8,0},{12,4},{16,24},{20,28},{24,16},{28,20},{1,9},{5... | collective-permute-start | bytes 1769480 | tf_op jit(solution)/shard_map/ppermute | solution.py:566
  110.8 43.8 %collective-permute-start.22 = (bf16[2,192,1536]{2,1,0:T(8,128)(2,1)S(1)}, bf16[2,192,1536]{2,1,0:T(8,128)(2,1)S(1)}, u32[]{:S(2)}, u32[]{:S(2)}) collective-permute-start(bf16[2,192,1536]{2,1,0:T(8,128)(2,1)S(1)} %pad_maximum_fusion.10), channel_id=1, source_target_pairs={{0,16},{4,20},{8,24},{12,28},{16,0},{20,4},{24,8},{28,12},{1,17},{... | collective-permute-start | bytes 3538952 | tf_op jit(solution)/shard_map/ppermute | solution.py:566
  111.9 41.8 %collective-permute-start.19 = (bf16[256,1536]{1,0:T(8,128)(2,1)S(1)}, bf16[256,1536]{1,0:T(8,128)(2,1)S(1)}, u32[]{:S(2)}, u32[]{:S(2)}) collective-permute-start(bf16[256,1536]{1,0:T(8,128)(2,1)S(1)} %bitcast.163), channel_id=1, source_target_pairs={{0,2},{1,3},{2,0},{3,1},{4,6},{5,7},{6,4},{7,5},{8,10},{9,11},{10,... | collective-permute-start | bytes 2359304 | tf_op jit(solution)/shard_map/ppermute | solution.py:566
  156.0 20.9 %collective-permute-start.26 = (bf16[256,1536]{1,0:T(8,128)(2,1)S(1)}, bf16[256,1536]{1,0:T(8,128)(2,1)}, u32[]{:S(2)}, u32[]{:S(2)}) collective-permute-start(bf16[256,1536]{1,0:T(8,128)(2,1)S(1)} %bitcast.164), channel_id=1, source_target_pairs={{0,1},{1,0},{2,3},{3,2},{4,5},{5,4},{6,7},{7,6},{8,9},{9,8},{10,11... | collective-permute-start | bytes 2359304 | tf_op jit(solution)/shard_map/ppermute | solution.py:566
  177.0 22.4 %collective-permute-start.30 = (bf16[272,1536]{1,0:T(8,128)(2,1)S(1)}, bf16[272,1536]{1,0:T(8,128)(2,1)S(1)}, u32[]{:S(2)}, u32[]{:S(2)}) collective-permute-start(bf16[272,1536]{1,0:T(8,128)(2,1)S(1)} %maximum_maximum_fusion.h_ref.refs_12_), channel_id=1, source_target_pairs={{0,1},{1,0},{2,3},{3,2},{4,5},{5,4},{6,7},{7,6},{8,9},{9,8},{10,11... | collective-permute-start | bytes 2506760 | tf_op jit(solution)/shard_map/ppermute | solution.py:566
  181.0 18.4 %collective-permute-start.31 = (bf16[272,1536]{1,0:T(8,128)(2,1)S(1)}, bf16[272,1536]{1,0:T(8,128)(2,1)S(1)}, u32[]{:S(2)}, u32[]{:S(2)}) collective-permute-start(bf16[272,1536]{1,0:T(8,128)(2,1)S(1)} %maximum_maximum_fusion.h_ref.refs_12_), channel_id=1, source_target_pairs={{1,2},{2,1},{5,6},{6,5},{9,10},{10,9},{13,14},{14,13},{17,18},{18,... | collective-permute-start | bytes 2506760 | tf_op jit(solution)/shard_map/ppermute | solution.py:566
  199.4 40.1 %collective-permute-start.32 = (bf16[272,1536]{1,0:T(8,128)(2,1)S(1)}, bf16[272,1536]{1,0:T(8,128)(2,1)S(1)}, u32[]{:S(2)}, u32[]{:S(2)}) collective-permute-start(bf16[272,1536]{1,0:T(8,128)(2,1)S(1)} %maximum_maximum_fusion.h_ref.refs_12_), channel_id=1, source_target_pairs={{0,2},{1,3},{2,0},{3,1},{4,6},{5,7},{6,4},{7,5},{8,10},{9,11},{10,... | collective-permute-start | bytes 2506760 | tf_op jit(solution)/shard_map/ppermute | solution.py:566
  203.8 35.7 %collective-permute-start.33 = (bf16[256,1536]{1,0:T(8,128)(2,1)S(1)}, bf16[256,1536]{1,0:T(8,128)(2,1)S(1)}, u32[]{:S(2)}, u32[]{:S(2)}) collective-permute-start(bf16[256,1536]{1,0:T(8,128)(2,1)S(1)} %copy-done.14), channel_id=1, source_target_pairs={{1,0},{2,3},{5,4},{6,7},{9,8},{10,11},{13,12},{14,15},{17,16},{18,... | collective-permute-start | bytes 2359304 | tf_op jit(solution)/shard_map/ppermute | solution.py:566
  239.5 20.6 %collective-permute-start.34 = (bf16[272,1536]{1,0:T(8,128)(2,1)S(1)}, bf16[272,1536]{1,0:T(8,128)(2,1)}, u32[]{:S(2)}, u32[]{:S(2)}) collective-permute-start(bf16[272,1536]{1,0:T(8,128)(2,1)S(1)} %collective-permute-done.32.h_ref.refs_14_), channel_id=1, source_target_pairs={{1,0},{2,3},{5,4},{6,7},{9,8},{10,11},{13,12},{14,15},{17,16},{18,... | collective-permute-start | bytes 2506760 | tf_op jit(solution)/shard_map/ppermute | solution.py:566
  260.2 18.8 %collective-permute-start.35 = (bf16[272,1536]{1,0:T(8,128)(2,1)S(1)}, bf16[272,1536]{1,0:T(8,128)(2,1)S(1)}, u32[]{:S(2)}, u32[]{:S(2)}) collective-permute-start(bf16[272,1536]{1,0:T(8,128)(2,1)S(1)} %copy-done.54), channel_id=1, source_target_pairs={{0,1},{1,0},{2,3},{3,2},{4,5},{5,4},{6,7},{7,6},{8,9},{9,8},{10,11... | collective-permute-start | bytes 2506760 | tf_op jit(solution)/shard_map/ppermute | solution.py:566
  298.4 43.4 %collective-permute-start.39 = (bf16[4,576,1536]{2,1,0:T(8,128)(2,1)}, bf16[4,576,1536]{2,1,0:T(8,128)(2,1)}, u32[]{:S(2)}, u32[]{:S(2)}) collective-permute-start(bf16[4,576,1536]{2,1,0:T(8,128)(2,1)} %bitcast.188), channel_id=1, source_target_pairs={{0,4},{4,0},{8,12},{12,8},{16,20},{20,16},{24,28},{28,24},{1,5},{5... | collective-permute-start | bytes 21233672 | tf_op jit(solution)/shard_map/ppermute | solution.py:566
  298.6 41.4 %collective-permute-start.38 = (bf16[272,1536]{1,0:T(8,128)(2,1)S(1)}, bf16[272,1536]{1,0:T(8,128)(2,1)}, u32[]{:S(2)}, u32[]{:S(2)}) collective-permute-start(bf16[272,1536]{1,0:T(8,128)(2,1)S(1)} %add_convert_fusion.8), channel_id=1, source_target_pairs={{0,2},{1,3},{2,0},{3,1},{4,6},{5,7},{6,4},{7,5},{8,10},{9,11},{10,... | collective-permute-start | bytes 2506760 | tf_op jit(solution)/shard_map/ppermute | solution.py:566
  341.8 48.2 %collective-permute-start.41 = (bf16[256,1536]{1,0:T(8,128)(2,1)S(1)}, bf16[256,1536]{1,0:T(8,128)(2,1)}, u32[]{:S(2)}, u32[]{:S(2)}) collective-permute-start(bf16[256,1536]{1,0:T(8,128)(2,1)S(1)} %copy-done.58), channel_id=1, source_target_pairs={{1,2},{2,1},{5,6},{6,5},{9,10},{10,9},{13,14},{14,13},{17,18},{18,... | collective-permute-start | bytes 2359304 | tf_op jit(solution)/shard_map/ppermute | solution.py:566
  343.9 46.2 %collective-permute-start.42 = (bf16[256,1536]{1,0:T(8,128)(2,1)S(1)}, bf16[256,1536]{1,0:T(8,128)(2,1)}, u32[]{:S(2)}, u32[]{:S(2)}) collective-permute-start(bf16[256,1536]{1,0:T(8,128)(2,1)S(1)} %copy-done.58), channel_id=1, source_target_pairs={{0,1},{3,2},{4,5},{7,6},{8,9},{11,10},{12,13},{15,14},{16,17},{19,... | collective-permute-start | bytes 2359304 | tf_op jit(solution)/shard_map/ppermute | solution.py:566
  352.6 40.2 %collective-permute-start.44 = (bf16[2,288,1536]{2,1,0:T(8,128)(2,1)}, bf16[2,288,1536]{2,1,0:T(8,128)(2,1)}, u32[]{:S(2)}, u32[]{:S(2)}) collective-permute-start(bf16[2,288,1536]{2,1,0:T(8,128)(2,1)} %pad_maximum_fusion.6), channel_id=1, source_target_pairs={{0,8},{4,12},{8,0},{12,4},{16,24},{20,28},{24,16},{28,20},{1,9},{5... | collective-permute-start | bytes 5308424 | tf_op jit(solution)/shard_map/ppermute | solution.py:566
  355.5 39.9 %collective-permute-start.43 = (bf16[2,288,1536]{2,1,0:T(8,128)(2,1)}, bf16[2,288,1536]{2,1,0:T(8,128)(2,1)}, u32[]{:S(2)}, u32[]{:S(2)}) collective-permute-start(bf16[2,288,1536]{2,1,0:T(8,128)(2,1)} %pad_maximum_fusion.5), channel_id=1, source_target_pairs={{0,16},{4,20},{8,24},{12,28},{16,0},{20,4},{24,8},{28,12},{1,17},{... | collective-permute-start | bytes 5308424 | tf_op jit(solution)/shard_map/ppermute | solution.py:566
  356.9 33.2 %collective-permute-start.40 = (bf16[256,1536]{1,0:T(8,128)(2,1)S(1)}, bf16[256,1536]{1,0:T(8,128)(2,1)}, u32[]{:S(2)}, u32[]{:S(2)}) collective-permute-start(bf16[256,1536]{1,0:T(8,128)(2,1)S(1)} %copy-done.56), channel_id=1, source_target_pairs={{0,1},{1,0},{2,3},{3,2},{4,5},{5,4},{6,7},{7,6},{8,9},{9,8},{10,11... | collective-permute-start | bytes 2359304 | tf_op jit(solution)/shard_map/ppermute | solution.py:566
  395.4 38.2 %collective-permute-start.50 = (bf16[4,4,48,1536]{3,2,1,0:T(8,128)(2,1)}, bf16[4,4,48,1536]{3,2,1,0:T(8,128)(2,1)}, u32[]{:S(2)}, u32[]{:S(2)}) collective-permute-start(bf16[4,4,48,1536]{3,2,1,0:T(8,128)(2,1)} %get-tuple-element.269), channel_id=1, source_target_pairs={{0,4},{4,0},{8,12},{12,8},{16,20},{20,16},{24,28},{28,24},{1,5},{5... | collective-permute-start | bytes 7077896 | tf_op jit(solution)/shard_map/ppermute | solution.py:566
  399.9 27.6 %collective-permute-start.49 = (bf16[1,288,1536]{2,1,0:T(8,128)(2,1)}, bf16[1,288,1536]{2,1,0:T(8,128)(2,1)}, u32[]{:S(2)}, u32[]{:S(2)}) collective-permute-start(bf16[1,288,1536]{2,1,0:T(8,128)(2,1)} %get-tuple-element.268), channel_id=1, source_target_pairs={{0,16},{4,20},{8,24},{12,28},{16,0},{20,4},{24,8},{28,12},{1,17},{... | collective-permute-start | bytes 2654216 | tf_op jit(solution)/shard_map/ppermute | solution.py:566
  400.4 27.1 %collective-permute-start.48 = (bf16[1,288,1536]{2,1,0:T(8,128)(2,1)}, bf16[1,288,1536]{2,1,0:T(8,128)(2,1)}, u32[]{:S(2)}, u32[]{:S(2)}) collective-permute-start(bf16[1,288,1536]{2,1,0:T(8,128)(2,1)} %get-tuple-element.267), channel_id=1, source_target_pairs={{0,8},{4,12},{8,0},{12,4},{16,24},{20,28},{24,16},{28,20},{1,9},{5... | collective-permute-start | bytes 2654216 | tf_op jit(solution)/shard_map/ppermute | solution.py:566
  402.3 23.2 %collective-permute-start.46 = (bf16[2,256,256]{2,1,0:T(8,128)(2,1)S(1)}, bf16[2,256,256]{2,1,0:T(8,128)(2,1)S(1)}, u32[]{:S(2)}, u32[]{:S(2)}) collective-permute-start(bf16[2,256,256]{2,1,0:T(8,128)(2,1)S(1)} %get-tuple-element.265), channel_id=1, source_target_pairs={{2,0},{3,1},{6,4},{7,5},{10,8},{11,9},{14,12},{15,13},{18,16},{19,... | collective-permute-start | bytes 786440 | tf_op jit(solution)/shard_map/ppermute | solution.py:566
  434.2 27.7 %collective-permute-start.54 = (bf16[384,384]{1,0:T(8,128)(2,1)}, bf16[384,384]{1,0:T(8,128)(2,1)S(1)}, u32[]{:S(2)}, u32[]{:S(2)}) collective-permute-start(bf16[384,384]{1,0:T(8,128)(2,1)} %get-tuple-element.276), channel_id=1, source_target_pairs={{0,2},{1,3},{2,0},{3,1},{4,6},{5,7},{6,4},{7,5},{8,10},{9,11},{10,... | collective-permute-start | bytes 884744 | tf_op jit(solution)/shard_map/ppermute | solution.py:566
  440.2 40.1 %collective-permute-start.53 = (bf16[384,384]{1,0:T(8,128)(2,1)}, bf16[384,384]{1,0:T(8,128)(2,1)}, u32[]{:S(2)}, u32[]{:S(2)}) collective-permute-start(bf16[384,384]{1,0:T(8,128)(2,1)} %get-tuple-element.275), channel_id=1, source_target_pairs={{0,1},{1,0},{2,3},{3,2},{4,5},{5,4},{6,7},{7,6},{8,9},{9,8},{10,11... | collective-permute-start | bytes 884744 | tf_op jit(solution)/shard_map/ppermute | solution.py:566
  442.9 37.3 %collective-permute-start.52 = (bf16[2,2,48,1536]{3,2,1,0:T(8,128)(2,1)}, bf16[2,2,48,1536]{3,2,1,0:T(8,128)(2,1)}, u32[]{:S(2)}, u32[]{:S(2)}) collective-permute-start(bf16[2,2,48,1536]{3,2,1,0:T(8,128)(2,1)} %pad_maximum_fusion.30), channel_id=1, source_target_pairs={{0,8},{4,12},{8,0},{12,4},{16,24},{20,28},{24,16},{28,20},{1,9},{5... | collective-permute-start | bytes 1769480 | tf_op jit(solution)/shard_map/ppermute | solution.py:566
  445.3 35.0 %collective-permute-start.51 = (bf16[2,2,48,1536]{3,2,1,0:T(8,128)(2,1)}, bf16[2,2,48,1536]{3,2,1,0:T(8,128)(2,1)}, u32[]{:S(2)}, u32[]{:S(2)}) collective-permute-start(bf16[2,2,48,1536]{3,2,1,0:T(8,128)(2,1)} %pad_maximum_fusion.29), channel_id=1, source_target_pairs={{0,16},{4,20},{8,24},{12,28},{16,0},{20,4},{24,8},{28,12},{1,17},{... | collective-permute-start | bytes 1769480 | tf_op jit(solution)/shard_map/ppermute | solution.py:566
  447.4 32.9 %collective-permute-start.57 = (bf16[1,96,1536]{2,1,0:T(8,128)(2,1)S(1)}, bf16[1,96,1536]{2,1,0:T(8,128)(2,1)}, u32[]{:S(2)}, u32[]{:S(2)}) collective-permute-start(bf16[1,96,1536]{2,1,0:T(8,128)(2,1)S(1)} %get-tuple-element.279), channel_id=1, source_target_pairs={{0,16},{4,20},{8,24},{12,28},{16,0},{20,4},{24,8},{28,12},{1,17},{... | collective-permute-start | bytes 884744 | tf_op jit(solution)/shard_map/ppermute | solution.py:566
  461.9 18.4 %collective-permute-start.56 = (bf16[1,96,1536]{2,1,0:T(8,128)(2,1)}, bf16[1,96,1536]{2,1,0:T(8,128)(2,1)}, u32[]{:S(2)}, u32[]{:S(2)}) collective-permute-start(bf16[1,96,1536]{2,1,0:T(8,128)(2,1)} %get-tuple-element.278), channel_id=1, source_target_pairs={{0,8},{4,12},{8,0},{12,4},{16,24},{20,28},{24,16},{28,20},{1,9},{5... | collective-permute-start | bytes 884744 | tf_op jit(solution)/shard_map/ppermute | solution.py:566
  489.1 22.3 %collective-permute-start.62 = (bf16[2,96,1536]{2,1,0:T(8,128)(2,1)S(1)}, bf16[2,96,1536]{2,1,0:T(8,128)(2,1)S(1)}, u32[]{:S(2)}, u32[]{:S(2)}) collective-permute-start(bf16[2,96,1536]{2,1,0:T(8,128)(2,1)S(1)} %pad_maximum_fusion.32), channel_id=1, source_target_pairs={{0,8},{4,12},{8,0},{12,4},{16,24},{20,28},{24,16},{28,20},{1,9},{5... | collective-permute-start | bytes 1769480 | tf_op jit(solution)/shard_map/ppermute | solution.py:566
  489.8 21.6 %collective-permute-start.61 = (bf16[2,96,1536]{2,1,0:T(8,128)(2,1)S(1)}, bf16[2,96,1536]{2,1,0:T(8,128)(2,1)S(1)}, u32[]{:S(2)}, u32[]{:S(2)}) collective-permute-start(bf16[2,96,1536]{2,1,0:T(8,128)(2,1)S(1)} %pad_maximum_fusion.31), channel_id=1, source_target_pairs={{0,16},{4,20},{8,24},{12,28},{16,0},{20,4},{24,8},{28,12},{1,17},{... | collective-permute-start | bytes 1769480 | tf_op jit(solution)/shard_map/ppermute | solution.py:566
  492.8 18.6 %collective-permute-start.60 = (bf16[1,2,48,1536]{3,2,1,0:T(8,128)(2,1)S(1)}, bf16[1,2,48,1536]{3,2,1,0:T(8,128)(2,1)S(1)}, u32[]{:S(2)}, u32[]{:S(2)}) collective-permute-start(bf16[1,2,48,1536]{3,2,1,0:T(8,128)(2,1)S(1)} %get-tuple-element.283), channel_id=1, source_target_pairs={{0,16},{4,20},{8,24},{12,28},{16,0},{20,4},{24,8},{28,12},{1,17},{... | collective-permute-start | bytes 884744 | tf_op jit(solution)/shard_map/ppermute | solution.py:566
  511.4 22.7 %collective-permute-start.64 = (bf16[2,768,256]{2,1,0:T(8,128)(2,1)S(1)}, bf16[2,768,256]{2,1,0:T(8,128)(2,1)S(1)}, u32[]{:S(2)}, u32[]{:S(2)}) collective-permute-start(bf16[2,768,256]{2,1,0:T(8,128)(2,1)S(1)} %pad_maximum_fusion.24), channel_id=1, source_target_pairs={{0,8},{4,12},{8,0},{12,4},{16,24},{20,28},{24,16},{28,20},{1,9},{5... | collective-permute-start | bytes 2359304 | tf_op jit(solution)/shard_map/ppermute | solution.py:566
  512.9 21.2 %collective-permute-start.63 = (bf16[2,768,256]{2,1,0:T(8,128)(2,1)S(1)}, bf16[2,768,256]{2,1,0:T(8,128)(2,1)S(1)}, u32[]{:S(2)}, u32[]{:S(2)}) collective-permute-start(bf16[2,768,256]{2,1,0:T(8,128)(2,1)S(1)} %pad_maximum_fusion.23), channel_id=1, source_target_pairs={{0,16},{4,20},{8,24},{12,28},{16,0},{20,4},{24,8},{28,12},{1,17},{... | collective-permute-start | bytes 2359304 | tf_op jit(solution)/shard_map/ppermute | solution.py:566
  538.6 24.4 %collective-permute-start.75 = (bf16[1,384,768]{2,1,0:T(8,128)(2,1)}, bf16[1,384,768]{2,1,0:T(8,128)(2,1)}, u32[]{:S(2)}, u32[]{:S(2)}) collective-permute-start(bf16[1,384,768]{2,1,0:T(8,128)(2,1)} %copy.72), channel_id=1, source_target_pairs={{0,8},{4,12},{8,0},{12,4},{16,24},{20,28},{24,16},{28,20},{1,9},{5... | collective-permute-start | bytes 1769480 | tf_op jit(solution)/shard_map/ppermute | solution.py:566
  539.3 36.7 %collective-permute-start.71 = (bf16[256,1536]{1,0:T(8,128)(2,1)}, bf16[256,1536]{1,0:T(8,128)(2,1)}, u32[]{:S(2)}, u32[]{:S(2)}) collective-permute-start(bf16[256,1536]{1,0:T(8,128)(2,1)} %add_convert_fusion.10), channel_id=1, source_target_pairs={{0,2},{1,3},{2,0},{3,1},{4,6},{5,7},{6,4},{7,5},{8,10},{9,11},{10,... | collective-permute-start | bytes 2359304 | tf_op jit(solution)/shard_map/ppermute | solution.py:566
  542.0 20.9 %collective-permute-start.74 = (bf16[1,768,256]{2,1,0:T(8,128)(2,1)}, bf16[1,768,256]{2,1,0:T(8,128)(2,1)}, u32[]{:S(2)}, u32[]{:S(2)}) collective-permute-start(bf16[1,768,256]{2,1,0:T(8,128)(2,1)} %get-tuple-element.297), channel_id=1, source_target_pairs={{0,16},{4,20},{8,24},{12,28},{16,0},{20,4},{24,8},{28,12},{1,17},{... | collective-permute-start | bytes 1179656 | tf_op jit(solution)/shard_map/ppermute | solution.py:566
  543.5 19.4 %collective-permute-start.73 = (bf16[1,768,256]{2,1,0:T(8,128)(2,1)}, bf16[1,768,256]{2,1,0:T(8,128)(2,1)}, u32[]{:S(2)}, u32[]{:S(2)}) collective-permute-start(bf16[1,768,256]{2,1,0:T(8,128)(2,1)} %get-tuple-element.296), channel_id=1, source_target_pairs={{0,8},{4,12},{8,0},{12,4},{16,24},{20,28},{24,16},{28,20},{1,9},{5... | collective-permute-start | bytes 1179656 | tf_op jit(solution)/shard_map/ppermute | solution.py:566
  575.9 28.3 %collective-permute-start.80 = (bf16[2,384,768]{2,1,0:T(8,128)(2,1)}, bf16[2,384,768]{2,1,0:T(8,128)(2,1)}, u32[]{:S(2)}, u32[]{:S(2)}) collective-permute-start(bf16[2,384,768]{2,1,0:T(8,128)(2,1)} %pad_maximum_fusion.16), channel_id=1, source_target_pairs={{0,8},{4,12},{8,0},{12,4},{16,24},{20,28},{24,16},{28,20},{1,9},{5... | collective-permute-start | bytes 3538952 | tf_op jit(solution)/shard_map/ppermute | solution.py:566
  578.9 34.8 %collective-permute-start.79 = (bf16[2,384,768]{2,1,0:T(8,128)(2,1)S(1)}, bf16[2,384,768]{2,1,0:T(8,128)(2,1)S(1)}, u32[]{:S(2)}, u32[]{:S(2)}) collective-permute-start(bf16[2,384,768]{2,1,0:T(8,128)(2,1)S(1)} %pad_maximum_fusion.15), channel_id=1, source_target_pairs={{0,16},{4,20},{8,24},{12,28},{16,0},{20,4},{24,8},{28,12},{1,17},{... | collective-permute-start | bytes 3538952 | tf_op jit(solution)/shard_map/ppermute | solution.py:566
  583.5 25.9 %collective-permute-start.84 = (bf16[384,256]{1,0:T(8,128)(2,1)S(1)}, bf16[384,256]{1,0:T(8,128)(2,1)S(1)}, u32[]{:S(2)}, u32[]{:S(2)}) collective-permute-start(bf16[384,256]{1,0:T(8,128)(2,1)S(1)} %get-tuple-element.307), channel_id=1, source_target_pairs={{0,3},{1,2},{2,1},{3,0},{4,7},{5,6},{6,5},{7,4},{8,11},{9,10},{10,... | collective-permute-start | bytes 589832 | tf_op jit(solution)/shard_map/ppermute | solution.py:566
  586.1 23.3 %collective-permute-start.83 = (bf16[384,256]{1,0:T(8,128)(2,1)S(1)}, bf16[384,256]{1,0:T(8,128)(2,1)S(1)}, u32[]{:S(2)}, u32[]{:S(2)}) collective-permute-start(bf16[384,256]{1,0:T(8,128)(2,1)S(1)} %get-tuple-element.306), channel_id=1, source_target_pairs={{0,2},{1,3},{2,0},{3,1},{4,6},{5,7},{6,4},{7,5},{8,10},{9,11},{10,... | collective-permute-start | bytes 589832 | tf_op jit(solution)/shard_map/ppermute | solution.py:566
  586.1 27.6 %collective-permute-start.81 = (bf16[2,48,1536]{2,1,0:T(8,128)(2,1)S(1)}, bf16[2,48,1536]{2,1,0:T(8,128)(2,1)S(1)}, u32[]{:S(2)}, u32[]{:S(2)}) collective-permute-start(bf16[2,48,1536]{2,1,0:T(8,128)(2,1)S(1)} %pad_maximum_fusion.37), channel_id=1, source_target_pairs={{0,16},{4,20},{8,24},{12,28},{16,0},{20,4},{24,8},{28,12},{1,17},{... | collective-permute-start | bytes 884744 | tf_op jit(solution)/shard_map/ppermute | solution.py:566
  641.5 18.6 %collective-permute-start.93 = (bf16[4,384,256]{2,1,0:T(8,128)(2,1)S(1)}, bf16[4,384,256]{2,1,0:T(8,128)(2,1)S(1)}, u32[]{:S(2)}, u32[]{:S(2)}) collective-permute-start(bf16[4,384,256]{2,1,0:T(8,128)(2,1)S(1)} %pad_maximum_fusion.26.near_ref), channel_id=1, source_target_pairs={{0,4},{4,0},{8,12},{12,8},{16,20},{20,16},{24,28},{28,24},{1,5},{5... | collective-permute-start | bytes 2359304 | tf_op jit(solution)/shard_map/ppermute | solution.py:566
  (169 other events, 1637.0 us)

commit v3 on v2

--- a/solution.py
+++ b/solution.py
@@ -340,40 +340,43 @@
     )(chunk_of, h, z, *wg, *wu, wd)
 
 
-def expert_grads_kernel(n, fc, *refs):
-    a, dg, du = refs[:n], refs[n : 2 * n], refs[2 * n : 3 * n]
-    h, z, out_ref = refs[3 * n : 4 * n], refs[4 * n : 5 * n], refs[5 * n]
+def expert_grads_kernel(n, fc, pairs, *refs):
+    out_ref = refs[-1]
     per = out_ref.shape[0]
-    for which, (left, right) in enumerate(((dg, h), (du, h), (a, z))):
+    rights = refs[pairs * n : -1]
+    for which in range(pairs):
+        left, right = refs[which * n : (which + 1) * n], rights
         total = dot_tn(left[0][...], right[0][...])
         for s in range(1, n):
             total += dot_tn(left[s][...], right[s][...])
         out_ref[:, which] = total.astype(bf16).reshape(per, fc, total.shape[-1])
 
 
-def expert_grads(side, fc, a, dg, du, h, z):
-    n = len(a)
-    t, width = a[0].shape
+def expert_grads(side, fc, lefts, right):
+    n = len(right)
+    t, width = lefts[0][0].shape
     width = width // 2
-    d = h[0].shape[1]
+    d = right[0].shape[1]
     ct = min(width, 384)
     per = ct // fc
     steps = width // ct
     tile = pl.BlockSpec((t, ct), lambda j: (0, side * steps + j))
     rows = pl.BlockSpec((t, d), lambda j: (0, 0))
     if width % HEAD_WIDTH:
-        a, dg, du = ([x[:, side * width : (side + 1) * width] for x in xs] for xs in (a, dg, du))
+        lefts = [[x[:, side * width : (side + 1) * width] for x in xs] for xs in lefts]
         tile = pl.BlockSpec((t, width), lambda j: (0, 0))
+    pairs = len(lefts)
+    flat = [x for xs in lefts for x in xs]
     return pl.pallas_call(
-        functools.partial(expert_grads_kernel, n, fc),
+        functools.partial(expert_grads_kernel, n, fc, pairs),
         grid=(steps,),
-        in_specs=[tile] * (3 * n) + [rows] * (2 * n),
-        out_specs=pl.BlockSpec((per, 3, fc, d), lambda j: (j, 0, 0, 0)),
-        out_shape=jax.ShapeDtypeStruct((width // fc, 3, fc, d), bf16),
+        in_specs=[tile] * (pairs * n) + [rows] * n,
+        out_specs=pl.BlockSpec((per, pairs, fc, d), lambda j: (j, 0, 0, 0)),
+        out_shape=jax.ShapeDtypeStruct((width // fc, pairs, fc, d), bf16),
         compiler_params=params(58),
-        cost_estimate=cost(6 * n * t * d * width, 6 * d * width),
+        cost_estimate=cost(2 * pairs * n * t * d * width, 2 * pairs * d * width),
         name="expert_grads",
-    )(*a, *dg, *du, *h, *z)
+    )(*flat, *right)
 
 
 def join_kernel(half, slot_ref, *refs):
@@ -424,39 +427,6 @@
     )(slot_of, *flat)
 
 
-def split_kernel(half, chunk_ref, in_ref, near_ref, far_ref):
-    j = pl.program_id(0)
-
-    @pl.when(j < half)
-    def _():
-        far_ref[0] = in_ref[:, 0]
-
-    @pl.when(j >= half)
-    def _():
-        near_ref[0] = in_ref[:, 0]
-
-
-def split(chunk_of, x):
-    n, m, c, d = x.shape
-    half = m // 2
-    return pl.pallas_call(
-        functools.partial(split_kernel, half),
-        grid_spec=pltpu.PrefetchScalarGridSpec(
-            num_scalar_prefetch=1,
-            grid=(m,),
-            in_specs=[pl.BlockSpec((n, 1, c, d), lambda j, s: (0, s[(j + half) % m], 0, 0))],
-            out_specs=[
-                pl.BlockSpec((1, n, c, d), lambda j, s: (jnp.maximum(j - half, 0), 0, 0, 0)),
-                pl.BlockSpec((1, n, c, d), lambda j, s: (jnp.minimum(j, half - 1), 0, 0, 0)),
-            ],
-        ),
-        out_shape=[jax.ShapeDtypeStruct((half, n, c, d), x.dtype)] * 2,
-        compiler_params=params(16),
-        cost_estimate=cost(0, 4 * x.size),
-        name="split",
-    )(chunk_of, x)
-
-
 def columns_kernel(half, counts, slot_ref, near_ref, far_ref, *out_refs):
     j = pl.program_id(0)
     near = slot_ref[j] < half
@@ -497,8 +467,8 @@
     )(slot_of, near, far)
 
 
-def arrange_kernel(n, fc, rc, rank_ref, *refs):
-    slots, (gate_ref, up_ref, a_ref, b_ref) = refs[:n], refs[n:]
+def arrange_kernel(n, fc, rank_ref, *refs):
+    slots, (gate_ref, up_ref) = refs[:n], refs[n:]
     dl = slots[0].shape[1]
 
     def run(rank):
@@ -506,26 +476,55 @@
             block = slots[q ^ rank]
             gate_ref[:, q * dl : (q + 1) * dl] = block[:fc]
             up_ref[:, q * dl : (q + 1) * dl] = block[fc : 2 * fc]
-            out_ref = (a_ref, b_ref)[q // (n // 2)]
-            for b in range(n):
-                at = 2 * fc + b * rc
-                out_ref[q % (n // 2), :, b * dl : (b + 1) * dl] = block[at : at + rc]
 
     for rank in range(n):
         pl.when(rank_ref[0] == rank)(functools.partial(run, rank))
 
 
-def arrange(rank, slots, fc, rc):
+def arrange(rank, slots, fc):
     n, d = len(slots), len(slots) * slots[0].shape[1]
     vmem = pl.BlockSpec(memory_space=pltpu.VMEM)
     return pl.pallas_call(
-        functools.partial(arrange_kernel, n, fc, rc),
+        functools.partial(arrange_kernel, n, fc),
         in_specs=[pl.BlockSpec(memory_space=pltpu.SMEM)] + [vmem] * n,
-        out_specs=[vmem] * 4,
-        out_shape=[jax.ShapeDtypeStruct((fc, d), bf16)] * 2 + [jax.ShapeDtypeStruct((n // 2, rc, d), bf16)] * 2,
+        out_specs=[vmem] * 2,
+        out_shape=[jax.ShapeDtypeStruct((fc, d), bf16)] * 2,
         compiler_params=params(16),
         cost_estimate=cost(0, 8 * fc * d),
         name="arrange",
+    )(rank, *slots)
+
+
+def turn_back_kernel(n, fc, rank_ref, *refs):
+    slots, out_ref, rows = refs[:n], refs[n], refs[n + 1]
+
+    def run(rank):
+        for k in range(2):
+            for q in range(n):
+                rows[k, q * fc : (q + 1) * fc] = slots[q ^ rank][k * fc : (k + 1) * fc].astype(f32)
+
+    for rank in range(n):
+        pl.when(rank_ref[0] == rank)(functools.partial(run, rank))
+    for k in range(2):
+        out_ref[k] = rows[k].T.astype(bf16)
+
+
+def turn_back(rank, slots, fc):
+    n, dl = len(slots), slots[0].shape[1]
+    if fc % 16 or dl % HEAD_WIDTH or n * fc % HEAD_WIDTH:
+        stacked = jnp.stack(slots).reshape(n, 2, fc, dl)
+        stacked = jnp.take(stacked, jnp.arange(n) ^ rank, axis=0)
+        return jnp.transpose(stacked, (1, 3, 0, 2)).reshape(2, dl, n * fc)
+    vmem = pl.BlockSpec(memory_space=pltpu.VMEM)
+    return pl.pallas_call(
+        functools.partial(turn_back_kernel, n, fc),
+        in_specs=[pl.BlockSpec(memory_space=pltpu.SMEM)] + [vmem] * n,
+        out_specs=vmem,
+        out_shape=jax.ShapeDtypeStruct((2, dl, n * fc), bf16),
+        scratch_shapes=[pltpu.VMEM((2, n * fc, dl), f32)],
+        compiler_params=params(24),
+        cost_estimate=cost(0, 8 * n * fc * dl),
+        name="turn_back",
     )(rank, *slots)
 
 
@@ -733,56 +732,53 @@
         for w in (w_gate, w_up)
     ]
     flipped = lax.dynamic_index_in_dim(jnp.stack(flipped, 1), i % sub, 2, keepdims=False).reshape(n, 2 * fc, dl)
-    out_rows = lax.dynamic_slice_in_dim(w_out, i * rc, rc, 0).reshape(rc, n, dl)
-    out_rows = jnp.swapaxes(out_rows, 0, 1).reshape(1, n * rc, dl)
-    flipped = jnp.concatenate([flipped, jnp.broadcast_to(out_rows, (n, n * rc, dl))], 1)
     flipped = rounds.leave(flipped)
+    out_rows = lax.dynamic_slice_in_dim(w_out, i * rc, rc, 0)
     cos, sin = rotary(r * t + jnp.arange(t, dtype=jnp.int32))
     rounds.leave(cos, sin)
 
     rounds.turn()
     qkv_gather = Gather(along, own_qkv[: d // 2], own_qkv[d // 2 :])
     qkv_gather.step()
-    mix = [along.pieces(flipped, 0), along.cross(along.pieces(flipped, 1), 1)]
+    own_out = along.gather_cp(out_rows)
     normed_one, scaled_one, inverse_one = norm_forward(inputs, gain_one)
     h1 = rounds.leave(normed_one.astype(bf16))
     rounds.turn()
     qkv_gather.rest()
-    mix.append(along.cross(along.pieces(flipped, 2), 2))
+    mix = [along.pieces(flipped, 0)] + [along.cross(along.pieces(flipped, s), s) for s in (1, 2)]
+    own_out = rounds.leave(along.ranked(own_out))
     rounds.turn()
     qkv_a, qkv_b = qkv_gather.finish()
     mix.extend(along.cross(along.pieces(flipped, s), s, late=True) for s in range(3, n))
     rounds.turn()
     rank = r.reshape(1)
+    out_gather = Gather(along, own_out[: n // 2], own_out[n // 2 :])
+    out_gather.step()
     qkv = rounds.leave(project(along.slot_of, rounds.enter(h1), qkv_a, qkv_b, cos, sin))
     rounds.turn()
 
     own_kv = qkv[:, query_columns:]
     kv = jnp.concatenate([own_kv] + [along.cross(own_kv, s, up) for s in range(1, n)], 0)
+    out_gather.rest()
     if dl % HEAD_WIDTH == 0:
-        gate_rows, up_rows, out_first, out_second = arrange(rank, [rounds.enter(x) for x in mix], fc, rc)
+        gate_rows, up_rows = arrange(rank, [rounds.enter(x) for x in mix], fc)
     else:
-        got = along.ranked(mix)
-        gate_rows, up_rows = jnp.swapaxes(got[:, : 2 * fc], 0, 1).reshape(2, fc, d)
-        own_out = jnp.swapaxes(got[:, 2 * fc :].reshape(n, n, rc, dl), 1, 2).reshape(n, rc, d)
-        out_first, out_second = own_out[: n // 2], own_out[n // 2 :]
-    out_gather = Gather(along, out_first, out_second)
-    out_gather.step()
+        gate_rows, up_rows = jnp.swapaxes(along.ranked(mix), 0, 1).reshape(2, fc, d)
     mix_gather = Gather(along, gate_rows, up_rows)
     mix_gather.step()
     rounds.turn()
     z_relay = Relay(along, dz)
     z_relay.two()
-    out_gather.rest()
     mix_gather.rest()
+    out_a, out_b = out_gather.finish()
     ob = rounds.leave(attend(rank, qkv, rounds.enter(kv)))
+    full_out = join(along.slot_of, [out_a, out_b], bf16, True).reshape(n * dl, d)
+    full_out = rounds.leave(full_out)
     rounds.turn()
     z_relay.one()
     z_relay.middle()
-    out_a, out_b = out_gather.finish()
     wg, wu = mix_gather.finish()
     wd = w_down.reshape(m, fc, d)
-    full_out = join(along.slot_of, [out_a, out_b], bf16, True).reshape(n * dl, d)
 
     middle = inputs + dot_nn(rounds.enter(ob), full_out)
     normed_two, scaled_two, inverse_two = norm_forward(middle, gain_two)
@@ -832,22 +828,21 @@
     else:
         for s in range(3, n):
             h2_back = h2_back + along.cross(done[s][4], s).astype(f32)
-    mix_far = rounds.leave(expert_grads(1, fc, *triples, h_slots, z_slots).reshape(m // 2, 3 * fc, d))
+    mix_far = rounds.leave(expert_grads(1, fc, triples[1:], h_slots).reshape(m // 2, 2 * fc, d))
+    mix_reduce = Reduce(along, mix_far)
+    mix_near = rounds.leave(expert_grads(0, fc, triples[1:], h_slots).reshape(m // 2, 2 * fc, d))
     rounds.turn()
     h2_back = h2_back + along.cross(second, 2).astype(f32)
-    mix_reduce = Reduce(along, mix_far)
-    triples = [[rounds.enter(x) for x in xs] for xs in triples]
-    mix_near = rounds.leave(expert_grads(0, fc, *triples, h_slots, z_slots).reshape(m // 2, 3 * fc, d))
-    rounds.turn()
     mix_reduce.add(mix_near)
-    mix_reduce.step()
-
+    mix_reduce.rest()
+    acts = [rounds.enter(x) for x in triples[0]]
+    down_grads = [expert_grads(side, fc, [acts], z_slots).reshape(m // 2, fc, d) for side in (0, 1)]
+    down_grads = rounds.leave(join(along.slot_of, [down_grads], bf16))
+    rounds.turn()
+    own_mix = mix_reduce.finish()
+    back = [lax.dynamic_slice_in_dim(own_mix, (r ^ s) * dl, dl, 1) for s in range(n)]
+    back = [back[0]] + [along.cross(back[s], s) for s in range(1, n)]
     mixed = done[0][3] + along.cross(done[1][3], 1).astype(f32)
-    second_out = done[2][3]
-    if n == 4:
-        mixed = mixed + along.send(done[3][3], "cp", Relay.inside).astype(f32)
-        second_out = second_out.astype(f32) + along.send(done[3][3], "cp", Relay.turned).astype(f32)
-        second_out = second_out.astype(bf16)
     h2_back = rounds.enter(h2_back)
     slot_gate_grad = h2_back[t : t + m, :t] + h2_back[t : t + m, t : 2 * t]
     gate_grad = jnp.sum(slot_gate_grad.T[:, None, :] * slot_flags, -1)
@@ -861,92 +856,80 @@
     branch = middle_grad.astype(bf16)
 
     dob = dot_nt(branch, full_out).astype(bf16)
-    out_grads = dot_tn(ob, branch).astype(bf16)
-    out_near, out_far = split(along.chunk_of, out_grads.reshape(n, m, rc, d))
+    out_grads = jnp.swapaxes(dot_tn(ob, branch).astype(bf16).reshape(n, m, rc, d), 0, 1).reshape(m * n * rc, d)
+    out_grads = lax.psum_scatter(out_grads, "dp", scatter_dimension=0, tiled=True)
     dq, dkv = attend_back(rank, qkv, kv, dob, cos, sin)
-    rounds.leave(dkv, out_near, out_far)
+    rounds.leave(dkv)
     rounds.turn()
     dkv_own = dkv[:, :t].astype(f32)
     for s in range(1, n):
         dkv_own = dkv_own + along.cross(dkv[:, s * t : (s + 1) * t], s, down).astype(f32)
-    mix_reduce.rest()
-    out_reduce = Reduce(along, out_far)
-    rounds.turn()
-    out_reduce.add(out_near)
-    out_reduce.step()
+    back = turn_back(rank, [rounds.enter(x) for x in back], fc)
+    back_gather = Gather(along, back[0], back[1])
+    back_gather.step()
+    rounds.turn()
+    back_gather.rest()
+    down_grads = lax.psum(rounds.enter(after(down_grads, out_grads)), "dp")
+    grad_w_down = down_grads.reshape(EXPERTS, fs, d).astype(f32)
+    second_out = done[2][3]
+    if n == 4:
+        mixed = mixed + along.send(done[3][3], "cp", Relay.inside).astype(f32)
+        second_out = second_out.astype(f32) + along.send(done[3][3], "cp", Relay.turned).astype(f32)
+        second_out = second_out.astype(bf16)
     dkv_own = rounds.enter(dkv_own)
     dk = dkv_own[0].reshape(t, KEY_VALUE_HEADS, HEAD_WIDTH)
     half = HEAD_WIDTH // 2
     dk = dk * cos[:, None] - jnp.concatenate([dk[..., half:], dk[..., :half]], -1) * sin[:, None]
     dqkv = jnp.concatenate([dq, dk.reshape(t, key_columns).astype(bf16), dkv_own[1].astype(bf16)], 1)
-    own_mix = mix_reduce.finish()
-    back = [lax.dynamic_slice_in_dim(own_mix[: 2 * fc], (r ^ s) * dl, dl, 1) for s in range(n)]
-    back = [back[0]] + [along.cross(back[s], s) for s in range(1, n)]
-    own_down = own_mix[2 * fc :]
-    down_gather = Gather(along, own_down[: fc // 2], own_down[fc // 2 :])
-    down_gather.step()
     h1_grad, qkv_near, qkv_far = project_back(along.chunk_of, h1, dqkv, qkv_a, qkv_b)
     rounds.leave(h1_grad, qkv_near, qkv_far)
-    rounds.turn()
-
-    def sum_cp(x):
-        return functools.reduce(jnp.add, [y.astype(f32) for y in along.scatter_cp(x)]).astype(bf16)
-
     qkv_reduce = Reduce(along, qkv_far)
-    out_reduce.rest()
-    down_gather.rest()
-    input_norm_grad, gain_one_grad = norm_backward(h1_grad, gain_one, scaled_one, inverse_one)
+    rounds.turn()
+    qkv_reduce.add(qkv_near)
+    qkv_reduce.step()
+    back_slots = back_gather.finish()
+    out_grads = lax.all_to_all(rounds.enter(out_grads.reshape(n, rc, d)), "cp", 0, 0, tiled=True)
+    out_grads = rounds.leave(jnp.sum(out_grads.astype(f32), 0).astype(bf16))
+    input_norm_grad, gain_one_grad = norm_backward(rounds.enter(h1_grad), gain_one, scaled_one, inverse_one)
     input_grad = (middle_grad + input_norm_grad).astype(bf16)[None]
     small_grads = jnp.concatenate([gain_one_grad[None], gain_two_grad[None], router_grad], 0)
-    small_grads = rounds.leave(jnp.transpose(small_grads.reshape(2 + EXPERTS, n, dl), (1, 0, 2)))
-    back = along.ranked(back).reshape(n, 2, fc, dl)
-    back = rounds.leave(jnp.transpose(back, (1, 3, 0, 2)).reshape(2, dl, n * fc))
-    rounds.turn()
-    qkv_reduce.add(qkv_near)
-    qkv_reduce.step()
-    own_out = sum_cp(out_reduce.finish())
-    small_grads = functools.reduce(jnp.add, along.scatter_cp(small_grads))
+    rounds.leave(small_grads)
     rounds.turn()
     qkv_reduce.rest()
-    back_gather = Gather(along, back[0], back[1])
-    back_gather.step()
-    out_gather = Gather(along, own_out)
-    out_gather.step()
     small_grads = small_grads + along.swap(small_grads, along.inner)
-    mixed = mixed + along.cross(second_out, 2).astype(f32)
-    rounds.turn()
-    back_gather.rest()
-    out_gather.rest()
-    own_qkv = sum_cp(qkv_reduce.finish().reshape(n, dl, cw))
-    small_grads = small_grads + along.swap(small_grads, 0)
-    if n != 4:
-        for s in range(3, n):
-            mixed = mixed + along.cross(done[s][3], s).astype(f32)
-    rounds.turn()
-    qkv_gather = Gather(along, own_qkv)
-    qkv_gather.step()
-    back_slots = back_gather.finish()
-    (out_slots,) = out_gather.finish()
-    down_a, down_b = down_gather.finish()
-    for bit in range(1, along.inner):
-        small_grads = small_grads + along.swap(small_grads, bit)
-    output = (middle + mixed).astype(bf16)[None]
-    rounds.turn()
-    qkv_gather.rest()
-    grad_w_down = join(along.slot_of, [down_a, down_b], f32)
-    rounds.leave(grad_w_down)
-    grad_w_down = grad_w_down.reshape(EXPERTS, fs, d)
-    rounds.turn()
-    (qkv_slots,) = qkv_gather.finish()
+    second_out = rounds.enter(second_out)
+    mixed = mixed + lax.ppermute(second_out, "cp", [(k, k ^ 2) for k in range(n)]).astype(f32)
+    grad_w_out = lax.all_gather(rounds.enter(out_grads), "dp", axis=0, tiled=True).astype(f32)
     grads = []
     for slots in back_slots:
-        g = join(along.slot_of, [slots], f32)
+        g = rounds.leave(join(along.slot_of, [[rounds.enter(x) for x in slots]], f32))
         if sub > 1:
             g = g.reshape(EXPERTS, sub, dl, n, fc)
             g = jnp.transpose(g, (0, 2, 3, 1, 4))
         grads.append(g.reshape(EXPERTS, dl, ff))
     grad_w_gate, grad_w_up = grads
-    grad_w_out = join(along.slot_of, [out_slots], f32).reshape(dl, d)
+    rounds.turn()
+    own_qkv = qkv_reduce.finish().reshape(n, dl, cw)
+    own_qkv = [along.pieces(own_qkv, 0)] + [along.cross(along.pieces(own_qkv, s), s) for s in range(1, n)]
+    own_qkv = functools.reduce(jnp.add, [x.astype(f32) for x in own_qkv]).astype(bf16)
+    small_grads = small_grads + along.swap(small_grads, 0)
+    if n != 4:
+        for s in range(3, n):
+            mixed = mixed + along.cross(done[s][3], s).astype(f32)
+    rounds.turn()
+    qkv_gather = Gather(along, own_qkv)
+    qkv_gather.step()
+    for bit in range(1, along.inner):
+        small_grads = small_grads + along.swap(small_grads, bit)
+    rounds.turn()
+    qkv_gather.rest()
+    small_grads = small_grads + along.cross(small_grads, 1)
+    rounds.turn()
+    (qkv_slots,) = qkv_gather.finish()
+    for bit in range(1, n.bit_length() - 1):
+        small_grads = small_grads + along.cross(small_grads, 1 << bit)
+    output = (middle + mixed).astype(bf16)[None]
+    small_grads = lax.dynamic_index_in_dim(small_grads.reshape(2 + EXPERTS, n, dl), r, 1, keepdims=False)
     grad_w_query, grad_w_key, grad_w_value = columns(
         along.slot_of, *qkv_slots, (query_columns, key_columns, key_columns)
     )

time: 675 us -> 645 us (0.956)
  starting transfers between devices: 135 us -> 117 us
  other arithmetic: 78.9 us -> 63.4 us
  between operations: 2.76 us -> 15.9 us
  waiting for transfers between devices: 235 us -> 224 us
    ppermute x94 -> x78, waiting for transfers between devices: 235 us -> 197 us  [send(): return leave(lax.ppermute(self.rounds.enter(x), axis, pairs))]
    ppermute x94 -> x78, starting transfers between devices: 135 us -> 112 us  [send(): return leave(lax.ppermute(self.rounds.enter(x), axis, pairs))]
    ppermute x0 -> x1, waiting for transfers between devices: none -> 14.9 us  [local(): lax.ppermute(second_out, 'cp', [(k, k ^ 2) for k in range(n)]).astype(f32)]
    all_gather x0 -> x1, waiting for transfers between devices: none -> 12.2 us  [local(): lax.all_gather(rounds.enter(out_grads), 'dp', axis=0, tiled=True)]
    convert_element_type x0 -> x2, other arithmetic: none -> 10.4 us  [the longest x1 7.4 us: local(): grad_w_down = down_grads.reshape(EXPERTS, fs, d).astype(f32)]
    convert_element_type x6 -> x4, other arithmetic: 16.4 us -> 7.64 us  [step(): held[h].astype(bf16)]
    unnamed x247 -> x216, local copies, waits for them, and re-layouts: 34.4 us -> 28 us
    another operation x13 -> x9, other arithmetic: 14.6 us -> 9.33 us  [finish(): near = [jnp.stack([held[h] for h in sorted(held)]) for held in self.parts]]
  transfers between devices with their start and end apart: 94 -> 83, of which waited for: 37 -> 36; matrix products, arithmetic and copies ran while one was open for 14% -> 12% of each run, Pallas kernels for 23% -> 24%
where the time goes in v3:
time: 645 us; the launch traced here: 635 us
  waiting for transfers between devices  224 us (35%)
  Pallas kernels  161 us (25%)
  starting transfers between devices  117 us (18%)
  other arithmetic  63.4 us (10%)
  local copies, waits for them, and re-layouts  44.1 us (7%)
  between operations  15.9 us (2%)
  matrix products  9.21 us (1%)
    ppermute x78, waiting for transfers between devices, send(): return leave(lax.ppermute(self.rounds.enter(x), axis, pairs))  197 us
    ppermute x78, starting transfers between devices, send(): return leave(lax.ppermute(self.rounds.enter(x), axis, pairs))  112 us
    pallas_call x4, Pallas kernels, experts(): pl.pallas_call(experts_kernel, in_specs=[pl.BlockSpec(memory_space=pltpu....  54.8 us
    pallas_call x4, Pallas kernels, expert_grads(): pl.pallas_call(functools.partial(expert_grads_kernel, n, fc, pairs), grid...  31.3 us
    unnamed x216, local copies, waits for them, and re-layouts  28 us
    pallas_call x4, Pallas kernels, join(): pl.pallas_call(functools.partial(join_kernel, half), grid_spec=pltpu.Pref...  25.4 us
    pallas_call x1, Pallas kernels, attend_back(): pl.pallas_call(attend_back_kernel, grid_spec=pltpu.PrefetchScalarGridSpec...  23.9 us
    ppermute x1, waiting for transfers between devices, local(): lax.ppermute(second_out, 'cp', [(k, k ^ 2) for k in range(n)]).astype(f32)  14.9 us
  transfers between devices with their start and end apart: 83, of which 36 were waited for; matrix products, arithmetic and copies ran while one was open for 12% of the time, Pallas kernels for 24%

profile of v3, /device:TPU:0, one launch (start us, length us, event | category | flops | bytes accessed | tf_op | source)
XLA Modules:
  0.0 634.5 jit_solution(3539035793729324292)
XLA Ops:
  10.4 5.1 collective-permute-start
  23.1 10.0 %collective-permute-done.1 = bf16[400,256]{1,0:T(8,128)(2,1)} collective-permute-done((bf16[400,256]{1,0:T(8,128)(2,1)S(1)}, bf16[400,256]{1,0:T(8,128)(2,1)}, u32[]{:S(2)}, u32[]{:S(2)}) %collective-permute-start.1) | collective-permute-done | bytes 204832 | tf_op jit(solution)/shard_map/ppermute | solution.py:565
  42.4 5.9 collective-permute-done.4
  55.9 10.5 %collective-permute-done.9 = bf16[2,768,256]{2,1,0:T(8,128)(2,1)S(1)} collective-permute-done((bf16[2,768,256]{2,1,0:T(8,128)(2,1)S(1)}, bf16[2,768,256]{2,1,0:T(8,128)(2,1)S(1)}, u32[]{:S(2)}, u32[]{:S(2)}) %collective-permute-start.9) | collective-permute-done | bytes 786464 | tf_op jit(solution)/shard_map/ppermute | solution.py:565
  74.6 4.5 project.1.q_ref
  87.3 4.0 collective-permute-start.17
  91.3 4.3 collective-permute-done.17
  99.3 4.0 collective-permute-start.19
  107.2 3.6 collective-permute-done.21
  116.2 12.4 %collective-permute-start.24 = (bf16[256,1536]{1,0:T(8,128)(2,1)}, bf16[256,1536]{1,0:T(8,128)(2,1)}, u32[]{:S(2)}, u32[]{:S(2)}) collective-permute-start(bf16[256,1536]{1,0:T(8,128)(2,1)} %bitcast.30.z_ref.refs_4_), channel_id=1, source_target_pairs={{0,2},{1,3},{2,0},{3,1},{4,6},{5,7},{6,4},{7,5},{8,10},{9,11},{10,... | collective-permute-start | bytes 2359304 | tf_op jit(solution)/shard_map/ppermute | solution.py:565
  130.1 10.3 %attend.1 = bf16[256,1536]{1,0:T(8,128)(2,1)S(1)} custom-call(s32[1]{0:T(128)} %bitcast.1.rank_ref, bf16[256,2048]{1,0:T(8,128)(2,1)S(1)} %copy-done.6, bf16[1024,512]{1,0:T(8,128)(2,1)S(1)} %pad_maximum_fusion.15.k_ref.v_ref, bf16[1024,512]{1,0:T(8,128)(2,1)S(1)} %pad_maximum_fusion.15.k_ref.v_ref), custom_call_target="tpu_custom_call" | custom-call | flops 16106 | bytes 15 | tf_op jit(solution)/shard_map/attend/pallas_call | solution.py:165
  140.4 6.2 join.4
  146.7 16.5 %collective-permute-done.24.z_ref.refs_6_ = bf16[256,1536]{1,0:T(8,128)(2,1)} collective-permute-done((bf16[256,1536]{1,0:T(8,128)(2,1)}, bf16[256,1536]{1,0:T(8,128)(2,1)}, u32[]{:S(2)}, u32[]{:S(2)}) %collective-permute-start.24) | collective-permute-done | bytes 786464 | tf_op jit(solution)/shard_map/ppermute | solution.py:565
  175.5 7.3 %collective-permute-done.29.z_ref.refs_5_ = bf16[256,1536]{1,0:T(8,128)(2,1)} collective-permute-done((bf16[256,1536]{1,0:T(8,128)(2,1)}, bf16[256,1536]{1,0:T(8,128)(2,1)}, u32[]{:S(2)}, u32[]{:S(2)}) %collective-permute-start.29) | collective-permute-done | bytes 786464 | tf_op jit(solution)/shard_map/ppermute | solution.py:565
  182.8 3.6 collective-permute-start.33
  187.4 14.2 %experts.4 = (bf16[256,1536]{1,0:T(8,128)(2,1)S(1)}, bf16[256,1536]{1,0:T(8,128)(2,1)S(1)}, bf16[256,1536]{1,0:T(8,128)(2,1)S(1)}, f32[256,1536]{1,0:T(8,128)S(1)}, f32[272,1536]{1,0:T(8,128)}) custom-call(s32[8]{0:T(128)S(1)} %fusion.53.chunk_ref, bf16[272,1536]{1,0:T(8,128)(2,1)S(1)} %maximum_maximum_fusion.h_ref.refs_8_, ...), custom_call_target="tpu_custom_call" | custom-call | flops 72477 | bytes 141 | tf_op jit(solution)/shard_map/experts/pallas_call | solution.py:319
  209.9 13.6 %experts.5 = (bf16[256,1536]{1,0:T(8,128)(2,1)S(1)}, bf16[256,1536]{1,0:T(8,128)(2,1)S(1)}, bf16[256,1536]{1,0:T(8,128)(2,1)S(1)}, bf16[256,1536]{1,0:T(8,128)(2,1)S(1)}, bf16[272,1536]{1,0:T(8,128)(2,1)S(1)}) custom-call(s32[8]{0:T(128)S(1)} %fusion.53.chunk_ref, bf16[272,1536]{1,0:T(8,128)(2,1)S(1)} %collective-permute-done.33.h_ref.refs_9_, ...), custom_call_target="tpu_custom_call" | custom-call | flops 72477 | bytes 141 | tf_op jit(solution)/shard_map/experts/pallas_call | solution.py:319
  228.0 16.5 %collective-permute-done.36 = bf16[256,1536]{1,0:T(8,128)(2,1)S(1)} collective-permute-done((bf16[256,1536]{1,0:T(8,128)(2,1)}, bf16[256,1536]{1,0:T(8,128)(2,1)S(1)}, u32[]{:S(2)}, u32[]{:S(2)}) %collective-permute-start.36) | collective-permute-done | bytes 786464 | tf_op jit(solution)/shard_map/ppermute | solution.py:565
  246.8 13.9 %experts.6 = (bf16[256,1536]{1,0:T(8,128)(2,1)S(1)}, bf16[256,1536]{1,0:T(8,128)(2,1)S(1)}, bf16[256,1536]{1,0:T(8,128)(2,1)S(1)}, bf16[256,1536]{1,0:T(8,128)(2,1)S(1)}, bf16[272,1536]{1,0:T(8,128)(2,1)S(1)}) custom-call(s32[8]{0:T(128)S(1)} %fusion.53.chunk_ref, bf16[272,1536]{1,0:T(8,128)(2,1)} %collective-permute-done.35.h_ref.refs_10_, ...), custom_call_target="tpu_custom_call" | custom-call | flops 72477 | bytes 141 | tf_op jit(solution)/shard_map/experts/pallas_call | solution.py:319
  261.7 4.5 collective-permute-done.37
  267.9 13.2 %experts.7 = (bf16[256,1536]{1,0:T(8,128)(2,1)S(1)}, bf16[256,1536]{1,0:T(8,128)(2,1)S(1)}, bf16[256,1536]{1,0:T(8,128)(2,1)S(1)}, bf16[256,1536]{1,0:T(8,128)(2,1)S(1)}, bf16[272,1536]{1,0:T(8,128)(2,1)S(1)}) custom-call(s32[8]{0:T(128)S(1)} %fusion.53.chunk_ref, bf16[272,1536]{1,0:T(8,128)(2,1)S(1)} %broadcast_select_fusion.h_ref.refs_11_, ...), custom_call_target="tpu_custom_call" | custom-call | flops 72477 | bytes 141 | tf_op jit(solution)/shard_map/experts/pallas_call | solution.py:319
  285.6 9.4 %expert_grads.4 = bf16[4,2,192,1536]{3,2,1,0:T(8,128)(2,1)} custom-call(bf16[256,1536]{1,0:T(8,128)(2,1)} %copy-done.25, bf16[256,1536]{1,0:T(8,128)(2,1)} %copy-done.27, bf16[256,1536]{1,0:T(8,128)(2,1)} %copy-done.29, bf16[256,1536]{1,0:T(8,128)(2,1)} %copy-done.31, bf16[256,1536]{1,0:T(8,128)(2,1)} %copy-done.26, bf16[256,1536]{1,0:T(8,128)(2,1)} %copy-done.28, ...), custom_call_target="tpu_custom_call" | custom-call | flops 48318 | bytes 47 | tf_op jit(solution)/shard_map/expert_grads/pallas_call | solution.py:370
  295.0 4.5 collective-permute-start.39
  301.5 9.4 %expert_grads.5 = bf16[4,2,192,1536]{3,2,1,0:T(8,128)(2,1)} custom-call(bf16[256,1536]{1,0:T(8,128)(2,1)} %copy-done.25, bf16[256,1536]{1,0:T(8,128)(2,1)} %copy-done.27, bf16[256,1536]{1,0:T(8,128)(2,1)} %copy-done.29, bf16[256,1536]{1,0:T(8,128)(2,1)} %copy-done.31, bf16[256,1536]{1,0:T(8,128)(2,1)} %copy-done.26, bf16[256,1536]{1,0:T(8,128)(2,1)} %copy-done.28, ...), custom_call_target="tpu_custom_call" | custom-call | flops 48318 | bytes 47 | tf_op jit(solution)/shard_map/expert_grads/pallas_call | solution.py:370
  321.2 3.6 collective-permute-start.42
  324.8 6.2 expert_grads.7
  330.9 6.3 expert_grads.6
  350.9 10.4 %collective-permute-done.42 = bf16[272,1536]{1,0:T(8,128)(2,1)} collective-permute-done((bf16[272,1536]{1,0:T(8,128)(2,1)}, bf16[272,1536]{1,0:T(8,128)(2,1)}, u32[]{:S(2)}, u32[]{:S(2)}) %collective-permute-start.42) | collective-permute-done | bytes 835616 | tf_op jit(solution)/shard_map/ppermute | solution.py:565
  380.7 5.1 convolution_convert_fusion.1.g_ref
  385.9 23.9 %attend_back.1 = (bf16[256,1536]{1,0:T(8,128)(2,1)}, bf16[2,1024,256]{2,1,0:T(8,128)(2,1)}) custom-call(s32[1]{0:T(128)} %bitcast.1.rank_ref, bf16[256,2048]{1,0:T(8,128)(2,1)} %copy-done.5, bf16[1024,512]{1,0:T(8,128)(2,1)} %copy-done, bf16[1024,512]{1,0:T(8,128)(2,1)} %copy-done, bf16[256,1536]{1,0:T(8,128)(2,1)} %convolution_convert_fusion.1.g_ref, ...), custom_call_target="tpu_custom_call" | custom-call | flops 40265 | bytes 31 | tf_op jit(solution)/shard_map/attend_back/pallas_call | solution.py:214
  418.5 9.0 %collective-permute-done.53 = bf16[2,256,256]{2,1,0:T(8,128)(2,1)S(1)} collective-permute-done((bf16[2,256,256]{2,1,0:T(8,128)(2,1)S(1)}, bf16[2,256,256]{2,1,0:T(8,128)(2,1)S(1)}, u32[]{:S(2)}, u32[]{:S(2)}) %collective-permute-start.53) | collective-permute-done | bytes 262176 | tf_op jit(solution)/shard_map/ppermute | solution.py:565
  427.5 9.3 %collective-permute-done.52 = bf16[2,256,256]{2,1,0:T(8,128)(2,1)S(1)} collective-permute-done((bf16[2,256,256]{2,1,0:T(8,128)(2,1)S(1)}, bf16[2,256,256]{2,1,0:T(8,128)(2,1)S(1)}, u32[]{:S(2)}, u32[]{:S(2)}) %collective-permute-start.52) | collective-permute-done | bytes 262176 | tf_op jit(solution)/shard_map/ppermute | solution.py:565
  446.0 6.0 project_back.1
  459.0 21.7 %collective-permute-done.59 = bf16[2,384,768]{2,1,0:T(8,128)(2,1)S(1)} collective-permute-done((bf16[2,384,768]{2,1,0:T(8,128)(2,1)S(1)}, bf16[2,384,768]{2,1,0:T(8,128)(2,1)S(1)}, u32[]{:S(2)}, u32[]{:S(2)}) %collective-permute-start.59) | collective-permute-done | bytes 1179680 | tf_op jit(solution)/shard_map/ppermute | solution.py:565
  489.2 4.2 all-to-all-start
  495.9 9.4 %collective-permute-done.62 = bf16[2,768,256]{2,1,0:T(8,128)(2,1)} collective-permute-done((bf16[2,768,256]{2,1,0:T(8,128)(2,1)}, bf16[2,768,256]{2,1,0:T(8,128)(2,1)}, u32[]{:S(2)}, u32[]{:S(2)}) %collective-permute-start.62) | collective-permute-done | bytes 786464 | tf_op jit(solution)/shard_map/ppermute | solution.py:565
  505.3 3.7 collective-permute-done.61
  515.4 10.1 %join.7 = f32[8,384,768]{2,1,0:T(8,128)} custom-call(s32[8]{0:T(128)S(1)} %shift-left_or_fusion.slot_ref, bf16[4,384,768]{2,1,0:T(8,128)(2,1)} %pad_maximum_fusion.3.refs_0_, bf16[4,384,768]{2,1,0:T(8,128)(2,1)} %collective-permute-done.64.refs_1_), custom_call_target="tpu_custom_call" | custom-call | bytes 141 | tf_op jit(solution)/shard_map/join/pallas_call | solution.py:418
  525.5 8.0 %join.6 = f32[8,384,768]{2,1,0:T(8,128)} custom-call(s32[8]{0:T(128)S(1)} %shift-left_or_fusion.slot_ref, bf16[4,384,768]{2,1,0:T(8,128)(2,1)S(1)} %pad_maximum_fusion.2.refs_0_, bf16[4,384,768]{2,1,0:T(8,128)(2,1)} %collective-permute-done.63.refs_1_), custom_call_target="tpu_custom_call" | custom-call | bytes 141 | tf_op jit(solution)/shard_map/join/pallas_call | solution.py:418
  535.8 4.3 collective-permute-start.70
  545.4 7.0 %collective-permute-done.71 = bf16[384,256]{1,0:T(8,128)(2,1)S(1)} collective-permute-done((bf16[384,256]{1,0:T(8,128)(2,1)S(1)}, bf16[384,256]{1,0:T(8,128)(2,1)S(1)}, u32[]{:S(2)}, u32[]{:S(2)}) %collective-permute-start.71) | collective-permute-done | bytes 196640 | tf_op jit(solution)/shard_map/ppermute | solution.py:565
  554.9 7.6 %collective-permute-done.74 = bf16[1,384,256]{2,1,0:T(8,128)(2,1)S(1)} collective-permute-done((bf16[1,384,256]{2,1,0:T(8,128)(2,1)S(1)}, bf16[1,384,256]{2,1,0:T(8,128)(2,1)S(1)}, u32[]{:S(2)}, u32[]{:S(2)}) %collective-permute-start.74) | collective-permute-done | bytes 196640 | tf_op jit(solution)/shard_map/ppermute | solution.py:565
  563.0 11.2 %collective-permute-done.76 = bf16[2,384,256]{2,1,0:T(8,128)(2,1)S(1)} collective-permute-done((bf16[2,384,256]{2,1,0:T(8,128)(2,1)S(1)}, bf16[2,384,256]{2,1,0:T(8,128)(2,1)S(1)}, u32[]{:S(2)}, u32[]{:S(2)}) %collective-permute-start.76) | collective-permute-done | bytes 393248 | tf_op jit(solution)/shard_map/ppermute | solution.py:565
  574.3 5.4 collective-permute-done.75
  582.9 14.9 %collective-permute-done.65 = bf16[256,1536]{1,0:T(8,128)(2,1)S(1)} collective-permute-done((bf16[256,1536]{1,0:T(8,128)(2,1)S(1)}, bf16[256,1536]{1,0:T(8,128)(2,1)S(1)}, u32[]{:S(2)}, u32[]{:S(2)}) %collective-permute-start.65) | collective-permute-done | bytes 786464 | tf_op jit(solution)/shard_map/ppermute | solution.py:901
  601.1 7.4 %convert_element_type.483 = f32[8,192,1536]{2,1,0:T(8,128)} convert(bf16[8,192,1536]{2,1,0:T(8,128)(2,1)} %all-reduce.4.cloned.1.call-done) | non-fusion elementwise | flops 2359296 | bytes 14155776 | tf_op jit(solution)/shard_map/convert_element_type | solution.py:873
  608.5 4.1 columns.1
  612.6 12.2 %all-gather.2.cloned.1.call-done = bf16[384,1536]{1,0:T(8,128)(2,1)} async-done(((bf16[48,1536]{1,0:T(8,128)(2,1)}), bf16[384,1536]{1,0:T(8,128)(2,1)}) %all-gather.2.cloned.1.call-update) | async-done | bytes 1179664 | tf_op jit(solution)/shard_map/all_gather | solution.py:902
  (489 shorter events, 200.4 us)
Async XLA Ops:
  7.2 482.0 %reduce-scatter.2.cloned.1.call-start = ((), (), s32[]{:S(2)}) async-start(), calls=%async_computation.2 | async-start | bytes 5308416 | tf_op jit(solution)/shard_map/reduce_scatter | solution.py:860
  84.2 22.9 %collective-permute-start.22 = (bf16[1,192,1536]{2,1,0:T(8,128)(2,1)S(1)}, bf16[1,192,1536]{2,1,0:T(8,128)(2,1)S(1)}, u32[]{:S(2)}, u32[]{:S(2)}) collective-permute-start(bf16[1,192,1536]{2,1,0:T(8,128)(2,1)S(1)} %bitcast.139), channel_id=1, source_target_pairs={{0,8},{4,12},{8,0},{12,4},{16,24},{20,28},{24,16},{28,20},{1,9},{5... | collective-permute-start | bytes 1769480 | tf_op jit(solution)/shard_map/ppermute | solution.py:565
  85.0 25.8 %collective-permute-start.21 = (bf16[2,2,48,1536]{3,2,1,0:T(8,128)(2,1)S(1)}, bf16[2,2,48,1536]{3,2,1,0:T(8,128)(2,1)S(1)}, u32[]{:S(2)}, u32[]{:S(2)}) collective-permute-start(bf16[2,2,48,1536]{3,2,1,0:T(8,128)(2,1)S(1)} %pad_maximum_fusion.25), channel_id=1, source_target_pairs={{0,8},{4,12},{8,0},{12,4},{16,24},{20,28},{24,16},{28,20},{1,9},{5... | collective-permute-start | bytes 1769480 | tf_op jit(solution)/shard_map/ppermute | solution.py:565
  86.4 24.4 %collective-permute-start.20 = (bf16[2,2,48,1536]{3,2,1,0:T(8,128)(2,1)S(1)}, bf16[2,2,48,1536]{3,2,1,0:T(8,128)(2,1)S(1)}, u32[]{:S(2)}, u32[]{:S(2)}) collective-permute-start(bf16[2,2,48,1536]{3,2,1,0:T(8,128)(2,1)S(1)} %pad_maximum_fusion.24), channel_id=1, source_target_pairs={{0,16},{4,20},{8,24},{12,28},{16,0},{20,4},{24,8},{28,12},{1,17},{... | collective-permute-start | bytes 1769480 | tf_op jit(solution)/shard_map/ppermute | solution.py:565
  110.8 52.4 %collective-permute-start.26 = (bf16[2,192,1536]{2,1,0:T(8,128)(2,1)}, bf16[2,192,1536]{2,1,0:T(8,128)(2,1)}, u32[]{:S(2)}, u32[]{:S(2)}) collective-permute-start(bf16[2,192,1536]{2,1,0:T(8,128)(2,1)} %pad_maximum_fusion.8), channel_id=1, source_target_pairs={{0,8},{4,12},{8,0},{12,4},{16,24},{20,28},{24,16},{28,20},{1,9},{5... | collective-permute-start | bytes 3538952 | tf_op jit(solution)/shard_map/ppermute | solution.py:565
  112.8 27.6 %collective-permute-start.28 = (bf16[4,2,48,1536]{3,2,1,0:T(8,128)(2,1)}, bf16[4,2,48,1536]{3,2,1,0:T(8,128)(2,1)}, u32[]{:S(2)}, u32[]{:S(2)}) collective-permute-start(bf16[4,2,48,1536]{3,2,1,0:T(8,128)(2,1)} %pad_maximum_fusion.10.refs_2_), channel_id=1, source_target_pairs={{0,4},{4,0},{8,12},{12,8},{16,20},{20,16},{24,28},{28,24},{1,5},{5... | collective-permute-start | bytes 3538952 | tf_op jit(solution)/shard_map/ppermute | solution.py:565
  113.9 26.5 %collective-permute-start.27 = (bf16[4,2,48,1536]{3,2,1,0:T(8,128)(2,1)}, bf16[4,2,48,1536]{3,2,1,0:T(8,128)(2,1)}, u32[]{:S(2)}, u32[]{:S(2)}) collective-permute-start(bf16[4,2,48,1536]{3,2,1,0:T(8,128)(2,1)} %pad_maximum_fusion.9.refs_0_), channel_id=1, source_target_pairs={{0,4},{4,0},{8,12},{12,8},{16,20},{20,16},{24,28},{28,24},{1,5},{5... | collective-permute-start | bytes 3538952 | tf_op jit(solution)/shard_map/ppermute | solution.py:565
  115.6 47.6 %collective-permute-start.25 = (bf16[2,192,1536]{2,1,0:T(8,128)(2,1)}, bf16[2,192,1536]{2,1,0:T(8,128)(2,1)}, u32[]{:S(2)}, u32[]{:S(2)}) collective-permute-start(bf16[2,192,1536]{2,1,0:T(8,128)(2,1)} %pad_maximum_fusion.7), channel_id=1, source_target_pairs={{0,16},{4,20},{8,24},{12,28},{16,0},{20,4},{24,8},{28,12},{1,17},{... | collective-permute-start | bytes 3538952 | tf_op jit(solution)/shard_map/ppermute | solution.py:565
  116.2 47.0 %collective-permute-start.24 = (bf16[256,1536]{1,0:T(8,128)(2,1)}, bf16[256,1536]{1,0:T(8,128)(2,1)}, u32[]{:S(2)}, u32[]{:S(2)}) collective-permute-start(bf16[256,1536]{1,0:T(8,128)(2,1)} %bitcast.30.z_ref.refs_4_), channel_id=1, source_target_pairs={{0,2},{1,3},{2,0},{3,1},{4,6},{5,7},{6,4},{7,5},{8,10},{9,11},{10,... | collective-permute-start | bytes 2359304 | tf_op jit(solution)/shard_map/ppermute | solution.py:565
  163.2 19.6 %collective-permute-start.29 = (bf16[256,1536]{1,0:T(8,128)(2,1)}, bf16[256,1536]{1,0:T(8,128)(2,1)}, u32[]{:S(2)}, u32[]{:S(2)}) collective-permute-start(bf16[256,1536]{1,0:T(8,128)(2,1)} %bitcast.30.z_ref.refs_4_), channel_id=1, source_target_pairs={{0,1},{1,0},{2,3},{3,2},{4,5},{5,4},{6,7},{7,6},{8,9},{9,8},{10,11... | collective-permute-start | bytes 2359304 | tf_op jit(solution)/shard_map/ppermute | solution.py:565
  163.2 19.6 %collective-permute-start.30 = (bf16[256,1536]{1,0:T(8,128)(2,1)}, bf16[256,1536]{1,0:T(8,128)(2,1)}, u32[]{:S(2)}, u32[]{:S(2)}) collective-permute-start(bf16[256,1536]{1,0:T(8,128)(2,1)} %bitcast.30.z_ref.refs_4_), channel_id=1, source_target_pairs={{1,2},{2,1},{5,6},{6,5},{9,10},{10,9},{13,14},{14,13},{17,18},{18,... | collective-permute-start | bytes 2359304 | tf_op jit(solution)/shard_map/ppermute | solution.py:565
  182.8 22.6 %collective-permute-start.33 = (bf16[272,1536]{1,0:T(8,128)(2,1)S(1)}, bf16[272,1536]{1,0:T(8,128)(2,1)S(1)}, u32[]{:S(2)}, u32[]{:S(2)}) collective-permute-start(bf16[272,1536]{1,0:T(8,128)(2,1)S(1)} %maximum_maximum_fusion.h_ref.refs_8_), channel_id=1, source_target_pairs={{0,1},{1,0},{2,3},{3,2},{4,5},{5,4},{6,7},{7,6},{8,9},{9,8},{10,11... | collective-permute-start | bytes 2506760 | tf_op jit(solution)/shard_map/ppermute | solution.py:565
  186.4 19.0 %collective-permute-start.34 = (bf16[272,1536]{1,0:T(8,128)(2,1)S(1)}, bf16[272,1536]{1,0:T(8,128)(2,1)S(1)}, u32[]{:S(2)}, u32[]{:S(2)}) collective-permute-start(bf16[272,1536]{1,0:T(8,128)(2,1)S(1)} %maximum_maximum_fusion.h_ref.refs_8_), channel_id=1, source_target_pairs={{1,2},{2,1},{5,6},{6,5},{9,10},{10,9},{13,14},{14,13},{17,18},{18,... | collective-permute-start | bytes 2506760 | tf_op jit(solution)/shard_map/ppermute | solution.py:565
  205.5 39.0 %collective-permute-start.35 = (bf16[272,1536]{1,0:T(8,128)(2,1)S(1)}, bf16[272,1536]{1,0:T(8,128)(2,1)}, u32[]{:S(2)}, u32[]{:S(2)}) collective-permute-start(bf16[272,1536]{1,0:T(8,128)(2,1)S(1)} %maximum_maximum_fusion.h_ref.refs_8_), channel_id=1, source_target_pairs={{0,2},{1,3},{2,0},{3,1},{4,6},{5,7},{6,4},{7,5},{8,10},{9,11},{10,... | collective-permute-start | bytes 2506760 | tf_op jit(solution)/shard_map/ppermute | solution.py:565
  208.2 36.2 %collective-permute-start.36 = (bf16[256,1536]{1,0:T(8,128)(2,1)}, bf16[256,1536]{1,0:T(8,128)(2,1)S(1)}, u32[]{:S(2)}, u32[]{:S(2)}) collective-permute-start(bf16[256,1536]{1,0:T(8,128)(2,1)} %collective-permute-done.24.z_ref.refs_6_), channel_id=1, source_target_pairs={{1,0},{2,3},{5,4},{6,7},{9,8},{10,11},{13,12},{14,15},{17,16},{18,... | collective-permute-start | bytes 2359304 | tf_op jit(solution)/shard_map/ppermute | solution.py:565
  245.3 20.9 %collective-permute-start.37 = (bf16[272,1536]{1,0:T(8,128)(2,1)}, bf16[272,1536]{1,0:T(8,128)(2,1)}, u32[]{:S(2)}, u32[]{:S(2)}) collective-permute-start(bf16[272,1536]{1,0:T(8,128)(2,1)} %collective-permute-done.35.h_ref.refs_10_), channel_id=1, source_target_pairs={{1,0},{2,3},{5,4},{6,7},{9,8},{10,11},{13,12},{14,15},{17,16},{18,... | collective-permute-start | bytes 2506760 | tf_op jit(solution)/shard_map/ppermute | solution.py:565
  266.2 18.5 %collective-permute-start.38 = (bf16[272,1536]{1,0:T(8,128)(2,1)S(1)}, bf16[272,1536]{1,0:T(8,128)(2,1)S(1)}, u32[]{:S(2)}, u32[]{:S(2)}) collective-permute-start(bf16[272,1536]{1,0:T(8,128)(2,1)S(1)} %copy-done.48), channel_id=1, source_target_pairs={{0,1},{1,0},{2,3},{3,2},{4,5},{5,4},{6,7},{7,6},{8,9},{9,8},{10,11... | collective-permute-start | bytes 2506760 | tf_op jit(solution)/shard_map/ppermute | solution.py:565
  295.0 22.1 %collective-permute-start.39 = (bf16[272,1536]{1,0:T(8,128)(2,1)S(1)}, bf16[272,1536]{1,0:T(8,128)(2,1)}, u32[]{:S(2)}, u32[]{:S(2)}) collective-permute-start(bf16[272,1536]{1,0:T(8,128)(2,1)S(1)} %get-tuple-element.211), channel_id=1, source_target_pairs={{0,1},{3,2},{4,5},{7,6},{8,9},{11,10},{12,13},{15,14},{16,17},{19,... | collective-permute-start | bytes 2506760 | tf_op jit(solution)/shard_map/ppermute | solution.py:565
  299.5 17.6 %collective-permute-start.40 = (bf16[272,1536]{1,0:T(8,128)(2,1)S(1)}, bf16[272,1536]{1,0:T(8,128)(2,1)}, u32[]{:S(2)}, u32[]{:S(2)}) collective-permute-start(bf16[272,1536]{1,0:T(8,128)(2,1)S(1)} %get-tuple-element.211), channel_id=1, source_target_pairs={{1,2},{2,1},{5,6},{6,5},{9,10},{10,9},{13,14},{14,13},{17,18},{18,... | collective-permute-start | bytes 2506760 | tf_op jit(solution)/shard_map/ppermute | solution.py:565
  317.1 27.9 %collective-permute-start.44 = (bf16[2,192,1536]{2,1,0:T(8,128)(2,1)}, bf16[2,192,1536]{2,1,0:T(8,128)(2,1)}, u32[]{:S(2)}, u32[]{:S(2)}) collective-permute-start(bf16[2,192,1536]{2,1,0:T(8,128)(2,1)} %pad_maximum_fusion.12), channel_id=1, source_target_pairs={{0,8},{4,12},{8,0},{12,4},{16,24},{20,28},{24,16},{28,20},{1,9},{5... | collective-permute-start | bytes 3538952 | tf_op jit(solution)/shard_map/ppermute | solution.py:565
  318.5 27.6 %collective-permute-start.43 = (bf16[2,192,1536]{2,1,0:T(8,128)(2,1)}, bf16[2,192,1536]{2,1,0:T(8,128)(2,1)}, u32[]{:S(2)}, u32[]{:S(2)}) collective-permute-start(bf16[2,192,1536]{2,1,0:T(8,128)(2,1)} %pad_maximum_fusion.11), channel_id=1, source_target_pairs={{0,16},{4,20},{8,24},{12,28},{16,0},{20,4},{24,8},{28,12},{1,17},{... | collective-permute-start | bytes 3538952 | tf_op jit(solution)/shard_map/ppermute | solution.py:565
  321.2 40.1 %collective-permute-start.42 = (bf16[272,1536]{1,0:T(8,128)(2,1)}, bf16[272,1536]{1,0:T(8,128)(2,1)}, u32[]{:S(2)}, u32[]{:S(2)}) collective-permute-start(bf16[272,1536]{1,0:T(8,128)(2,1)} %add_convert_fusion), channel_id=1, source_target_pairs={{0,2},{1,3},{2,0},{3,1},{4,6},{5,7},{6,4},{7,5},{8,10},{9,11},{10,... | collective-permute-start | bytes 2506760 | tf_op jit(solution)/shard_map/ppermute | solution.py:565
  369.8 40.0 %collective-permute-start.47 = (bf16[256,1536]{1,0:T(8,128)(2,1)}, bf16[256,1536]{1,0:T(8,128)(2,1)S(1)}, u32[]{:S(2)}, u32[]{:S(2)}) collective-permute-start(bf16[256,1536]{1,0:T(8,128)(2,1)} %copy-done.51), channel_id=1, source_target_pairs={{0,1},{1,0},{2,3},{3,2},{4,5},{5,4},{6,7},{7,6},{8,9},{9,8},{10,11... | collective-permute-start | bytes 2359304 | tf_op jit(solution)/shard_map/ppermute | solution.py:565
  376.3 33.4 %collective-permute-start.50 = (bf16[384,384]{1,0:T(8,128)(2,1)S(1)}, bf16[384,384]{1,0:T(8,128)(2,1)S(1)}, u32[]{:S(2)}, u32[]{:S(2)}) collective-permute-start(bf16[384,384]{1,0:T(8,128)(2,1)S(1)} %get-tuple-element.239), channel_id=1, source_target_pairs={{0,3},{1,2},{2,1},{3,0},{4,7},{5,6},{6,5},{7,4},{8,11},{9,10},{10,... | collective-permute-start | bytes 884744 | tf_op jit(solution)/shard_map/ppermute | solution.py:565
  378.0 31.8 %collective-permute-start.49 = (bf16[384,384]{1,0:T(8,128)(2,1)S(1)}, bf16[384,384]{1,0:T(8,128)(2,1)S(1)}, u32[]{:S(2)}, u32[]{:S(2)}) collective-permute-start(bf16[384,384]{1,0:T(8,128)(2,1)S(1)} %get-tuple-element.238), channel_id=1, source_target_pairs={{0,2},{1,3},{2,0},{3,1},{4,6},{5,7},{6,4},{7,5},{8,10},{9,11},{10,... | collective-permute-start | bytes 884744 | tf_op jit(solution)/shard_map/ppermute | solution.py:565
  378.0 31.8 %collective-permute-start.48 = (bf16[384,384]{1,0:T(8,128)(2,1)S(1)}, bf16[384,384]{1,0:T(8,128)(2,1)S(1)}, u32[]{:S(2)}, u32[]{:S(2)}) collective-permute-start(bf16[384,384]{1,0:T(8,128)(2,1)S(1)} %get-tuple-element.237), channel_id=1, source_target_pairs={{0,1},{1,0},{2,3},{3,2},{4,5},{5,4},{6,7},{7,6},{8,9},{9,8},{10,11... | collective-permute-start | bytes 884744 | tf_op jit(solution)/shard_map/ppermute | solution.py:565
  411.4 25.7 %collective-permute-start.55 = (bf16[1,384,768]{2,1,0:T(8,128)(2,1)S(1)}, bf16[1,384,768]{2,1,0:T(8,128)(2,1)S(1)}, u32[]{:S(2)}, u32[]{:S(2)}) collective-permute-start(bf16[1,384,768]{2,1,0:T(8,128)(2,1)S(1)} %get-tuple-element.248), channel_id=1, source_target_pairs={{0,16},{4,20},{8,24},{12,28},{16,0},{20,4},{24,8},{28,12},{1,17},{... | collective-permute-start | bytes 1769480 | tf_op jit(solution)/shard_map/ppermute | solution.py:565
  412.9 24.2 %collective-permute-start.54 = (bf16[1,384,768]{2,1,0:T(8,128)(2,1)S(1)}, bf16[1,384,768]{2,1,0:T(8,128)(2,1)S(1)}, u32[]{:S(2)}, u32[]{:S(2)}) collective-permute-start(bf16[1,384,768]{2,1,0:T(8,128)(2,1)S(1)} %get-tuple-element.247), channel_id=1, source_target_pairs={{0,8},{4,12},{8,0},{12,4},{16,24},{20,28},{24,16},{28,20},{1,9},{5... | collective-permute-start | bytes 1769480 | tf_op jit(solution)/shard_map/ppermute | solution.py:565
  415.9 20.9 %collective-permute-start.52 = (bf16[2,256,256]{2,1,0:T(8,128)(2,1)S(1)}, bf16[2,256,256]{2,1,0:T(8,128)(2,1)S(1)}, u32[]{:S(2)}, u32[]{:S(2)}) collective-permute-start(bf16[2,256,256]{2,1,0:T(8,128)(2,1)S(1)} %get-tuple-element.241), channel_id=1, source_target_pairs={{2,0},{3,1},{6,4},{7,5},{10,8},{11,9},{14,12},{15,13},{18,16},{19,... | collective-permute-start | bytes 786440 | tf_op jit(solution)/shard_map/ppermute | solution.py:565
  417.2 19.6 %collective-permute-start.51 = (bf16[2,256,256]{2,1,0:T(8,128)(2,1)S(1)}, bf16[2,256,256]{2,1,0:T(8,128)(2,1)S(1)}, u32[]{:S(2)}, u32[]{:S(2)}) collective-permute-start(bf16[2,256,256]{2,1,0:T(8,128)(2,1)S(1)} %get-tuple-element.240), channel_id=1, source_target_pairs={{1,0},{3,2},{5,4},{7,6},{9,8},{11,10},{13,12},{15,14},{17,16},{19,... | collective-permute-start | bytes 786440 | tf_op jit(solution)/shard_map/ppermute | solution.py:565
  452.1 31.0 %collective-permute-start.58 = (bf16[4,1536,256]{2,1,0:T(8,128)(2,1)S(1)}, bf16[4,1536,256]{2,1,0:T(8,128)(2,1)S(1)}, u32[]{:S(2)}, u32[]{:S(2)}) collective-permute-start(bf16[4,1536,256]{2,1,0:T(8,128)(2,1)S(1)} %get-tuple-element.254), channel_id=1, source_target_pairs={{0,4},{4,0},{8,12},{12,8},{16,20},{20,16},{24,28},{28,24},{1,5},{5... | collective-permute-start | bytes 9437192 | tf_op jit(solution)/shard_map/ppermute | solution.py:565
  452.3 28.4 %collective-permute-start.59 = (bf16[2,384,768]{2,1,0:T(8,128)(2,1)S(1)}, bf16[2,384,768]{2,1,0:T(8,128)(2,1)S(1)}, u32[]{:S(2)}, u32[]{:S(2)}) collective-permute-start(bf16[2,384,768]{2,1,0:T(8,128)(2,1)S(1)} %pad_maximum_fusion.13), channel_id=1, source_target_pairs={{0,16},{4,20},{8,24},{12,28},{16,0},{20,4},{24,8},{28,12},{1,17},{... | collective-permute-start | bytes 3538952 | tf_op jit(solution)/shard_map/ppermute | solution.py:565
  454.3 27.0 %collective-permute-start.60 = (bf16[2,384,768]{2,1,0:T(8,128)(2,1)S(1)}, bf16[2,384,768]{2,1,0:T(8,128)(2,1)S(1)}, u32[]{:S(2)}, u32[]{:S(2)}) collective-permute-start(bf16[2,384,768]{2,1,0:T(8,128)(2,1)S(1)} %pad_maximum_fusion.14), channel_id=1, source_target_pairs={{0,8},{4,12},{8,0},{12,4},{16,24},{20,28},{24,16},{28,20},{1,9},{5... | collective-permute-start | bytes 3538952 | tf_op jit(solution)/shard_map/ppermute | solution.py:565
  455.1 28.0 %collective-permute-start.56 = (bf16[256,1536]{1,0:T(8,128)(2,1)S(1)}, bf16[256,1536]{1,0:T(8,128)(2,1)S(1)}, u32[]{:S(2)}, u32[]{:S(2)}) collective-permute-start(bf16[256,1536]{1,0:T(8,128)(2,1)S(1)} %copy-done.50), channel_id=1, source_target_pairs={{1,2},{2,1},{5,6},{6,5},{9,10},{10,9},{13,14},{14,13},{17,18},{18,... | collective-permute-start | bytes 2359304 | tf_op jit(solution)/shard_map/ppermute | solution.py:565
  455.8 27.3 %collective-permute-start.57 = (bf16[256,1536]{1,0:T(8,128)(2,1)S(1)}, bf16[256,1536]{1,0:T(8,128)(2,1)S(1)}, u32[]{:S(2)}, u32[]{:S(2)}) collective-permute-start(bf16[256,1536]{1,0:T(8,128)(2,1)S(1)} %copy-done.50), channel_id=1, source_target_pairs={{0,1},{3,2},{4,5},{7,6},{8,9},{11,10},{12,13},{15,14},{16,17},{19,... | collective-permute-start | bytes 2359304 | tf_op jit(solution)/shard_map/ppermute | solution.py:565
  483.1 29.8 %collective-permute-start.64 = (bf16[4,384,768]{2,1,0:T(8,128)(2,1)}, bf16[4,384,768]{2,1,0:T(8,128)(2,1)}, u32[]{:S(2)}, u32[]{:S(2)}) collective-permute-start(bf16[4,384,768]{2,1,0:T(8,128)(2,1)} %pad_maximum_fusion.3.refs_0_), channel_id=1, source_target_pairs={{0,4},{4,0},{8,12},{12,8},{16,20},{20,16},{24,28},{28,24},{1,5},{5... | collective-permute-start | bytes 7077896 | tf_op jit(solution)/shard_map/ppermute | solution.py:565
  483.2 29.7 %collective-permute-start.63 = (bf16[4,384,768]{2,1,0:T(8,128)(2,1)S(1)}, bf16[4,384,768]{2,1,0:T(8,128)(2,1)}, u32[]{:S(2)}, u32[]{:S(2)}) collective-permute-start(bf16[4,384,768]{2,1,0:T(8,128)(2,1)S(1)} %pad_maximum_fusion.2.refs_0_), channel_id=1, source_target_pairs={{0,4},{4,0},{8,12},{12,8},{16,20},{20,16},{24,28},{28,24},{1,5},{5... | collective-permute-start | bytes 7077896 | tf_op jit(solution)/shard_map/ppermute | solution.py:565
  486.2 19.1 %collective-permute-start.62 = (bf16[2,768,256]{2,1,0:T(8,128)(2,1)}, bf16[2,768,256]{2,1,0:T(8,128)(2,1)}, u32[]{:S(2)}, u32[]{:S(2)}) collective-permute-start(bf16[2,768,256]{2,1,0:T(8,128)(2,1)} %pad_maximum_fusion.20), channel_id=1, source_target_pairs={{0,8},{4,12},{8,0},{12,4},{16,24},{20,28},{24,16},{28,20},{1,9},{5... | collective-permute-start | bytes 2359304 | tf_op jit(solution)/shard_map/ppermute | solution.py:565
  488.5 20.5 %collective-permute-start.61 = (bf16[2,768,256]{2,1,0:T(8,128)(2,1)}, bf16[2,768,256]{2,1,0:T(8,128)(2,1)}, u32[]{:S(2)}, u32[]{:S(2)}) collective-permute-start(bf16[2,768,256]{2,1,0:T(8,128)(2,1)} %pad_maximum_fusion.19), channel_id=1, source_target_pairs={{0,16},{4,20},{8,24},{12,28},{16,0},{20,4},{24,8},{28,12},{1,17},{... | collective-permute-start | bytes 2359304 | tf_op jit(solution)/shard_map/ppermute | solution.py:565
  489.2 21.8 %all-to-all-start = ((bf16[4,48,1536]{2,1,0:T(8,128)(2,1)}), bf16[4,48,1536]{2,1,0:T(8,128)(2,1)}, u32[]{:S(2)}, u32[]{:S(2)}) async-start(bf16[4,48,1536]{2,1,0:T(8,128)(2,1)} %bitcast.164), calls=%async_computation.1 | async-start | bytes 1179648 | tf_op jit(solution)/shard_map/all_to_all | solution.py:891
  493.4 107.7 %all-reduce.4.cloned.1.call-start = ((), (), s32[]{:S(2)}) async-start(), calls=%async_computation.4 | async-start | bytes 9437184 | tf_op jit(solution)/shard_map/psum | solution.py:872
  495.8 129.0 %all-gather.2.cloned.1.call-start = ((), (), s32[]{:S(2)}) async-start(), calls=%async_computation.3 | async-start | bytes 1327104 | tf_op jit(solution)/shard_map/all_gather | solution.py:902
  512.9 20.6 %collective-permute-start.68 = (bf16[1,768,256]{2,1,0:T(8,128)(2,1)S(1)}, bf16[1,768,256]{2,1,0:T(8,128)(2,1)S(1)}, u32[]{:S(2)}, u32[]{:S(2)}) collective-permute-start(bf16[1,768,256]{2,1,0:T(8,128)(2,1)S(1)} %get-tuple-element.267), channel_id=1, source_target_pairs={{0,16},{4,20},{8,24},{12,28},{16,0},{20,4},{24,8},{28,12},{1,17},{... | collective-permute-start | bytes 1179656 | tf_op jit(solution)/shard_map/ppermute | solution.py:565
  515.4 18.1 %collective-permute-start.67 = (bf16[1,768,256]{2,1,0:T(8,128)(2,1)S(1)}, bf16[1,768,256]{2,1,0:T(8,128)(2,1)S(1)}, u32[]{:S(2)}, u32[]{:S(2)}) collective-permute-start(bf16[1,768,256]{2,1,0:T(8,128)(2,1)S(1)} %get-tuple-element.266), channel_id=1, source_target_pairs={{0,8},{4,12},{8,0},{12,4},{16,24},{20,28},{24,16},{28,20},{1,9},{5... | collective-permute-start | bytes 1179656 | tf_op jit(solution)/shard_map/ppermute | solution.py:565
  515.4 20.3 %collective-permute-start.66 = (f32[10,1536]{1,0:T(8,128)S(1)}, f32[10,1536]{1,0:T(8,128)S(1)}, u32[]{:S(2)}, u32[]{:S(2)}) collective-permute-start(f32[10,1536]{1,0:T(8,128)S(1)} %pad_maximum_fusion.32), channel_id=1, source_target_pairs={{0,4},{4,0},{8,12},{12,8},{16,20},{20,16},{24,28},{28,24},{1,5},{5... | collective-permute-start | bytes 184328 | tf_op jit(solution)/shard_map/ppermute | solution.py:565
  562.8 35.0 %collective-permute-start.65 = (bf16[256,1536]{1,0:T(8,128)(2,1)S(1)}, bf16[256,1536]{1,0:T(8,128)(2,1)S(1)}, u32[]{:S(2)}, u32[]{:S(2)}) collective-permute-start(bf16[256,1536]{1,0:T(8,128)(2,1)S(1)} %add_convert_fusion.2), channel_id=1, source_target_pairs={{0,2},{1,3},{2,0},{3,1},{4,6},{5,7},{6,4},{7,5},{8,10},{9,11},{10,... | collective-permute-start | bytes 2359304 | tf_op jit(solution)/shard_map/ppermute | solution.py:901
  579.7 28.8 %collective-permute-start.78 = (bf16[4,384,256]{2,1,0:T(8,128)(2,1)S(1)}, bf16[4,384,256]{2,1,0:T(8,128)(2,1)S(1)}, u32[]{:S(2)}, u32[]{:S(2)}) collective-permute-start(bf16[4,384,256]{2,1,0:T(8,128)(2,1)S(1)} %pad_maximum_fusion.22.near_ref), channel_id=1, source_target_pairs={{0,4},{4,0},{8,12},{12,8},{16,20},{20,16},{24,28},{28,24},{1,5},{5... | collective-permute-start | bytes 2359304 | tf_op jit(solution)/shard_map/ppermute | solution.py:565
  581.1 18.7 %collective-permute-start.77 = (f32[10,1536]{1,0:T(8,128)S(1)}, f32[10,1536]{1,0:T(8,128)S(1)}, u32[]{:S(2)}, u32[]{:S(2)}) collective-permute-start(f32[10,1536]{1,0:T(8,128)S(1)} %add.349), channel_id=1, source_target_pairs={{0,2},{1,3},{2,0},{3,1},{4,6},{5,7},{6,4},{7,5},{8,10},{9,11},{10,... | collective-permute-start | bytes 184328 | tf_op jit(solution)/shard_map/ppermute | solution.py:565
  (142 other events, 1445.0 us)
Sparse Core Ops, SparseCore 0:
  369.9 58.7 reduce-scatter.1
  497.9 100.8 all-reduce.3
  600.6 24.1 all-gather.1

commit v4 on v3

--- a/solution.py
+++ b/solution.py
@@ -856,11 +856,11 @@
     branch = middle_grad.astype(bf16)
 
     dob = dot_nt(branch, full_out).astype(bf16)
-    out_grads = jnp.swapaxes(dot_tn(ob, branch).astype(bf16).reshape(n, m, rc, d), 0, 1).reshape(m * n * rc, d)
-    out_grads = lax.psum_scatter(out_grads, "dp", scatter_dimension=0, tiled=True)
     dq, dkv = attend_back(rank, qkv, kv, dob, cos, sin)
     rounds.leave(dkv)
     rounds.turn()
+    out_grads = jnp.swapaxes(dot_tn(ob, rounds.enter(branch)).astype(bf16).reshape(n, m, rc, d), 0, 1).reshape(m * n * rc, d)
+    out_grads = lax.psum_scatter(out_grads, "dp", scatter_dimension=0, tiled=True)
     dkv_own = dkv[:, :t].astype(f32)
     for s in range(1, n):
         dkv_own = dkv_own + along.cross(dkv[:, s * t : (s + 1) * t], s, down).astype(f32)

time: 645 us -> 659 us (1.022)
  other arithmetic: 63.4 us -> 75 us
    ppermute x78, waiting for transfers between devices: 197 us -> 214 us  [send(): return leave(lax.ppermute(self.rounds.enter(x), axis, pairs))]
    all_gather x1, waiting for transfers between devices: 12.2 us -> 0.01 us  [local(): lax.all_gather(rounds.enter(out_grads), 'dp', axis=0, tiled=True)]
    ppermute x1, waiting for transfers between devices: 14.9 us -> 7.41 us  [local(): lax.ppermute(second_out, 'cp', [(k, k ^ 2) for k in range(n)]).astype(f32)]
    unnamed x216 -> x258, local copies, waits for them, and re-layouts: 28 us -> 29.4 us
  transfers between devices with their start and end apart: 83 -> 83, of which waited for: 36 -> 35; matrix products, arithmetic and copies ran while one was open for 12% -> 14% of each run, Pallas kernels for 24% -> 24%
where the time goes in v4:
time: 659 us; the launch traced here: 649 us
  waiting for transfers between devices  222 us (34%)
  Pallas kernels  163 us (25%)
  starting transfers between devices  122 us (19%)
  other arithmetic  75 us (11%)
  local copies, waits for them, and re-layouts  44.3 us (7%)
  between operations  15.9 us (2%)
  matrix products  8.06 us (1%)
    ppermute x78, waiting for transfers between devices, send(): return leave(lax.ppermute(self.rounds.enter(x), axis, pairs))  214 us
    ppermute x78, starting transfers between devices, send(): return leave(lax.ppermute(self.rounds.enter(x), axis, pairs))  117 us
    pallas_call x4, Pallas kernels, experts(): pl.pallas_call(experts_kernel, in_specs=[pl.BlockSpec(memory_space=pltpu....  54.2 us
    pallas_call x4, Pallas kernels, expert_grads(): pl.pallas_call(functools.partial(expert_grads_kernel, n, fc, pairs), grid...  31.3 us
    unnamed x258, local copies, waits for them, and re-layouts  29.4 us
    pallas_call x4, Pallas kernels, join(): pl.pallas_call(functools.partial(join_kernel, half), grid_spec=pltpu.Pref...  25.3 us
    pallas_call x1, Pallas kernels, attend_back(): pl.pallas_call(attend_back_kernel, grid_spec=pltpu.PrefetchScalarGridSpec...  23.9 us
  transfers between devices with their start and end apart: 83, of which 35 were waited for; matrix products, arithmetic and copies ran while one was open for 14% of the time, Pallas kernels for 24%

profile of v4, /device:TPU:0, one launch (start us, length us, event | category | flops | bytes accessed | tf_op | source)
XLA Modules:
  0.0 649.5 jit_solution(16818385905988193568)
XLA Ops:
  10.4 5.1 collective-permute-start
  23.0 10.0 %collective-permute-done.1 = bf16[400,256]{1,0:T(8,128)(2,1)S(1)} collective-permute-done((bf16[400,256]{1,0:T(8,128)(2,1)S(1)}, bf16[400,256]{1,0:T(8,128)(2,1)S(1)}, u32[]{:S(2)}, u32[]{:S(2)}) %collective-permute-start.1) | collective-permute-done | bytes 204832 | tf_op jit(solution)/shard_map/ppermute | solution.py:565
  42.7 5.3 collective-permute-done.4
  55.7 10.5 %collective-permute-done.9 = bf16[2,768,256]{2,1,0:T(8,128)(2,1)S(1)} collective-permute-done((bf16[2,768,256]{2,1,0:T(8,128)(2,1)S(1)}, bf16[2,768,256]{2,1,0:T(8,128)(2,1)S(1)}, u32[]{:S(2)}, u32[]{:S(2)}) %collective-permute-start.9) | collective-permute-done | bytes 786464 | tf_op jit(solution)/shard_map/ppermute | solution.py:565
  74.3 4.5 project.1.q_ref
  87.0 4.3 collective-permute-start.17
  91.3 4.3 collective-permute-done.17
  98.9 4.0 collective-permute-start.19
  115.9 12.8 %collective-permute-start.24 = (bf16[256,1536]{1,0:T(8,128)(2,1)S(1)}, bf16[256,1536]{1,0:T(8,128)(2,1)}, u32[]{:S(2)}, u32[]{:S(2)}) collective-permute-start(bf16[256,1536]{1,0:T(8,128)(2,1)S(1)} %bitcast.143), channel_id=1, source_target_pairs={{0,2},{1,3},{2,0},{3,1},{4,6},{5,7},{6,4},{7,5},{8,10},{9,11},{10,... | collective-permute-start | bytes 2359304 | tf_op jit(solution)/shard_map/ppermute | solution.py:565
  130.7 10.3 %attend.1 = bf16[256,1536]{1,0:T(8,128)(2,1)S(1)} custom-call(s32[1]{0:T(128)} %bitcast.1.rank_ref, bf16[256,2048]{1,0:T(8,128)(2,1)S(1)} %project.1.q_ref, bf16[1024,512]{1,0:T(8,128)(2,1)S(1)} %pad_maximum_fusion.15.k_ref.v_ref, bf16[1024,512]{1,0:T(8,128)(2,1)S(1)} %pad_maximum_fusion.15.k_ref.v_ref), custom_call_target="tpu_custom_call" | custom-call | flops 16106 | bytes 15 | tf_op jit(solution)/shard_map/attend/pallas_call | solution.py:165
  141.0 6.2 join.4
  147.3 15.9 %collective-permute-done.24.z_ref.refs_6_ = bf16[256,1536]{1,0:T(8,128)(2,1)} collective-permute-done((bf16[256,1536]{1,0:T(8,128)(2,1)S(1)}, bf16[256,1536]{1,0:T(8,128)(2,1)}, u32[]{:S(2)}, u32[]{:S(2)}) %collective-permute-start.24) | collective-permute-done | bytes 786464 | tf_op jit(solution)/shard_map/ppermute | solution.py:565
  177.3 5.3 collective-permute-done.29.z_ref.refs_5_
  182.6 3.6 collective-permute-start.33
  186.9 13.5 %experts.4 = (bf16[256,1536]{1,0:T(8,128)(2,1)S(1)}, bf16[256,1536]{1,0:T(8,128)(2,1)S(1)}, bf16[256,1536]{1,0:T(8,128)(2,1)S(1)}, f32[256,1536]{1,0:T(8,128)S(1)}, f32[272,1536]{1,0:T(8,128)}) custom-call(s32[8]{0:T(128)S(1)} %fusion.51.chunk_ref, bf16[272,1536]{1,0:T(8,128)(2,1)S(1)} %maximum_maximum_fusion.h_ref.refs_8_, bf16[256,1536]{1,0:T(8,128)(2,1)S(1)} %bitcast.146, ...), custom_call_target="tpu_custom_call" | custom-call | flops 72477 | bytes 141 | tf_op jit(solution)/shard_map/experts/pallas_call | solution.py:319
  209.0 13.6 %experts.5 = (bf16[256,1536]{1,0:T(8,128)(2,1)S(1)}, bf16[256,1536]{1,0:T(8,128)(2,1)S(1)}, bf16[256,1536]{1,0:T(8,128)(2,1)S(1)}, bf16[256,1536]{1,0:T(8,128)(2,1)S(1)}, bf16[272,1536]{1,0:T(8,128)(2,1)S(1)}) custom-call(s32[8]{0:T(128)S(1)} %fusion.51.chunk_ref, bf16[272,1536]{1,0:T(8,128)(2,1)S(1)} %collective-permute-done.33.h_ref.refs_9_, ...), custom_call_target="tpu_custom_call" | custom-call | flops 72477 | bytes 141 | tf_op jit(solution)/shard_map/experts/pallas_call | solution.py:319
  227.1 16.2 %collective-permute-done.36 = bf16[256,1536]{1,0:T(8,128)(2,1)S(1)} collective-permute-done((bf16[256,1536]{1,0:T(8,128)(2,1)}, bf16[256,1536]{1,0:T(8,128)(2,1)S(1)}, u32[]{:S(2)}, u32[]{:S(2)}) %collective-permute-start.36) | collective-permute-done | bytes 786464 | tf_op jit(solution)/shard_map/ppermute | solution.py:565
  245.7 13.9 %experts.6 = (bf16[256,1536]{1,0:T(8,128)(2,1)S(1)}, bf16[256,1536]{1,0:T(8,128)(2,1)S(1)}, bf16[256,1536]{1,0:T(8,128)(2,1)S(1)}, bf16[256,1536]{1,0:T(8,128)(2,1)S(1)}, bf16[272,1536]{1,0:T(8,128)(2,1)S(1)}) custom-call(s32[8]{0:T(128)S(1)} %fusion.51.chunk_ref, bf16[272,1536]{1,0:T(8,128)(2,1)} %collective-permute-done.35.h_ref.refs_10_, ...), custom_call_target="tpu_custom_call" | custom-call | flops 72477 | bytes 141 | tf_op jit(solution)/shard_map/experts/pallas_call | solution.py:319
  260.5 4.5 collective-permute-done.37
  266.8 13.2 %experts.7 = (bf16[256,1536]{1,0:T(8,128)(2,1)S(1)}, bf16[256,1536]{1,0:T(8,128)(2,1)S(1)}, bf16[256,1536]{1,0:T(8,128)(2,1)S(1)}, bf16[256,1536]{1,0:T(8,128)(2,1)S(1)}, bf16[272,1536]{1,0:T(8,128)(2,1)S(1)}) custom-call(s32[8]{0:T(128)S(1)} %fusion.51.chunk_ref, bf16[272,1536]{1,0:T(8,128)(2,1)S(1)} %broadcast_select_fusion.h_ref.refs_11_, ...), custom_call_target="tpu_custom_call" | custom-call | flops 72477 | bytes 141 | tf_op jit(solution)/shard_map/experts/pallas_call | solution.py:319
  285.3 9.5 %expert_grads.4 = bf16[4,2,192,1536]{3,2,1,0:T(8,128)(2,1)} custom-call(bf16[256,1536]{1,0:T(8,128)(2,1)} %copy-done.28, bf16[256,1536]{1,0:T(8,128)(2,1)} %copy-done.30, bf16[256,1536]{1,0:T(8,128)(2,1)} %copy-done.32, bf16[256,1536]{1,0:T(8,128)(2,1)} %copy-done.34, bf16[256,1536]{1,0:T(8,128)(2,1)} %copy-done.29, bf16[256,1536]{1,0:T(8,128)(2,1)} %copy-done.31, ...), custom_call_target="tpu_custom_call" | custom-call | flops 48318 | bytes 47 | tf_op jit(solution)/shard_map/expert_grads/pallas_call | solution.py:370
  294.8 4.6 collective-permute-start.39
  301.4 9.4 %expert_grads.5 = bf16[4,2,192,1536]{3,2,1,0:T(8,128)(2,1)} custom-call(bf16[256,1536]{1,0:T(8,128)(2,1)} %copy-done.28, bf16[256,1536]{1,0:T(8,128)(2,1)} %copy-done.30, bf16[256,1536]{1,0:T(8,128)(2,1)} %copy-done.32, bf16[256,1536]{1,0:T(8,128)(2,1)} %copy-done.34, bf16[256,1536]{1,0:T(8,128)(2,1)} %copy-done.29, bf16[256,1536]{1,0:T(8,128)(2,1)} %copy-done.31, ...), custom_call_target="tpu_custom_call" | custom-call | flops 48318 | bytes 47 | tf_op jit(solution)/shard_map/expert_grads/pallas_call | solution.py:370
  321.9 4.0 collective-permute-start.42
  325.9 6.2 expert_grads.7
  332.0 6.3 expert_grads.6
  350.6 11.4 %collective-permute-done.42 = bf16[272,1536]{1,0:T(8,128)(2,1)} collective-permute-done((bf16[272,1536]{1,0:T(8,128)(2,1)}, bf16[272,1536]{1,0:T(8,128)(2,1)}, u32[]{:S(2)}, u32[]{:S(2)}) %collective-permute-start.42) | collective-permute-done | bytes 835616 | tf_op jit(solution)/shard_map/ppermute | solution.py:565
  363.8 3.2 collective-permute-start.47
  381.0 23.9 %attend_back.1 = (bf16[256,1536]{1,0:T(8,128)(2,1)}, bf16[2,1024,256]{2,1,0:T(8,128)(2,1)}) custom-call(s32[1]{0:T(128)} %bitcast.1.rank_ref, bf16[256,2048]{1,0:T(8,128)(2,1)} %copy-done.9, bf16[1024,512]{1,0:T(8,128)(2,1)} %copy-done, bf16[1024,512]{1,0:T(8,128)(2,1)} %copy-done, bf16[256,1536]{1,0:T(8,128)(2,1)} %convolution_convert_fusion.1.g_ref, ...), custom_call_target="tpu_custom_call" | custom-call | flops 40265 | bytes 31 | tf_op jit(solution)/shard_map/attend_back/pallas_call | solution.py:214
  416.2 6.8 %collective-permute-done.51 = bf16[2,256,256]{2,1,0:T(8,128)(2,1)S(1)} collective-permute-done((bf16[2,256,256]{2,1,0:T(8,128)(2,1)S(1)}, bf16[2,256,256]{2,1,0:T(8,128)(2,1)S(1)}, u32[]{:S(2)}, u32[]{:S(2)}) %collective-permute-start.51) | collective-permute-done | bytes 262176 | tf_op jit(solution)/shard_map/ppermute | solution.py:565
  423.0 11.3 %collective-permute-done.52 = bf16[2,256,256]{2,1,0:T(8,128)(2,1)S(1)} collective-permute-done((bf16[2,256,256]{2,1,0:T(8,128)(2,1)S(1)}, bf16[2,256,256]{2,1,0:T(8,128)(2,1)S(1)}, u32[]{:S(2)}, u32[]{:S(2)}) %collective-permute-start.52) | collective-permute-done | bytes 262176 | tf_op jit(solution)/shard_map/ppermute | solution.py:565
  442.5 6.0 project_back.1
  452.0 6.6 %collective-permute-start.57 = (bf16[256,1536]{1,0:T(8,128)(2,1)S(1)}, bf16[256,1536]{1,0:T(8,128)(2,1)S(1)}, u32[]{:S(2)}, u32[]{:S(2)}) collective-permute-start(bf16[256,1536]{1,0:T(8,128)(2,1)S(1)} %copy-done.54), channel_id=1, source_target_pairs={{0,1},{3,2},{4,5},{7,6},{8,9},{11,10},{12,13},{15,14},{16,17},{19,... | collective-permute-start | bytes 2359304 | tf_op jit(solution)/shard_map/ppermute | solution.py:565
  458.6 24.9 %collective-permute-done.59 = bf16[2,384,768]{2,1,0:T(8,128)(2,1)S(1)} collective-permute-done((bf16[2,384,768]{2,1,0:T(8,128)(2,1)S(1)}, bf16[2,384,768]{2,1,0:T(8,128)(2,1)S(1)}, u32[]{:S(2)}, u32[]{:S(2)}) %collective-permute-start.59) | collective-permute-done | bytes 1179680 | tf_op jit(solution)/shard_map/ppermute | solution.py:565
  495.0 4.7 all-to-all-start
  503.8 24.5 %collective-permute-done.62 = bf16[2,768,256]{2,1,0:T(8,128)(2,1)} collective-permute-done((bf16[2,768,256]{2,1,0:T(8,128)(2,1)}, bf16[2,768,256]{2,1,0:T(8,128)(2,1)}, u32[]{:S(2)}, u32[]{:S(2)}) %collective-permute-start.62) | collective-permute-done | bytes 786464 | tf_op jit(solution)/shard_map/ppermute | solution.py:565
  537.8 10.1 %join.7 = f32[8,384,768]{2,1,0:T(8,128)} custom-call(s32[8]{0:T(128)S(1)} %shift-left_or_fusion.slot_ref, bf16[4,384,768]{2,1,0:T(8,128)(2,1)} %pad_maximum_fusion.3.refs_0_, bf16[4,384,768]{2,1,0:T(8,128)(2,1)} %collective-permute-done.64.refs_1_), custom_call_target="tpu_custom_call" | custom-call | bytes 141 | tf_op jit(solution)/shard_map/join/pallas_call | solution.py:418
  547.9 8.0 %join.6 = f32[8,384,768]{2,1,0:T(8,128)} custom-call(s32[8]{0:T(128)S(1)} %shift-left_or_fusion.slot_ref, bf16[4,384,768]{2,1,0:T(8,128)(2,1)S(1)} %pad_maximum_fusion.2.refs_0_, bf16[4,384,768]{2,1,0:T(8,128)(2,1)} %collective-permute-done.63.refs_1_), custom_call_target="tpu_custom_call" | custom-call | bytes 141 | tf_op jit(solution)/shard_map/join/pallas_call | solution.py:418
  558.4 4.4 collective-permute-start.71
  564.8 3.2 collective-permute-done.72
  568.0 12.1 %collective-permute-done.71 = bf16[384,256]{1,0:T(8,128)(2,1)S(1)} collective-permute-done((bf16[384,256]{1,0:T(8,128)(2,1)S(1)}, bf16[384,256]{1,0:T(8,128)(2,1)S(1)}, u32[]{:S(2)}, u32[]{:S(2)}) %collective-permute-start.71) | collective-permute-done | bytes 196640 | tf_op jit(solution)/shard_map/ppermute | solution.py:565
  583.6 8.4 %collective-permute-done.74 = bf16[1,384,256]{2,1,0:T(8,128)(2,1)S(1)} collective-permute-done((bf16[1,384,256]{2,1,0:T(8,128)(2,1)S(1)}, bf16[1,384,256]{2,1,0:T(8,128)(2,1)S(1)}, u32[]{:S(2)}, u32[]{:S(2)}) %collective-permute-start.74) | collective-permute-done | bytes 196640 | tf_op jit(solution)/shard_map/ppermute | solution.py:565
  593.7 8.1 %collective-permute-done.75 = f32[10,1536]{1,0:T(8,128)S(1)} collective-permute-done((f32[10,1536]{1,0:T(8,128)S(1)}, f32[10,1536]{1,0:T(8,128)S(1)}, u32[]{:S(2)}, u32[]{:S(2)}) %collective-permute-start.75) | collective-permute-done | bytes 61472 | tf_op jit(solution)/shard_map/ppermute | solution.py:565
  601.8 6.6 %collective-permute-done.76 = bf16[2,384,256]{2,1,0:T(8,128)(2,1)} collective-permute-done((bf16[2,384,256]{2,1,0:T(8,128)(2,1)S(1)}, bf16[2,384,256]{2,1,0:T(8,128)(2,1)}, u32[]{:S(2)}, u32[]{:S(2)}) %collective-permute-start.76) | collective-permute-done | bytes 393248 | tf_op jit(solution)/shard_map/ppermute | solution.py:565
  612.1 7.4 %collective-permute-done.65 = bf16[256,1536]{1,0:T(8,128)(2,1)} collective-permute-done((bf16[256,1536]{1,0:T(8,128)(2,1)}, bf16[256,1536]{1,0:T(8,128)(2,1)}, u32[]{:S(2)}, u32[]{:S(2)}) %collective-permute-start.65) | collective-permute-done | bytes 786464 | tf_op jit(solution)/shard_map/ppermute | solution.py:901
  619.5 5.1 fusion.13
  625.9 7.5 %convert_element_type.483 = f32[8,192,1536]{2,1,0:T(8,128)} convert(bf16[8,192,1536]{2,1,0:T(8,128)(2,1)} %all-reduce.4.cloned.1.call-done) | non-fusion elementwise | flops 2359296 | bytes 14155776 | tf_op jit(solution)/shard_map/convert_element_type | solution.py:873
  633.5 6.3 columns.1
  (531 shorter events, 206.2 us)
Async XLA Ops:
  7.2 481.7 %reduce-scatter.2.cloned.1.call-start = ((), (), s32[]{:S(2)}) async-start(), calls=%async_computation.2 | async-start | bytes 5308416 | tf_op jit(solution)/shard_map/reduce_scatter | solution.py:863
  83.9 23.6 %collective-permute-start.22 = (bf16[1,192,1536]{2,1,0:T(8,128)(2,1)S(1)}, bf16[1,192,1536]{2,1,0:T(8,128)(2,1)S(1)}, u32[]{:S(2)}, u32[]{:S(2)}) collective-permute-start(bf16[1,192,1536]{2,1,0:T(8,128)(2,1)S(1)} %bitcast.153), channel_id=1, source_target_pairs={{0,8},{4,12},{8,0},{12,4},{16,24},{20,28},{24,16},{28,20},{1,9},{5... | collective-permute-start | bytes 1769480 | tf_op jit(solution)/shard_map/ppermute | solution.py:565
  84.8 25.7 %collective-permute-start.21 = (bf16[2,2,48,1536]{3,2,1,0:T(8,128)(2,1)S(1)}, bf16[2,2,48,1536]{3,2,1,0:T(8,128)(2,1)S(1)}, u32[]{:S(2)}, u32[]{:S(2)}) collective-permute-start(bf16[2,2,48,1536]{3,2,1,0:T(8,128)(2,1)S(1)} %pad_maximum_fusion.25), channel_id=1, source_target_pairs={{0,8},{4,12},{8,0},{12,4},{16,24},{20,28},{24,16},{28,20},{1,9},{5... | collective-permute-start | bytes 1769480 | tf_op jit(solution)/shard_map/ppermute | solution.py:565
  86.1 24.4 %collective-permute-start.20 = (bf16[2,2,48,1536]{3,2,1,0:T(8,128)(2,1)S(1)}, bf16[2,2,48,1536]{3,2,1,0:T(8,128)(2,1)S(1)}, u32[]{:S(2)}, u32[]{:S(2)}) collective-permute-start(bf16[2,2,48,1536]{3,2,1,0:T(8,128)(2,1)S(1)} %pad_maximum_fusion.24), channel_id=1, source_target_pairs={{0,16},{4,20},{8,24},{12,28},{16,0},{20,4},{24,8},{28,12},{1,17},{... | collective-permute-start | bytes 1769480 | tf_op jit(solution)/shard_map/ppermute | solution.py:565
  110.5 52.7 %collective-permute-start.26 = (bf16[2,192,1536]{2,1,0:T(8,128)(2,1)}, bf16[2,192,1536]{2,1,0:T(8,128)(2,1)}, u32[]{:S(2)}, u32[]{:S(2)}) collective-permute-start(bf16[2,192,1536]{2,1,0:T(8,128)(2,1)} %pad_maximum_fusion.8), channel_id=1, source_target_pairs={{0,8},{4,12},{8,0},{12,4},{16,24},{20,28},{24,16},{28,20},{1,9},{5... | collective-permute-start | bytes 3538952 | tf_op jit(solution)/shard_map/ppermute | solution.py:565
  112.6 28.5 %collective-permute-start.28 = (bf16[4,2,48,1536]{3,2,1,0:T(8,128)(2,1)}, bf16[4,2,48,1536]{3,2,1,0:T(8,128)(2,1)}, u32[]{:S(2)}, u32[]{:S(2)}) collective-permute-start(bf16[4,2,48,1536]{3,2,1,0:T(8,128)(2,1)} %pad_maximum_fusion.10.refs_2_), channel_id=1, source_target_pairs={{0,4},{4,0},{8,12},{12,8},{16,20},{20,16},{24,28},{28,24},{1,5},{5... | collective-permute-start | bytes 3538952 | tf_op jit(solution)/shard_map/ppermute | solution.py:565
  113.7 27.3 %collective-permute-start.27 = (bf16[4,2,48,1536]{3,2,1,0:T(8,128)(2,1)}, bf16[4,2,48,1536]{3,2,1,0:T(8,128)(2,1)}, u32[]{:S(2)}, u32[]{:S(2)}) collective-permute-start(bf16[4,2,48,1536]{3,2,1,0:T(8,128)(2,1)} %pad_maximum_fusion.9.refs_0_), channel_id=1, source_target_pairs={{0,4},{4,0},{8,12},{12,8},{16,20},{20,16},{24,28},{28,24},{1,5},{5... | collective-permute-start | bytes 3538952 | tf_op jit(solution)/shard_map/ppermute | solution.py:565
  115.3 47.9 %collective-permute-start.25 = (bf16[2,192,1536]{2,1,0:T(8,128)(2,1)}, bf16[2,192,1536]{2,1,0:T(8,128)(2,1)}, u32[]{:S(2)}, u32[]{:S(2)}) collective-permute-start(bf16[2,192,1536]{2,1,0:T(8,128)(2,1)} %pad_maximum_fusion.7), channel_id=1, source_target_pairs={{0,16},{4,20},{8,24},{12,28},{16,0},{20,4},{24,8},{28,12},{1,17},{... | collective-permute-start | bytes 3538952 | tf_op jit(solution)/shard_map/ppermute | solution.py:565
  115.9 47.2 %collective-permute-start.24 = (bf16[256,1536]{1,0:T(8,128)(2,1)S(1)}, bf16[256,1536]{1,0:T(8,128)(2,1)}, u32[]{:S(2)}, u32[]{:S(2)}) collective-permute-start(bf16[256,1536]{1,0:T(8,128)(2,1)S(1)} %bitcast.143), channel_id=1, source_target_pairs={{0,2},{1,3},{2,0},{3,1},{4,6},{5,7},{6,4},{7,5},{8,10},{9,11},{10,... | collective-permute-start | bytes 2359304 | tf_op jit(solution)/shard_map/ppermute | solution.py:565
  163.2 19.4 %collective-permute-start.29 = (bf16[256,1536]{1,0:T(8,128)(2,1)S(1)}, bf16[256,1536]{1,0:T(8,128)(2,1)}, u32[]{:S(2)}, u32[]{:S(2)}) collective-permute-start(bf16[256,1536]{1,0:T(8,128)(2,1)S(1)} %bitcast.144), channel_id=1, source_target_pairs={{0,1},{1,0},{2,3},{3,2},{4,5},{5,4},{6,7},{7,6},{8,9},{9,8},{10,11... | collective-permute-start | bytes 2359304 | tf_op jit(solution)/shard_map/ppermute | solution.py:565
  163.2 19.4 %collective-permute-start.30 = (bf16[256,1536]{1,0:T(8,128)(2,1)S(1)}, bf16[256,1536]{1,0:T(8,128)(2,1)}, u32[]{:S(2)}, u32[]{:S(2)}) collective-permute-start(bf16[256,1536]{1,0:T(8,128)(2,1)S(1)} %bitcast.145), channel_id=1, source_target_pairs={{1,2},{2,1},{5,6},{6,5},{9,10},{10,9},{13,14},{14,13},{17,18},{18,... | collective-permute-start | bytes 2359304 | tf_op jit(solution)/shard_map/ppermute | solution.py:565
  182.6 21.7 %collective-permute-start.33 = (bf16[272,1536]{1,0:T(8,128)(2,1)S(1)}, bf16[272,1536]{1,0:T(8,128)(2,1)S(1)}, u32[]{:S(2)}, u32[]{:S(2)}) collective-permute-start(bf16[272,1536]{1,0:T(8,128)(2,1)S(1)} %maximum_maximum_fusion.h_ref.refs_8_), channel_id=1, source_target_pairs={{0,1},{1,0},{2,3},{3,2},{4,5},{5,4},{6,7},{7,6},{8,9},{9,8},{10,11... | collective-permute-start | bytes 2506760 | tf_op jit(solution)/shard_map/ppermute | solution.py:565
  186.2 18.1 %collective-permute-start.34 = (bf16[272,1536]{1,0:T(8,128)(2,1)S(1)}, bf16[272,1536]{1,0:T(8,128)(2,1)S(1)}, u32[]{:S(2)}, u32[]{:S(2)}) collective-permute-start(bf16[272,1536]{1,0:T(8,128)(2,1)S(1)} %maximum_maximum_fusion.h_ref.refs_8_), channel_id=1, source_target_pairs={{1,2},{2,1},{5,6},{6,5},{9,10},{10,9},{13,14},{14,13},{17,18},{18,... | collective-permute-start | bytes 2506760 | tf_op jit(solution)/shard_map/ppermute | solution.py:565
  204.3 39.0 %collective-permute-start.35 = (bf16[272,1536]{1,0:T(8,128)(2,1)S(1)}, bf16[272,1536]{1,0:T(8,128)(2,1)}, u32[]{:S(2)}, u32[]{:S(2)}) collective-permute-start(bf16[272,1536]{1,0:T(8,128)(2,1)S(1)} %maximum_maximum_fusion.h_ref.refs_8_), channel_id=1, source_target_pairs={{0,2},{1,3},{2,0},{3,1},{4,6},{5,7},{6,4},{7,5},{8,10},{9,11},{10,... | collective-permute-start | bytes 2506760 | tf_op jit(solution)/shard_map/ppermute | solution.py:565
  207.3 36.0 %collective-permute-start.36 = (bf16[256,1536]{1,0:T(8,128)(2,1)}, bf16[256,1536]{1,0:T(8,128)(2,1)S(1)}, u32[]{:S(2)}, u32[]{:S(2)}) collective-permute-start(bf16[256,1536]{1,0:T(8,128)(2,1)} %collective-permute-done.24.z_ref.refs_6_), channel_id=1, source_target_pairs={{1,0},{2,3},{5,4},{6,7},{9,8},{10,11},{13,12},{14,15},{17,16},{18,... | collective-permute-start | bytes 2359304 | tf_op jit(solution)/shard_map/ppermute | solution.py:565
  244.2 20.9 %collective-permute-start.37 = (bf16[272,1536]{1,0:T(8,128)(2,1)}, bf16[272,1536]{1,0:T(8,128)(2,1)}, u32[]{:S(2)}, u32[]{:S(2)}) collective-permute-start(bf16[272,1536]{1,0:T(8,128)(2,1)} %collective-permute-done.35.h_ref.refs_10_), channel_id=1, source_target_pairs={{1,0},{2,3},{5,4},{6,7},{9,8},{10,11},{13,12},{14,15},{17,16},{18,... | collective-permute-start | bytes 2506760 | tf_op jit(solution)/shard_map/ppermute | solution.py:565
  265.1 19.4 %collective-permute-start.38 = (bf16[272,1536]{1,0:T(8,128)(2,1)S(1)}, bf16[272,1536]{1,0:T(8,128)(2,1)S(1)}, u32[]{:S(2)}, u32[]{:S(2)}) collective-permute-start(bf16[272,1536]{1,0:T(8,128)(2,1)S(1)} %copy-done.50), channel_id=1, source_target_pairs={{0,1},{1,0},{2,3},{3,2},{4,5},{5,4},{6,7},{7,6},{8,9},{9,8},{10,11... | collective-permute-start | bytes 2506760 | tf_op jit(solution)/shard_map/ppermute | solution.py:565
  294.8 22.1 %collective-permute-start.39 = (bf16[272,1536]{1,0:T(8,128)(2,1)S(1)}, bf16[272,1536]{1,0:T(8,128)(2,1)}, u32[]{:S(2)}, u32[]{:S(2)}) collective-permute-start(bf16[272,1536]{1,0:T(8,128)(2,1)S(1)} %copy-done.52), channel_id=1, source_target_pairs={{0,1},{3,2},{4,5},{7,6},{8,9},{11,10},{12,13},{15,14},{16,17},{19,... | collective-permute-start | bytes 2506760 | tf_op jit(solution)/shard_map/ppermute | solution.py:565
  299.4 17.6 %collective-permute-start.40 = (bf16[272,1536]{1,0:T(8,128)(2,1)S(1)}, bf16[272,1536]{1,0:T(8,128)(2,1)}, u32[]{:S(2)}, u32[]{:S(2)}) collective-permute-start(bf16[272,1536]{1,0:T(8,128)(2,1)S(1)} %copy-done.52), channel_id=1, source_target_pairs={{1,2},{2,1},{5,6},{6,5},{9,10},{10,9},{13,14},{14,13},{17,18},{18,... | collective-permute-start | bytes 2506760 | tf_op jit(solution)/shard_map/ppermute | solution.py:565
  316.9 27.9 %collective-permute-start.44 = (bf16[2,192,1536]{2,1,0:T(8,128)(2,1)}, bf16[2,192,1536]{2,1,0:T(8,128)(2,1)}, u32[]{:S(2)}, u32[]{:S(2)}) collective-permute-start(bf16[2,192,1536]{2,1,0:T(8,128)(2,1)} %pad_maximum_fusion.12), channel_id=1, source_target_pairs={{0,8},{4,12},{8,0},{12,4},{16,24},{20,28},{24,16},{28,20},{1,9},{5... | collective-permute-start | bytes 3538952 | tf_op jit(solution)/shard_map/ppermute | solution.py:565
  319.2 27.6 %collective-permute-start.43 = (bf16[2,192,1536]{2,1,0:T(8,128)(2,1)}, bf16[2,192,1536]{2,1,0:T(8,128)(2,1)}, u32[]{:S(2)}, u32[]{:S(2)}) collective-permute-start(bf16[2,192,1536]{2,1,0:T(8,128)(2,1)} %pad_maximum_fusion.11), channel_id=1, source_target_pairs={{0,16},{4,20},{8,24},{12,28},{16,0},{20,4},{24,8},{28,12},{1,17},{... | collective-permute-start | bytes 3538952 | tf_op jit(solution)/shard_map/ppermute | solution.py:565
  321.9 40.1 %collective-permute-start.42 = (bf16[272,1536]{1,0:T(8,128)(2,1)}, bf16[272,1536]{1,0:T(8,128)(2,1)}, u32[]{:S(2)}, u32[]{:S(2)}) collective-permute-start(bf16[272,1536]{1,0:T(8,128)(2,1)} %add_convert_fusion), channel_id=1, source_target_pairs={{0,2},{1,3},{2,0},{3,1},{4,6},{5,7},{6,4},{7,5},{8,10},{9,11},{10,... | collective-permute-start | bytes 2506760 | tf_op jit(solution)/shard_map/ppermute | solution.py:565
  363.8 41.2 %collective-permute-start.47 = (bf16[256,1536]{1,0:T(8,128)(2,1)S(1)}, bf16[256,1536]{1,0:T(8,128)(2,1)}, u32[]{:S(2)}, u32[]{:S(2)}) collective-permute-start(bf16[256,1536]{1,0:T(8,128)(2,1)S(1)} %copy-done.56), channel_id=1, source_target_pairs={{0,1},{1,0},{2,3},{3,2},{4,5},{5,4},{6,7},{7,6},{8,9},{9,8},{10,11... | collective-permute-start | bytes 2359304 | tf_op jit(solution)/shard_map/ppermute | solution.py:565
  370.8 34.2 %collective-permute-start.50 = (bf16[384,384]{1,0:T(8,128)(2,1)}, bf16[384,384]{1,0:T(8,128)(2,1)S(1)}, u32[]{:S(2)}, u32[]{:S(2)}) collective-permute-start(bf16[384,384]{1,0:T(8,128)(2,1)} %get-tuple-element.240), channel_id=1, source_target_pairs={{0,3},{1,2},{2,1},{3,0},{4,7},{5,6},{6,5},{7,4},{8,11},{9,10},{10,... | collective-permute-start | bytes 884744 | tf_op jit(solution)/shard_map/ppermute | solution.py:565
  372.3 32.7 %collective-permute-start.49 = (bf16[384,384]{1,0:T(8,128)(2,1)}, bf16[384,384]{1,0:T(8,128)(2,1)S(1)}, u32[]{:S(2)}, u32[]{:S(2)}) collective-permute-start(bf16[384,384]{1,0:T(8,128)(2,1)} %get-tuple-element.239), channel_id=1, source_target_pairs={{0,2},{1,3},{2,0},{3,1},{4,6},{5,7},{6,4},{7,5},{8,10},{9,11},{10,... | collective-permute-start | bytes 884744 | tf_op jit(solution)/shard_map/ppermute | solution.py:565
  372.3 32.7 %collective-permute-start.48 = (bf16[384,384]{1,0:T(8,128)(2,1)}, bf16[384,384]{1,0:T(8,128)(2,1)S(1)}, u32[]{:S(2)}, u32[]{:S(2)}) collective-permute-start(bf16[384,384]{1,0:T(8,128)(2,1)} %get-tuple-element.238), channel_id=1, source_target_pairs={{0,1},{1,0},{2,3},{3,2},{4,5},{5,4},{6,7},{7,6},{8,9},{9,8},{10,11... | collective-permute-start | bytes 884744 | tf_op jit(solution)/shard_map/ppermute | solution.py:565
  409.0 217.0 %all-reduce.4.cloned.1.call-start = ((), (), s32[]{:S(2)}) async-start(), calls=%async_computation.4 | async-start | bytes 9437184 | tf_op jit(solution)/shard_map/psum | solution.py:872
  409.7 24.8 %collective-permute-start.55 = (bf16[1,384,768]{2,1,0:T(8,128)(2,1)S(1)}, bf16[1,384,768]{2,1,0:T(8,128)(2,1)S(1)}, u32[]{:S(2)}, u32[]{:S(2)}) collective-permute-start(bf16[1,384,768]{2,1,0:T(8,128)(2,1)S(1)} %get-tuple-element.249), channel_id=1, source_target_pairs={{0,16},{4,20},{8,24},{12,28},{16,0},{20,4},{24,8},{28,12},{1,17},{... | collective-permute-start | bytes 1769480 | tf_op jit(solution)/shard_map/ppermute | solution.py:565
  411.3 23.2 %collective-permute-start.54 = (bf16[1,384,768]{2,1,0:T(8,128)(2,1)S(1)}, bf16[1,384,768]{2,1,0:T(8,128)(2,1)S(1)}, u32[]{:S(2)}, u32[]{:S(2)}) collective-permute-start(bf16[1,384,768]{2,1,0:T(8,128)(2,1)S(1)} %get-tuple-element.248), channel_id=1, source_target_pairs={{0,8},{4,12},{8,0},{12,4},{16,24},{20,28},{24,16},{28,20},{1,9},{5... | collective-permute-start | bytes 1769480 | tf_op jit(solution)/shard_map/ppermute | solution.py:565
  413.6 20.7 %collective-permute-start.52 = (bf16[2,256,256]{2,1,0:T(8,128)(2,1)S(1)}, bf16[2,256,256]{2,1,0:T(8,128)(2,1)S(1)}, u32[]{:S(2)}, u32[]{:S(2)}) collective-permute-start(bf16[2,256,256]{2,1,0:T(8,128)(2,1)S(1)} %get-tuple-element.242), channel_id=1, source_target_pairs={{2,0},{3,1},{6,4},{7,5},{10,8},{11,9},{14,12},{15,13},{18,16},{19,... | collective-permute-start | bytes 786440 | tf_op jit(solution)/shard_map/ppermute | solution.py:565
  414.9 19.4 %collective-permute-start.53 = (bf16[2,256,256]{2,1,0:T(8,128)(2,1)S(1)}, bf16[2,256,256]{2,1,0:T(8,128)(2,1)S(1)}, u32[]{:S(2)}, u32[]{:S(2)}) collective-permute-start(bf16[2,256,256]{2,1,0:T(8,128)(2,1)S(1)} %get-tuple-element.243), channel_id=1, source_target_pairs={{2,1},{3,0},{6,5},{7,4},{10,9},{11,8},{14,13},{15,12},{18,17},{19,... | collective-permute-start | bytes 786440 | tf_op jit(solution)/shard_map/ppermute | solution.py:565
  448.5 38.0 %collective-permute-start.58 = (bf16[4,1536,256]{2,1,0:T(8,128)(2,1)S(1)}, bf16[4,1536,256]{2,1,0:T(8,128)(2,1)S(1)}, u32[]{:S(2)}, u32[]{:S(2)}) collective-permute-start(bf16[4,1536,256]{2,1,0:T(8,128)(2,1)S(1)} %get-tuple-element.255), channel_id=1, source_target_pairs={{0,4},{4,0},{8,12},{12,8},{16,20},{20,16},{24,28},{28,24},{1,5},{5... | collective-permute-start | bytes 9437192 | tf_op jit(solution)/shard_map/ppermute | solution.py:565
  448.8 34.7 %collective-permute-start.59 = (bf16[2,384,768]{2,1,0:T(8,128)(2,1)S(1)}, bf16[2,384,768]{2,1,0:T(8,128)(2,1)S(1)}, u32[]{:S(2)}, u32[]{:S(2)}) collective-permute-start(bf16[2,384,768]{2,1,0:T(8,128)(2,1)S(1)} %pad_maximum_fusion.13), channel_id=1, source_target_pairs={{0,16},{4,20},{8,24},{12,28},{16,0},{20,4},{24,8},{28,12},{1,17},{... | collective-permute-start | bytes 3538952 | tf_op jit(solution)/shard_map/ppermute | solution.py:565
  450.2 34.4 %collective-permute-start.60 = (bf16[2,384,768]{2,1,0:T(8,128)(2,1)S(1)}, bf16[2,384,768]{2,1,0:T(8,128)(2,1)S(1)}, u32[]{:S(2)}, u32[]{:S(2)}) collective-permute-start(bf16[2,384,768]{2,1,0:T(8,128)(2,1)S(1)} %pad_maximum_fusion.14), channel_id=1, source_target_pairs={{0,8},{4,12},{8,0},{12,4},{16,24},{20,28},{24,16},{28,20},{1,9},{5... | collective-permute-start | bytes 3538952 | tf_op jit(solution)/shard_map/ppermute | solution.py:565
  451.3 35.2 %collective-permute-start.56 = (bf16[256,1536]{1,0:T(8,128)(2,1)S(1)}, bf16[256,1536]{1,0:T(8,128)(2,1)S(1)}, u32[]{:S(2)}, u32[]{:S(2)}) collective-permute-start(bf16[256,1536]{1,0:T(8,128)(2,1)S(1)} %copy-done.54), channel_id=1, source_target_pairs={{1,2},{2,1},{5,6},{6,5},{9,10},{10,9},{13,14},{14,13},{17,18},{18,... | collective-permute-start | bytes 2359304 | tf_op jit(solution)/shard_map/ppermute | solution.py:565
  452.0 34.5 %collective-permute-start.57 = (bf16[256,1536]{1,0:T(8,128)(2,1)S(1)}, bf16[256,1536]{1,0:T(8,128)(2,1)S(1)}, u32[]{:S(2)}, u32[]{:S(2)}) collective-permute-start(bf16[256,1536]{1,0:T(8,128)(2,1)S(1)} %copy-done.54), channel_id=1, source_target_pairs={{0,1},{3,2},{4,5},{7,6},{8,9},{11,10},{12,13},{15,14},{16,17},{19,... | collective-permute-start | bytes 2359304 | tf_op jit(solution)/shard_map/ppermute | solution.py:565
  488.4 47.4 %collective-permute-start.64 = (bf16[4,384,768]{2,1,0:T(8,128)(2,1)}, bf16[4,384,768]{2,1,0:T(8,128)(2,1)}, u32[]{:S(2)}, u32[]{:S(2)}) collective-permute-start(bf16[4,384,768]{2,1,0:T(8,128)(2,1)} %pad_maximum_fusion.3.refs_0_), channel_id=1, source_target_pairs={{0,4},{4,0},{8,12},{12,8},{16,20},{20,16},{24,28},{28,24},{1,5},{5... | collective-permute-start | bytes 7077896 | tf_op jit(solution)/shard_map/ppermute | solution.py:565
  488.7 47.1 %collective-permute-start.63 = (bf16[4,384,768]{2,1,0:T(8,128)(2,1)S(1)}, bf16[4,384,768]{2,1,0:T(8,128)(2,1)}, u32[]{:S(2)}, u32[]{:S(2)}) collective-permute-start(bf16[4,384,768]{2,1,0:T(8,128)(2,1)S(1)} %pad_maximum_fusion.2.refs_0_), channel_id=1, source_target_pairs={{0,4},{4,0},{8,12},{12,8},{16,20},{20,16},{24,28},{28,24},{1,5},{5... | collective-permute-start | bytes 7077896 | tf_op jit(solution)/shard_map/ppermute | solution.py:565
  492.1 36.3 %collective-permute-start.62 = (bf16[2,768,256]{2,1,0:T(8,128)(2,1)}, bf16[2,768,256]{2,1,0:T(8,128)(2,1)}, u32[]{:S(2)}, u32[]{:S(2)}) collective-permute-start(bf16[2,768,256]{2,1,0:T(8,128)(2,1)} %pad_maximum_fusion.20), channel_id=1, source_target_pairs={{0,8},{4,12},{8,0},{12,4},{16,24},{20,28},{24,16},{28,20},{1,9},{5... | collective-permute-start | bytes 2359304 | tf_op jit(solution)/shard_map/ppermute | solution.py:565
  494.1 37.0 %collective-permute-start.61 = (bf16[2,768,256]{2,1,0:T(8,128)(2,1)}, bf16[2,768,256]{2,1,0:T(8,128)(2,1)}, u32[]{:S(2)}, u32[]{:S(2)}) collective-permute-start(bf16[2,768,256]{2,1,0:T(8,128)(2,1)} %pad_maximum_fusion.19), channel_id=1, source_target_pairs={{0,16},{4,20},{8,24},{12,28},{16,0},{20,4},{24,8},{28,12},{1,17},{... | collective-permute-start | bytes 2359304 | tf_op jit(solution)/shard_map/ppermute | solution.py:565
  495.0 38.9 %all-to-all-start = ((bf16[4,48,1536]{2,1,0:T(8,128)(2,1)}), bf16[4,48,1536]{2,1,0:T(8,128)(2,1)}, u32[]{:S(2)}, u32[]{:S(2)}) async-start(bf16[4,48,1536]{2,1,0:T(8,128)(2,1)} %bitcast.178), calls=%async_computation.1 | async-start | bytes 1179648 | tf_op jit(solution)/shard_map/all_to_all | solution.py:891
  499.7 140.0 %all-gather.2.cloned.1.call-start = ((), (), s32[]{:S(2)}) async-start(), calls=%async_computation.3 | async-start | bytes 1327104 | tf_op jit(solution)/shard_map/all_gather | solution.py:902
  535.8 20.1 %collective-permute-start.68 = (bf16[1,768,256]{2,1,0:T(8,128)(2,1)}, bf16[1,768,256]{2,1,0:T(8,128)(2,1)}, u32[]{:S(2)}, u32[]{:S(2)}) collective-permute-start(bf16[1,768,256]{2,1,0:T(8,128)(2,1)} %get-tuple-element.269), channel_id=1, source_target_pairs={{0,16},{4,20},{8,24},{12,28},{16,0},{20,4},{24,8},{28,12},{1,17},{... | collective-permute-start | bytes 1179656 | tf_op jit(solution)/shard_map/ppermute | solution.py:565
  536.8 19.1 %collective-permute-start.67 = (bf16[1,768,256]{2,1,0:T(8,128)(2,1)}, bf16[1,768,256]{2,1,0:T(8,128)(2,1)}, u32[]{:S(2)}, u32[]{:S(2)}) collective-permute-start(bf16[1,768,256]{2,1,0:T(8,128)(2,1)} %get-tuple-element.268), channel_id=1, source_target_pairs={{0,8},{4,12},{8,0},{12,4},{16,24},{20,28},{24,16},{28,20},{1,9},{5... | collective-permute-start | bytes 1179656 | tf_op jit(solution)/shard_map/ppermute | solution.py:565
  537.8 20.5 %collective-permute-start.66 = (f32[10,1536]{1,0:T(8,128)S(1)}, f32[10,1536]{1,0:T(8,128)}, u32[]{:S(2)}, u32[]{:S(2)}) collective-permute-start(f32[10,1536]{1,0:T(8,128)S(1)} %pad_maximum_fusion.32), channel_id=1, source_target_pairs={{0,4},{4,0},{8,12},{12,8},{16,20},{20,16},{24,28},{28,24},{1,5},{5... | collective-permute-start | bytes 184328 | tf_op jit(solution)/shard_map/ppermute | solution.py:565
  558.4 21.7 %collective-permute-start.71 = (bf16[384,256]{1,0:T(8,128)(2,1)S(1)}, bf16[384,256]{1,0:T(8,128)(2,1)S(1)}, u32[]{:S(2)}, u32[]{:S(2)}) collective-permute-start(bf16[384,256]{1,0:T(8,128)(2,1)S(1)} %get-tuple-element.276), channel_id=1, source_target_pairs={{0,2},{1,3},{2,0},{3,1},{4,6},{5,7},{6,4},{7,5},{8,10},{9,11},{10,... | collective-permute-start | bytes 589832 | tf_op jit(solution)/shard_map/ppermute | solution.py:565
  582.4 37.1 %collective-permute-start.65 = (bf16[256,1536]{1,0:T(8,128)(2,1)}, bf16[256,1536]{1,0:T(8,128)(2,1)}, u32[]{:S(2)}, u32[]{:S(2)}) collective-permute-start(bf16[256,1536]{1,0:T(8,128)(2,1)} %add_convert_fusion.2), channel_id=1, source_target_pairs={{0,2},{1,3},{2,0},{3,1},{4,6},{5,7},{6,4},{7,5},{8,10},{9,11},{10,... | collective-permute-start | bytes 2359304 | tf_op jit(solution)/shard_map/ppermute | solution.py:901
  609.5 24.0 %collective-permute-start.78 = (bf16[4,384,256]{2,1,0:T(8,128)(2,1)S(1)}, bf16[4,384,256]{2,1,0:T(8,128)(2,1)}, u32[]{:S(2)}, u32[]{:S(2)}) collective-permute-start(bf16[4,384,256]{2,1,0:T(8,128)(2,1)S(1)} %pad_maximum_fusion.22.near_ref), channel_id=1, source_target_pairs={{0,4},{4,0},{8,12},{12,8},{16,20},{20,16},{24,28},{28,24},{1,5},{5... | collective-permute-start | bytes 2359304 | tf_op jit(solution)/shard_map/ppermute | solution.py:565
  (163 other events, 1662.5 us)
Sparse Core Ops, SparseCore 0:
  409.1 60.1 reduce-scatter.1
  489.0 117.5 all-reduce.3
  608.5 26.3 all-gather.1
